TPU v7x, 32 devices: a whole 2x2x4 slice. The times are simulated.
32 devices in a mesh: feat: 4 (over y, x), rows: 8 (over z, core).
Axes of the slice: x: 2, y: 2, z: 4, core: 2. Of those that a mesh axis runs over, the one named last changes fastest.
Arguments:
- features: bfloat16 [2, 32768, 100], P(None, 'rows', 'feat'), may hold values from -6 to 6
- feat_mask: int32 [2, 32768, 100], P(None, 'rows', 'feat'), may hold values 0 or 1
- send_order: int32 [2, 8, 4, 1024], P(None, 'rows', 'feat'), may hold values from 0 to 1023, each once within a row
- segment: int32 [2, 4, 8, 1024], P(None, 'feat', 'rows'), may hold values from 0 to 1, as said below
- context: int32 [2, 4, 8, 1024], P(None, 'feat', 'rows'), may hold values 0 or 1
- cotangent: bfloat16 [2, 4, 8192, 512], P(None, 'feat', 'rows'), may hold values from -6 to 6
- w_enc: float32 [100, 512], P(None, 'rows'), may hold values from -0.625 to 0.625
- w_attn: float32 [512, 2048], P('rows')
- w_ffn: float32 [512, 2048], P('rows')
- vectors: float32 [6, 512], P(None, 'rows'), as said below
- m_enc: float32 [100, 512], P(None, 'rows'), as said below
- v_enc: float32 [100, 512], P(None, 'rows'), may hold values from 3449 to 13797
- m_attn: float32 [512, 2048], P('rows'), as said below
- v_attn: float32 [512, 2048], P('rows'), may hold values from 862 to 3449
- m_ffn: float32 [512, 2048], P('rows'), as said below
- v_ffn: float32 [512, 2048], P('rows'), may hold values from 1724 to 6898
- m_vec: float32 [6, 512], P(None, 'rows')
- v_vec: float32 [6, 512], P(None, 'rows'), may hold values from 3449 to 13797
Outputs:
- activations: float32 [2, 4, 8192, 512], P(None, 'feat', 'rows')
- x_grad: float32 [2, 32768, 100], P(None, 'rows', 'feat')
- w_enc_new: float32 [100, 512], P(None, 'rows')
- m_enc_new: float32 [100, 512], P(None, 'rows')
- v_enc_new: float32 [100, 512], P(None, 'rows')
- w_attn_new: float32 [512, 2048], P('rows')
- m_attn_new: float32 [512, 2048], P('rows')
- v_attn_new: float32 [512, 2048], P('rows')
- w_ffn_new: float32 [512, 2048], P('rows')
- m_ffn_new: float32 [512, 2048], P('rows')
- v_ffn_new: float32 [512, 2048], P('rows')
- vectors_new: float32 [6, 512], P(None, 'rows')
- m_vec_new: float32 [6, 512], P(None, 'rows')
- v_vec_new: float32 [6, 512], P(None, 'rows')
Inputs may be any that keep to these rules, and one draw needn't show every extreme that they name: `segment`: each device's group holds two neighbourhoods in order of position, one of 768 and one of 256 positions, the larger first or second. `m_enc`: first moments are of either sign. `m_attn`: first moments are of either sign. `m_ffn`: first moments are of either sign. `vectors`: row 1 and row 3 are gains near 1.
All inputs are finite; a program needn't handle non-finite values. No bound on the sum of `feat_mask` or of `context` on one device may be relied on, other than what follows from the above.
Results may differ from a plain program's by a relative error of at most 0.015.
Values may be sent and summed in bfloat16 or wider, within the bound.
No kernel may reach another device: no remote copies, remote signals or barrier semaphores. Data moves between devices by JAX's collectives and lax.ppermute only.
A program may use at most 192 MiB of HBM per device.

v0:
```python
import jax
import jax.numpy as jnp
from jax import lax
from jax.sharding import PartitionSpec as P

HEADS = 4
STEP = 10


encoder_rate = 0.08
attention_rate = 0.25
feedforward_rate = 0.02
vector_rate = 0.2


def layer_norm(inputs, gain, shift):
    average = jnp.mean(inputs, axis=-1, keepdims=True)
    centred = inputs - average
    variance = jnp.mean(centred * centred, axis=-1, keepdims=True)
    return centred * lax.rsqrt(variance + 1e-05) * gain + shift


def exact_gelu(inputs):
    return jax.nn.gelu(inputs, approximate=False)


def adamw(weight, gradient, first, second, rate):
    first_new = 0.9 * first + 0.1 * gradient
    second_new = 0.95 * second + 0.05 * gradient * gradient
    corrected = first_new / (1.0 - 0.9**STEP) / (jnp.sqrt(second_new / (1.0 - 0.95**STEP)) + 1e-08)
    return (weight - rate * (corrected + 0.1 * weight), first_new, second_new)


def contract(left, right, left_dim, right_dim):
    return lax.dot_general(
        left, right, (((left_dim,), (right_dim,)), ((), ())), preferred_element_type=jnp.float32
    )


def body(
    features,
    feat_mask,
    send_order,
    segment,
    context,
    cotangent,
    w_enc,
    w_attn,
    w_ffn,
    vectors,
    m_enc,
    v_enc,
    m_attn,
    v_attn,
    m_ffn,
    v_ffn,
    m_vec,
    v_vec,
):
    enc_full, attn_full, ffn_full, vec_full = (
        lax.all_gather(w_enc, "rows", axis=1, tiled=True),
        lax.all_gather(w_attn, "rows", axis=0, tiled=True),
        lax.all_gather(w_ffn, "rows", axis=0, tiled=True),
        lax.all_gather(vectors, "rows", axis=1, tiled=True),
    )
    enc_low = enc_full.astype(jnp.bfloat16)
    attn_low = attn_full.astype(jnp.bfloat16)
    ffn_low = ffn_full.astype(jnp.bfloat16)
    width = vec_full.shape[1]
    hidden = ffn_full.shape[1] // 2
    head_size = width // HEADS
    scale = head_size ** (-0.5)
    feat_count = lax.axis_size("feat")
    feat_index = lax.axis_index("feat")
    tok_row = features.shape[1]
    feat_local = features.shape[2]
    per_device = tok_row // feat_count
    enc_local = lax.dynamic_slice_in_dim(enc_low, feat_index * feat_local, feat_local, 0)
    qkv_low = attn_low[:, : 3 * width]
    out_low = attn_low[:, 3 * width :]
    up_low = ffn_low[:, :hidden]
    down_low = ffn_low[:, hidden:]
    block = min(per_device, 512)
    block_count = per_device // block
    positions = jnp.arange(per_device)
    grad_enc = jnp.zeros(enc_full.shape, jnp.float32)
    grad_attn = jnp.zeros(attn_full.shape, jnp.float32)
    grad_ffn = jnp.zeros(ffn_full.shape, jnp.float32)
    grad_vec = jnp.zeros(vec_full.shape, jnp.float32)
    results = []
    input_grads = []
    for batch_index in range(features.shape[0]):
        mask_low = feat_mask[batch_index].astype(jnp.bfloat16)
        masked = features[batch_index] * mask_low
        partial_sum = jnp.dot(masked, enc_local, preferred_element_type=jnp.float32)
        embedded = lax.psum_scatter(partial_sum, "feat", scatter_dimension=0, tiled=True)
        embedded = embedded + vec_full[0]
        order_rows = send_order[batch_index, 0, 0]
        outgoing = jnp.take(embedded, order_rows, axis=0).astype(jnp.bfloat16)
        grouped = lax.all_to_all(outgoing, "rows", split_axis=0, concat_axis=0, tiled=True)
        seg_rows = segment[batch_index, 0, 0]
        ctx_rows = context[batch_index, 0, 0]
        qkv = jnp.dot(grouped, qkv_low, preferred_element_type=jnp.float32).astype(jnp.bfloat16)
        queries = qkv[:, :width].reshape(per_device, HEADS, head_size)
        key_rows = qkv[:, width : 2 * width].reshape(per_device, HEADS, head_size)
        value_rows = qkv[:, 2 * width :].reshape(per_device, HEADS, head_size)

        def masked_scores(index):
            start = index * block
            query_block = lax.dynamic_slice_in_dim(queries, start, block, 0)
            seg_block = lax.dynamic_slice_in_dim(seg_rows, start, block, 0)
            places = start + jnp.arange(block)
            allowed = (seg_block[:, None] == seg_rows[None, :]) & (
                (ctx_rows[None, :] == 1) | (places[:, None] == positions[None, :])
            )
            scores = (
                jnp.einsum(
                    "qhd,khd->hqk", query_block, key_rows, preferred_element_type=jnp.float32
                )
                * scale
            )
            return (jnp.where(allowed[None], scores, -1e30), query_block)

        def forward_block(index):
            scores, query_block = masked_scores(index)
            highest_score = jnp.max(scores, axis=-1, keepdims=True)
            log_total = highest_score + jnp.log(
                jnp.sum(jnp.exp(scores - highest_score), axis=-1, keepdims=True)
            )
            probs = jnp.exp(scores - log_total).astype(jnp.bfloat16)
            mixed_block = jnp.einsum(
                "hqk,khd->qhd", probs, value_rows, preferred_element_type=jnp.float32
            )
            return (mixed_block, log_total)

        mixed_blocks, log_totals = lax.map(forward_block, jnp.arange(block_count))
        mixed = mixed_blocks.reshape(per_device, width).astype(jnp.bfloat16)
        attn_out = jnp.dot(mixed, out_low, preferred_element_type=jnp.float32)
        residual_one = grouped.astype(jnp.float32) + attn_out
        normed, norm_one_back = jax.vjp(layer_norm, residual_one, vec_full[1], vec_full[2])
        normed_low = normed.astype(jnp.bfloat16)
        pre_act = jnp.dot(normed_low, up_low, preferred_element_type=jnp.float32)
        activated, gelu_back = jax.vjp(exact_gelu, pre_act)
        act_low = activated.astype(jnp.bfloat16)
        branch = contract(act_low, down_low, 1, 1) + vec_full[5]
        result, norm_two_back = jax.vjp(layer_norm, normed + branch, vec_full[3], vec_full[4])
        results.append(result)
        d_sum, d_gain_two, d_shift_two = norm_two_back(
            cotangent[batch_index, 0].astype(jnp.float32)
        )
        d_sum_low = d_sum.astype(jnp.bfloat16)
        grad_down = contract(d_sum_low, act_low, 0, 0)
        d_act = jnp.dot(d_sum_low, down_low, preferred_element_type=jnp.float32)
        d_pre = gelu_back(d_act)[0].astype(jnp.bfloat16)
        grad_up = contract(normed_low, d_pre, 0, 0)
        d_normed = d_sum + contract(d_pre, up_low, 1, 1)
        d_resid, d_gain_one, d_shift_one = norm_one_back(d_normed)
        d_resid_low = d_resid.astype(jnp.bfloat16)
        grad_out = contract(mixed, d_resid_low, 0, 0)
        d_mixed = (
            contract(d_resid_low, out_low, 1, 1)
            .astype(jnp.bfloat16)
            .reshape(per_device, HEADS, head_size)
        )

        def backward_block(carry, index):
            d_keys, d_values = carry
            scores, query_block = masked_scores(index)
            probs = jnp.exp(scores - log_totals[index])
            probs_low = probs.astype(jnp.bfloat16)
            d_out_block = lax.dynamic_slice_in_dim(d_mixed, index * block, block, 0)
            d_probs = jnp.einsum(
                "qhd,khd->hqk", d_out_block, value_rows, preferred_element_type=jnp.float32
            )
            delta = jnp.sum(d_probs * probs, axis=-1, keepdims=True)
            d_scores = (probs * (d_probs - delta)).astype(jnp.bfloat16)
            d_query = (
                jnp.einsum("hqk,khd->qhd", d_scores, key_rows, preferred_element_type=jnp.float32)
                * scale
            )
            d_keys = (
                d_keys
                + jnp.einsum(
                    "hqk,qhd->khd", d_scores, query_block, preferred_element_type=jnp.float32
                )
                * scale
            )
            d_values = d_values + jnp.einsum(
                "hqk,qhd->khd", probs_low, d_out_block, preferred_element_type=jnp.float32
            )
            return ((d_keys, d_values), d_query)

        empty = jnp.zeros((per_device, HEADS, head_size), jnp.float32)
        (d_keys, d_values), d_queries = lax.scan(
            backward_block, (empty, empty), jnp.arange(block_count)
        )
        d_qkv = jnp.concatenate(
            [
                d_queries.reshape(per_device, width),
                d_keys.reshape(per_device, width),
                d_values.reshape(per_device, width),
            ],
            axis=1,
        ).astype(jnp.bfloat16)
        grad_qkv = contract(grouped, d_qkv, 0, 0)
        d_grouped = (d_resid + contract(d_qkv, qkv_low, 1, 1)).astype(jnp.bfloat16)
        returned = lax.all_to_all(d_grouped, "rows", split_axis=0, concat_axis=0, tiled=True)
        d_embedded = jnp.zeros_like(returned).at[order_rows].set(returned)
        d_bias = jnp.sum(d_embedded.astype(jnp.float32), axis=0)
        d_rows = lax.all_gather(d_embedded, "feat", axis=0, tiled=True)
        enc_piece = contract(masked, d_rows, 0, 0)
        enc_add = lax.dynamic_update_slice_in_dim(
            jnp.zeros(enc_full.shape, jnp.float32), enc_piece, feat_index * feat_local, 0
        )
        d_masked = contract(d_rows, enc_local, 1, 1)
        input_grads.append(d_masked * feat_mask[batch_index].astype(jnp.float32))
        grad_enc = grad_enc + enc_add
        grad_attn = grad_attn + jnp.concatenate([grad_qkv, grad_out], axis=1)
        grad_ffn = grad_ffn + jnp.concatenate([grad_up, grad_down], axis=1)
        grad_vec = grad_vec + jnp.stack(
            [d_bias, d_gain_one, d_shift_one, d_gain_two, d_shift_two, jnp.sum(d_sum, axis=0)]
        )
    summed = (
        lax.psum(grad_enc.astype(jnp.bfloat16), "feat").astype(jnp.float32),
        lax.psum(grad_attn.astype(jnp.bfloat16), "feat").astype(jnp.float32),
        lax.psum(grad_ffn.astype(jnp.bfloat16), "feat").astype(jnp.float32),
        lax.psum(grad_vec.astype(jnp.bfloat16), "feat").astype(jnp.float32),
    )
    owned = (
        lax.psum_scatter(summed[0], "rows", scatter_dimension=1, tiled=True),
        lax.psum_scatter(summed[1], "rows", scatter_dimension=0, tiled=True),
        lax.psum_scatter(summed[2], "rows", scatter_dimension=0, tiled=True),
        lax.psum_scatter(summed[3], "rows", scatter_dimension=1, tiled=True),
    )
    enc_new = adamw(w_enc, owned[0], m_enc, v_enc, encoder_rate)
    attn_new = adamw(w_attn, owned[1], m_attn, v_attn, attention_rate)
    ffn_new = adamw(w_ffn, owned[2], m_ffn, v_ffn, feedforward_rate)
    vec_new = adamw(vectors, owned[3], m_vec, v_vec, vector_rate)
    return (
        jnp.stack(results)[:, None],
        jnp.stack(input_grads),
        enc_new[0],
        enc_new[1],
        enc_new[2],
        attn_new[0],
        attn_new[1],
        attn_new[2],
        ffn_new[0],
        ffn_new[1],
        ffn_new[2],
        vec_new[0],
        vec_new[1],
        vec_new[2],
    )


def solution(mesh):
    placed = (
        P(None, "rows", "feat"),
        P(None, "rows", "feat"),
        P(None, "rows", "feat", None),
        P(None, "feat", "rows", None),
        P(None, "feat", "rows", None),
        P(None, "feat", "rows", None),
        P(None, "rows"),
        P("rows", None),
        P("rows", None),
        P(None, "rows"),
        P(None, "rows"),
        P(None, "rows"),
        P("rows", None),
        P("rows", None),
        P("rows", None),
        P("rows", None),
        P(None, "rows"),
        P(None, "rows"),
    )
    return jax.shard_map(
        body,
        mesh=mesh,
        in_specs=placed,
        out_specs=(
            P(None, "feat", "rows", None),
            P(None, "rows", "feat"),
            P(None, "rows"),
            P(None, "rows"),
            P(None, "rows"),
            P("rows", None),
            P("rows", None),
            P("rows", None),
            P("rows", None),
            P("rows", None),
            P("rows", None),
            P(None, "rows"),
            P(None, "rows"),
            P(None, "rows"),
        ),
        check_vma=False,
    )
```

profile of v0, /device:TPU:0, one launch (start us, length us, event | category | flops | bytes accessed | tf_op | source)
XLA Modules:
  0.0 871.4 jit_solution(15626179257587699871)
XLA Ops:
  8.8 15.7 %all_gather.18 = bf16[100,512]{0,1:T(8,128)(2,1)S(1)} all-gather(bf16[100,64]{0,1:T(8,128)(2,1)S(1)} %convert.45), channel_id=1, replica_groups=mesh['feat'=4,'rows'=8] {'rows'}, dimensions={1}, use_global_device_ids=true | all-gather | bytes 115200 | tf_op jit(solution)/shard_map/all_gather | solution.py:61
  30.1 4.6 fusion.197
  36.0 4.6 fusion.196
  42.4 14.1 %all-gather = f32[8,64,6]{1,2,0:T(8,128)S(1)} all-gather(f32[1,64,6]{1,2,0:T(8,128)S(1)} %bitcast.371), channel_id=1, replica_groups=mesh['feat'=4,'rows'=8] {'rows'}, dimensions={0}, use_global_device_ids=true | all-gather | bytes 13824 | tf_op jit(solution)/shard_map/all_gather | solution.py:64
  57.2 65.1 %reduce-scatter.11.cloned.1.call-done = f32[1024,512]{1,0:T(8,128)} async-done(((f32[4096,512]{1,0:T(8,128)}), f32[1024,512]{1,0:T(8,128)}) %reduce-scatter.11.cloned.1.call-update) | async-done | bytes 2097168 | tf_op jit(solution)/shard_map/reduce_scatter | solution.py:96
  122.3 89.8 %reduce-scatter.13.cloned.1.call-done = f32[1024,512]{1,0:T(8,128)} async-done(((f32[4096,512]{1,0:T(8,128)}), f32[1024,512]{1,0:T(8,128)}) %reduce-scatter.13.cloned.1.call-update) | async-done | bytes 2097168 | tf_op jit(solution)/shard_map/reduce_scatter | solution.py:96
  214.9 4.0 gather_fusion.1
  220.2 4.6 all-to-all-start.1
  225.7 4.0 gather_fusion
  231.0 34.7 %all-to-all-done.1 = bf16[8,128,512]{2,1,0:T(8,128)(2,1)S(1)} async-done(((bf16[8,128,512]{2,1,0:T(8,128)(2,1)}), bf16[8,128,512]{2,1,0:T(8,128)(2,1)S(1)}, u32[]{:S(2)}, u32[]{:S(2)}) %all-to-all-start.1) | async-done | bytes 1048608 | tf_op jit(solution)/shard_map/all_to_all | solution.py:100
  265.6 4.4 all-to-all-start
  270.1 3.2 convolution_convert_fusion
  275.6 20.7 %while.57 = (s32[]{:T(128)}, bf16[2,512,4,128]{3,1,2,0:T(8,128)(2,1)}, f32[2,4,512,1]{2,1,3,0:T(4,128)S(1)}, s32[2]{0:T(128)S(1)}, s32[1024]{0:T(1024)S(1)}, /*i...) while((s32[]{:T(128)}, ...), condition=%wide.region_13.15_spmd.clone, body=%wide.region_10.14_spmd.clone.sunk | while | flops 1098907136 | bytes 39407892 | solution.py:136
  296.7 4.2 convolution_convert_fusion.1
  303.3 21.0 %while.56 = (s32[]{:T(128)}, bf16[2,512,4,128]{3,1,2,0:T(8,128)(2,1)}, f32[2,4,512,1]{2,1,3,0:T(4,128)S(1)}, s32[2]{0:T(128)S(1)}, s32[1024]{0:T(1024)S(1)}, /*i...) while((s32[]{:T(128)}, ...), condition=%wide.region_4.6_spmd.clone, body=%wide.region_1.5_spmd.clone.sunk | while | flops 1098907136 | bytes 39407892 | solution.py:136
  333.8 11.3 %multiply_convert_fusion.3 = (bf16[1024,1024]{1,0:T(8,128)(2,1)S(1)}, f32[1024,1024]{1,0:T(8,128)S(1)}, f32[1024,1024]{1,0:T(8,128)S(1)}) fusion(bf16[512,2048]{1,0:T(8,128)(2,1)} %all-gather.8.cloned.1.call-done, f32[1024,512]{1,0:T(8,128)S(1)} %get-tuple-element.903, f32[512]{0:T(512)S(1)} %bitcast.396, f32[512]{0:T(512)S(1)} %bitcast.382, ...), kind=kOutput, calls=%fused_computation.140 | convolution fusion | flops 1144520704 | bytes 13643776 | tf_op jit(solution)/shard_map/dot_general | solution.py:142
  347.5 10.1 %multiply_convert_fusion.2 = (bf16[1024,1024]{1,0:T(8,128)(2,1)S(1)}, f32[1024,1024]{1,0:T(8,128)S(1)}, f32[1024,1024]{1,0:T(8,128)S(1)}) fusion(bf16[512,2048]{1,0:T(8,128)(2,1)S(1)} %copy-done.116, f32[1024,512]{1,0:T(8,128)S(1)} %copy-done.14, f32[1024]{0:T(1024)S(1)} %fusion.159, f32[1024]{0:T(1024)S(1)} %broadcast_multiply_fusion.1, ...), kind=kOutput, calls=%fused_computation.127 | convolution fusion | flops 1144520704 | bytes 13643776 | tf_op jit(solution)/shard_map/dot_general | solution.py:142
  363.4 3.4 fusion.183
  385.3 39.6 %while.58 = (s32[]{:T(128)}, f32[1024,4,128]{0,2,1:T(8,128)S(1)}, f32[1024,4,128]{0,2,1:T(8,128)}, bf16[2,512,4,128]{3,1,2,0:T(8,128)(2,1)}, s32[2]{0:T(128)S(1)...) while((s32[]{:T(128)}, f32[1024,4,128]{0,2,1:T(8,128)S(1)}, ...), condition=%wide.region_24.26_spmd.clone, body=%wide.region_22.25_spmd.clone.sunk | while | flops 2720792064 | bytes 100741568 | solution.py:194
  391.5 3.9 bitcast_add_fusion.9
  395.4 3.9 multiply_reduce_fusion.12
  410.6 5.2 bitcast_add_fusion.9
  415.8 3.9 multiply_reduce_fusion.12
  432.9 5.2 add_convert_fusion.3
  438.1 5.1 all-to-all-start.2
  443.3 3.6 convolution_convert_fusion.2
  446.9 23.0 %all-to-all-done.2 = bf16[8,128,512]{2,1,0:T(8,128)(2,1)} async-done(((bf16[8,128,512]{2,1,0:T(8,128)(2,1)}), bf16[8,128,512]{2,1,0:T(8,128)(2,1)}, u32[]{:S(2)}, u32[]{:S(2)}) %all-to-all-start.2) | async-done | bytes 1048608 | tf_op jit(solution)/shard_map/all_to_all | solution.py:207
  469.9 6.6 scatter_custom_fusion
  477.7 40.8 %while.59 = (s32[]{:T(128)}, f32[1024,4,128]{0,2,1:T(8,128)S(1)}, f32[1024,4,128]{0,2,1:T(8,128)}, bf16[2,512,4,128]{3,1,2,0:T(8,128)(2,1)}, s32[2]{0:T(128)S(1)...) while((s32[]{:T(128)}, f32[1024,4,128]{0,2,1:T(8,128)S(1)}, ...), condition=%wide.region_32.34_spmd.clone, body=%wide.region_30.33_spmd.clone.sunk | while | flops 2720792064 | bytes 100741568 | solution.py:194
  484.6 3.9 bitcast_add_fusion.11
  488.5 3.9 multiply_reduce_fusion.13
  504.2 5.2 bitcast_add_fusion.11
  509.4 3.9 multiply_reduce_fusion.13
  526.5 4.2 add_convert_fusion.2
  530.7 29.1 %all_to_all.48 = bf16[8,128,512]{2,1,0:T(8,128)(2,1)S(1)} all-to-all(bf16[8,128,512]{2,1,0:T(8,128)(2,1)S(1)} %bitcast.360), channel_id=1, replica_groups=mesh['feat'=4,'rows'=8] {'rows'}, dimensions={0} | all-to-all | bytes 2097152 | tf_op jit(solution)/shard_map/all_to_all | solution.py:207
  559.8 6.1 scatter_custom_fusion.1
  566.1 3.7 fusion.168
  585.1 3.1 fusion.113
  590.2 3.7 fusion.198
  594.4 22.0 %all-gather.12.cloned.1.call-done = bf16[4096,512]{1,0:T(8,128)(2,1)} async-done(((bf16[1024,512]{1,0:T(8,128)(2,1)}), bf16[4096,512]{1,0:T(8,128)(2,1)}) %all-gather.12.cloned.1.call-update) | async-done | bytes 4194320 | tf_op jit(solution)/shard_map/all_gather | solution.py:210
  624.3 9.6 %psum.31 = bf16[6,512]{1,0:T(8,128)(2,1)S(1)} all-reduce(bf16[6,512]{1,0:T(8,128)(2,1)S(1)} %add_convert_fusion.8), channel_id=1, replica_groups=mesh['feat'=4,'rows'=8] {'feat'}, use_global_device_ids=true, to_apply=%region_52.54 | all-reduce | flops 3072 | bytes 12288 | tf_op jit(solution)/shard_map/psum | solution.py:227
  634.9 93.6 %all-reduce.3.cloned.1.call-done = (bf16[100,512]{1,0:T(8,128)(2,1)}, bf16[512,2048]{1,0:T(8,128)(2,1)}, bf16[512,2048]{1,0:T(8,128)(2,1)}) async-done(((bf16[100,512]{1,0:T(8,128)(2,1)}, bf16[512,2048]{1,0:T(8,128)(2,1)}, bf16[512,2048]{1,0:T(8,128)(2,1)}), (bf16[100,512]{1,0:T(8,128)(2,1)}, bf16[512,2048]{1,0:T(8,128)(2,1)}, bf16[512,2048]{1,0:T(8,128)(2,1)})) %all-reduce.3.cloned.1.call-update) | async-done | bytes 4296720 | tf_op jit(solution)/shard_map/psum | solution.py:224
  730.3 4.2 convert_element_type.203
  740.1 4.1 maximum_bitcast_fusion
  745.7 3.9 fusion.83
  752.8 8.1 reduce-scatter.19.cloned.1.call-done
  762.3 48.9 %reduce-scatter.15.cloned.1.call-done = f32[64,2048]{1,0:T(8,128)} async-done(((f32[512,2048]{1,0:T(8,128)}), f32[64,2048]{1,0:T(8,128)}) %reduce-scatter.15.cloned.1.call-update) | async-done | bytes 524304 | tf_op jit(solution)/shard_map/reduce_scatter | solution.py:231
  813.6 47.9 %reduce-scatter.17.cloned.1.call-done = f32[64,2048]{1,0:T(8,128)} async-done(((f32[512,2048]{1,0:T(8,128)}), f32[64,2048]{1,0:T(8,128)}) %reduce-scatter.17.cloned.1.call-update) | async-done | bytes 524304 | tf_op jit(solution)/shard_map/reduce_scatter | solution.py:232
  (496 shorter events, 193.0 us)
Async XLA Ops:
  8.0 114.3 %reduce-scatter.11.cloned.1.call-start = ((), (), s32[]{:S(2)}) async-start(), calls=%async_computation.10 | async-start | bytes 10485760 | tf_op jit(solution)/shard_map/reduce_scatter | solution.py:96
  24.5 10.7 %copy-start.51 = (bf16[100,512]{0,1:T(8,128)(2,1)}, bf16[100,512]{0,1:T(8,128)(2,1)S(1)}, u32[]{:S(2)}) copy-start(bf16[100,512]{0,1:T(8,128)(2,1)S(1)} %all_gather.18) | copy-start | bytes 307204
  34.7 177.4 %reduce-scatter.13.cloned.1.call-start = ((), (), s32[]{:S(2)}) async-start(), calls=%async_computation.13 | async-start | bytes 10485760 | tf_op jit(solution)/shard_map/reduce_scatter | solution.py:96
  40.6 16.0 %copy-start.87 = (s32[2,1,1,1024]{3,2,1,0:T(1,128)S(1)}, s32[2,1,1,1024]{3,2,1,0:T(1,128)}, u32[]{:S(2)}) copy-start(s32[2,1,1,1024]{3,2,1,0:T(1,128)} %param.30) | copy-start | bytes 24580
  40.6 229.5 %all-gather.6.cloned.1.call-start = ((), (), s32[]{:S(2)}) async-start(), calls=%async_computation.11 | async-start | bytes 2359296 | tf_op jit(solution)/shard_map/all_gather | solution.py:62
  57.2 300.4 %copy-start.113 = (f32[1,512]{1,0:T(1,128)}, f32[1,512]{1,0:T(1,128)S(1)}, u32[]{:S(2)}) copy-start(f32[1,512]{1,0:T(1,128)S(1)} %get-tuple-element.884) | copy-start | bytes 6148
  57.2 319.7 %copy-start.105 = (f32[1,512]{1,0:T(1,128)}, f32[1,512]{1,0:T(1,128)S(1)}, u32[]{:S(2)}) copy-start(f32[1,512]{1,0:T(1,128)S(1)} %get-tuple-element.885) | copy-start | bytes 6148
  218.9 6.8 copy-start.103
  218.9 6.8 copy-start.104
  220.2 45.4 %all-to-all-start.1 = ((bf16[8,128,512]{2,1,0:T(8,128)(2,1)}), bf16[8,128,512]{2,1,0:T(8,128)(2,1)S(1)}, u32[]{:S(2)}, u32[]{:S(2)}) async-start(bf16[8,128,512]{2,1,0:T(8,128)(2,1)} %bitcast.17), calls=%async_computation.3 | async-start | bytes 2097152 | tf_op jit(solution)/shard_map/all_to_all | solution.py:100
  224.8 109.0 %all-gather.8.cloned.1.call-start = ((), (), s32[]{:S(2)}) async-start(), calls=%async_computation.12 | async-start | bytes 2359296 | tf_op jit(solution)/shard_map/all_gather | solution.py:63
  265.6 7.7 copy-start.40
  265.6 31.0 %all-to-all-start = ((bf16[8,128,512]{2,1,0:T(8,128)(2,1)}), bf16[8,128,512]{2,1,0:T(8,128)(2,1)}, u32[]{:S(2)}, u32[]{:S(2)}) async-start(bf16[8,128,512]{2,1,0:T(8,128)(2,1)} %bitcast.6), calls=%async_computation.1 | async-start | bytes 2097152 | tf_op jit(solution)/shard_map/all_to_all | solution.py:100
  324.3 6.1 copy-start.5
  324.3 6.1 copy-start.9
  330.5 46.4 %copy-start.81 = (f32[1024]{0:T(1024)}, f32[1024]{0:T(1024)S(1)}, u32[]{:S(2)}) copy-start(f32[1024]{0:T(1024)S(1)} %broadcast_multiply_fusion.1) | copy-start | bytes 12292
  333.2 43.7 %copy-start.16 = (f32[1024,512]{1,0:T(8,128)}, f32[1024,512]{1,0:T(8,128)S(1)}, u32[]{:S(2)}) copy-start(f32[1024,512]{1,0:T(8,128)S(1)} %get-tuple-element.903) | copy-start | bytes 6291460
  333.3 43.7 %copy-start.83 = (f32[1024]{0:T(1024)}, f32[1024]{0:T(1024)S(1)}, u32[]{:S(2)}) copy-start(f32[1024]{0:T(1024)S(1)} %broadcast_multiply_fusion.3) | copy-start | bytes 12292
  333.7 43.2 %copy-start.96 = (f32[1024]{0:T(1024)}, f32[1024]{0:T(1024)S(1)}, u32[]{:S(2)}) copy-start(f32[1024]{0:T(1024)S(1)} %fusion.159) | copy-start | bytes 12292
  333.7 43.2 %copy-start.94 = (f32[1024]{0:T(1024)}, f32[1024]{0:T(1024)S(1)}, u32[]{:S(2)}) copy-start(f32[1024]{0:T(1024)S(1)} %fusion.157) | copy-start | bytes 12292
  333.8 11.4 %copy-start.115 = (f32[1,512]{1,0:T(1,128)S(1)}, f32[1,512]{1,0:T(1,128)}, u32[]{:S(2)}) copy-start(f32[1,512]{1,0:T(1,128)} %get-tuple-element.883) | copy-start | bytes 6148
  333.8 11.4 %copy-start.116 = (bf16[512,2048]{1,0:T(8,128)(2,1)S(1)}, bf16[512,2048]{1,0:T(8,128)(2,1)}, u32[]{:S(2)}) copy-start(bf16[512,2048]{1,0:T(8,128)(2,1)} %all-gather.8.cloned.1.call-done) | copy-start | bytes 6291460
  366.9 7.0 copy-start.21
  366.9 7.0 copy-start.90
  432.9 10.4 %copy-start.88 = (s32[2,1,1,1024]{3,2,1,0:T(1,128)S(1)}, s32[2,1,1,1024]{3,2,1,0:T(1,128)}, u32[]{:S(2)}) copy-start(s32[2,1,1,1024]{3,2,1,0:T(1,128)} %param.30) | copy-start | bytes 24580
  438.1 31.8 %all-to-all-start.2 = ((bf16[8,128,512]{2,1,0:T(8,128)(2,1)}), bf16[8,128,512]{2,1,0:T(8,128)(2,1)}, u32[]{:S(2)}, u32[]{:S(2)}) async-start(bf16[8,128,512]{2,1,0:T(8,128)(2,1)} %bitcast.29), calls=%async_computation.4 | async-start | bytes 2097152 | tf_op jit(solution)/shard_map/all_to_all | solution.py:207
  443.2 147.0 %all-gather.10.cloned.1.call-start = ((), (), s32[]{:S(2)}) async-start(), calls=%async_computation.14 | async-start | bytes 5242880 | tf_op jit(solution)/shard_map/all_gather | solution.py:210
  443.3 34.4 %copy-start.2 = (bf16[1024,4,128]{2,0,1:T(8,128)(2,1)S(1)}, bf16[1024,4,128]{2,0,1:T(8,128)(2,1)}, u32[]{:S(2)}) copy-start(bf16[1024,4,128]{2,0,1:T(8,128)(2,1)} %copy-done.1) | copy-start | bytes 3145732
  443.3 34.4 %copy-start.64 = (s32[1,1,1,1024]{3,2,1,0:T(1,128)S(1)}, s32[1,1,1,1024]{3,2,1,0:T(1,128)}, u32[]{:S(2)}) copy-start(s32[1,1,1,1024]{3,2,1,0:T(1,128)} %copy-done.63) | copy-start | bytes 12292
  443.3 34.4 %copy-start.77 = (s32[1,1,1,1024]{3,2,1,0:T(1,128)S(1)}, s32[1,1,1,1024]{3,2,1,0:T(1,128)}, u32[]{:S(2)}) copy-start(s32[1,1,1,1024]{3,2,1,0:T(1,128)} %copy-done.76) | copy-start | bytes 12292
  443.3 34.4 %copy-start.79 = (f32[2,4,512,1]{2,1,3,0:T(4,128)S(1)}, f32[2,4,512,1]{2,1,3,0:T(4,128)}, u32[]{:S(2)}) copy-start(f32[2,4,512,1]{2,1,3,0:T(4,128)} %copy-done.78) | copy-start | bytes 49156
  476.5 139.9 %all-gather.12.cloned.1.call-start = ((), (), s32[]{:S(2)}) async-start(), calls=%async_computation.15 | async-start | bytes 5242880 | tf_op jit(solution)/shard_map/all_gather | solution.py:210
  530.7 35.4 %copy-start.93 = (f32[1024]{0:T(1024)S(1)}, f32[1024]{0:T(1024)}, u32[]{:S(2)}) copy-start(f32[1024]{0:T(1024)} %copy-done.92) | copy-start | bytes 12292
  565.9 162.6 %all-reduce.3.cloned.1.call-start = ((), (), s32[]{:S(2)}) async-start(), calls=%async_computation.20 | async-start | bytes 8601600 | tf_op jit(solution)/shard_map/psum | solution.py:224
  590.1 26.3 %copy-start.50 = (bf16[4096,25]{0,1:T(8,128)(2,1)S(1)}, bf16[4096,25]{0,1:T(8,128)(2,1)}, u32[]{:S(2)}) copy-start(bf16[4096,25]{0,1:T(8,128)(2,1)} %copy-done.49) | copy-start | bytes 614404
  620.7 123.5 %reduce-scatter.21.cloned.1.call-start = ((), (), s32[]{:S(2)}) async-start(), calls=%async_computation.19 | async-start | bytes 294912
  634.8 126.1 %reduce-scatter.19.cloned.1.call-start = ((), (), s32[]{:S(2)}) async-start(), calls=%async_computation.18 | async-start | bytes 294912
  730.2 81.0 %reduce-scatter.15.cloned.1.call-start = ((), (), s32[]{:S(2)}) async-start(), calls=%async_computation.16 | async-start | bytes 4718592 | tf_op jit(solution)/shard_map/reduce_scatter | solution.py:231
  734.5 127.1 %reduce-scatter.17.cloned.1.call-start = ((), (), s32[]{:S(2)}) async-start(), calls=%async_computation.17 | async-start | bytes 4718592 | tf_op jit(solution)/shard_map/reduce_scatter | solution.py:232
  751.1 9.8 %copy-start.80 = (f32[100,64]{0,1:T(8,128)S(1)}, f32[100,64]{0,1:T(8,128)}, u32[]{:S(2)}) copy-start(f32[100,64]{0,1:T(8,128)} %param.34) | copy-start | bytes 76804
  751.1 9.8 %copy-start.85 = (f32[100,64]{0,1:T(8,128)S(1)}, f32[100,64]{0,1:T(8,128)}, u32[]{:S(2)}) copy-start(f32[100,64]{0,1:T(8,128)} %param.38) | copy-start | bytes 76804
  751.1 9.8 %copy-start.86 = (f32[100,64]{0,1:T(8,128)S(1)}, f32[100,64]{0,1:T(8,128)}, u32[]{:S(2)}) copy-start(f32[100,64]{0,1:T(8,128)} %param.39) | copy-start | bytes 76804
  751.1 60.1 %copy-start.55 = (f32[64,2048]{1,0:T(8,128)S(1)}, f32[64,2048]{1,0:T(8,128)}, u32[]{:S(2)}) copy-start(f32[64,2048]{1,0:T(8,128)} %param.35) | copy-start | bytes 1572868
  751.1 60.1 %copy-start.71 = (f32[64,2048]{1,0:T(8,128)S(1)}, f32[64,2048]{1,0:T(8,128)}, u32[]{:S(2)}) copy-start(f32[64,2048]{1,0:T(8,128)} %param.40) | copy-start | bytes 1572868
  751.1 60.1 %copy-start.72 = (f32[64,2048]{1,0:T(8,128)S(1)}, f32[64,2048]{1,0:T(8,128)}, u32[]{:S(2)}) copy-start(f32[64,2048]{1,0:T(8,128)} %param.41) | copy-start | bytes 1572868
  751.2 110.3 %copy-start.57 = (f32[64,2048]{1,0:T(8,128)S(1)}, f32[64,2048]{1,0:T(8,128)}, u32[]{:S(2)}) copy-start(f32[64,2048]{1,0:T(8,128)} %param.36) | copy-start | bytes 1572868
  751.3 110.3 %copy-start.73 = (f32[64,2048]{1,0:T(8,128)S(1)}, f32[64,2048]{1,0:T(8,128)}, u32[]{:S(2)}) copy-start(f32[64,2048]{1,0:T(8,128)} %param.42) | copy-start | bytes 1572868
  751.3 110.3 %copy-start.74 = (f32[64,2048]{1,0:T(8,128)S(1)}, f32[64,2048]{1,0:T(8,128)}, u32[]{:S(2)}) copy-start(f32[64,2048]{1,0:T(8,128)} %param.43) | copy-start | bytes 1572868
  (104 other events, 284.2 us)
Sparse Core Ops, SparseCore 0:
  34.9 87.3 reduce-scatter.10
  125.7 86.4 reduce-scatter.12
  476.7 50.4 all-gather.9
  566.0 50.4 all-gather.11
  621.7 106.7 all-reduce.2
Sparse Core Ops, SparseCore 1:
  43.3 30.0 all-gather.5
  227.5 42.3 all-gather.7
  634.9 30.2 reduce-scatter.20
  730.3 30.6 reduce-scatter.18
  763.2 47.9 reduce-scatter.14
  813.5 48.0 reduce-scatter.16
where the time goes:
time: 880 us; the launch traced here: 871 us
  waiting for transfers between devices  434 us (49%)
  matrix products  171 us (19%)
  local copies, waits for them, and re-layouts  79.1 us (9%)
  other arithmetic  73.6 us (8%)
  blocking collectives  68.5 us (8%)
  between operations  17.2 us (2%)
  starting transfers between devices  14.8 us (2%)
  loops' own time  14 us (2%)
    reduce_scatter x2, waiting for transfers between devices, body(): lax.psum_scatter(partial_sum, 'feat', scatter_dimension=0, tiled=True)  155 us
    psum x1, waiting for transfers between devices, body(): lax.psum(grad_enc.astype(jnp.bfloat16), 'feat').astype(jnp.float32)  93.6 us
    dot_general x20, matrix products, contract(): lax.dot_general(left, right, (((left_dim,), (right_dim,)), ((), ())), pre...  50.1 us
    reduce_scatter x1, waiting for transfers between devices, body(): lax.psum_scatter(summed[1], 'rows', scatter_dimension=0, tiled=True)  48.9 us
    reduce_scatter x1, waiting for transfers between devices, body(): lax.psum_scatter(summed[2], 'rows', scatter_dimension=0, tiled=True)  47.9 us
    all_to_all x2, waiting for transfers between devices, body(): lax.all_to_all(outgoing, 'rows', split_axis=0, concat_axis=0, tiled=True)  35.1 us
    all_to_all x1, blocking collectives, body(): lax.all_to_all(d_grouped, 'rows', split_axis=0, concat_axis=0, tiled=True)  29.1 us
    unnamed x231, local copies, waits for them, and re-layouts  23.5 us
  transfers between devices with their start and end apart: 14, of which 10 were waited for; matrix products, arithmetic and copies ran while one was open for 21% of the time, Pallas kernels for 0%

commit v1 on v0

v1 whole, which is shorter than its diff:
```python
import functools
import math

import jax
import jax.numpy as jnp
from jax import lax
from jax.experimental import pallas as pl
from jax.experimental.pallas import tpu as pltpu
from jax.sharding import PartitionSpec as P

bf16 = jnp.bfloat16
f32 = jnp.float32
HEADS = 4
STEP = 10
BIG = 3
LN2 = math.log(2.0)
LOG2E = math.log2(math.e)
SMEM = pl.BlockSpec(memory_space=pltpu.SMEM)
VMEM = pl.BlockSpec(memory_space=pltpu.VMEM)
HBM = pl.BlockSpec(memory_space=pltpu.HBM)


def dot(a, b, ca, cb):
    return lax.dot_general(a, b, (((ca,), (cb,)), ((), ())), preferred_element_type=f32)


def nn(a, b):
    return dot(a, b, 1, 0)


def nt(a, b):
    return dot(a, b, 1, 1)


def tn(a, b):
    return dot(a, b, 0, 0)


def lanes(shape):
    return lax.broadcasted_iota(jnp.int32, shape, 1)


def subl(shape):
    return lax.broadcasted_iota(jnp.int32, shape, 0)


def split3(x):
    a = x.astype(bf16).astype(f32)
    r = x - a
    b = r.astype(bf16).astype(f32)
    return a, b, r - b


def call(kernel, out_shape, *args, smem=0, scratch=(), name=None, flops=10**6, moved=10**6, mib=16, specs=None, outs=None):
    single = not isinstance(out_shape, (list, tuple))
    return pl.pallas_call(
        kernel,
        out_shape=out_shape,
        in_specs=specs or [SMEM] * smem + [VMEM] * (len(args) - smem),
        out_specs=outs or (VMEM if single else [VMEM] * len(out_shape)),
        scratch_shapes=list(scratch),
        compiler_params=pltpu.CompilerParams(vmem_limit_bytes=mib << 20),
        cost_estimate=pl.CostEstimate(flops=flops, bytes_accessed=moved, transcendentals=0),
        name=name,
    )(*args)


def shape(s, d):
    return jax.ShapeDtypeStruct(tuple(s), d)


def far(s, d):
    return pltpu.HBM(tuple(s), d)


def keep_far(x):
    return pltpu.with_memory_space_constraint(x, pltpu.HBM)


class Copies:
    def __init__(self, sems):
        self.sems, self.used, self.open = sems, 0, {}

    def start(self, key, src, dst):
        self.open[key] = pltpu.make_async_copy(src, dst, self.sems.at[self.used])
        self.used += 1
        self.open[key].start()

    def wait(self, key):
        if key in self.open:
            self.open.pop(key).wait()

    def wait_all(self):
        for key in list(self.open):
            self.wait(key)


CORE, FEAT, ZED = 0, 1, 2


def starts(seg_ref, m, T):
    q = T // 4
    first = seg_ref[m, 0, 0, 0] == seg_ref[m, 0, 0, q]
    big = jnp.where(first, 0, q)
    small = jnp.where(first, 3 * q, 0)
    return pl.multiple_of(big, q), pl.multiple_of(small, q)


def neighbourhoods(seg_ref, m, T):
    q = T // 4
    big, small = starts(seg_ref, m, T)
    for base, nb in ((big, BIG), (small, 4 - BIG)):
        yield base, nb, [pl.multiple_of(base + b * q, q) for b in range(nb)]


def split_rows(acc, core, keep_ref, send_ref, cols):
    nz, dl = keep_ref.shape[0], keep_ref.shape[1]
    for z in range(nz):
        mine = pl.multiple_of((2 * z + core) * dl, 8)
        other = pl.multiple_of((2 * z + 1 - core) * dl, 8)
        keep_ref[z, :, cols] = acc[pl.ds(mine, dl), :].astype(bf16)
        send_ref[z, :, cols] = acc[pl.ds(other, dl), :].astype(bf16)


def pack_kernel(WA, idx_ref, attn_ref, ffn_ref, enc_ref, vec_ref, out_ref, attn_s, ffn_s, enc_s, vec_s, x_s, sems):
    D3, Dl, q = WA - 128, enc_s.shape[0], out_ref.shape[0]
    D = D3 // 3
    rows = slice(None) if q == Dl else pl.ds(pl.multiple_of(idx_ref[FEAT] * q, q), q)
    copies = Copies(sems)
    for key, src, dst in (("e", enc_ref, enc_s), ("v", vec_ref, vec_s), ("a", attn_ref.at[rows, :], attn_s), ("f", ffn_ref.at[rows, :], ffn_s)):
        copies.start(key, src, dst)
    copies.wait("e")
    copies.wait("v")
    p = split3(vec_s[...])
    none = jnp.zeros((1, Dl), f32)
    t = jnp.concatenate([x[0:1] for x in p] + [none] + [x[1:6] for x in p] + [jnp.zeros((9, Dl), f32)], axis=0)
    x_s[...] = jnp.concatenate([enc_s[...], t.T], axis=1)
    out_ref[:, D3:WA] = x_s[rows, :].astype(bf16)
    copies.wait("a")
    out_ref[:, 0:D3] = attn_s[:, 0:D3].astype(bf16)
    out_ref[:, WA : WA + D] = attn_s[:, D3:].astype(bf16)
    copies.wait("f")
    out_ref[:, WA + D :] = ffn_s[...].astype(bf16)


def join_kernel(idx_ref, *refs):
    a_ref, b_ref = refs[-2:]
    A = a_ref.shape[2]
    for j, ref in enumerate(refs[:-2]):
        a_ref[idx_ref[ZED] ^ j] = ref[:, 0:A]
        b_ref[idx_ref[ZED] ^ j] = ref[:, A:]


def assemble(idx_ref, pieces, dst):
    if len(pieces) == 1:
        dst[...] = pieces[0][...]
        return
    nz, q, _ = pieces[0].shape
    nfeat = len(pieces) // 2
    for c in range(2):
        for k in range(nfeat):
            for j in range(nz):
                r = (j * 2 + (idx_ref[CORE] ^ c)) * (nfeat * q) + (idx_ref[FEAT] ^ k) * q
                dst[pl.ds(pl.multiple_of(r, q), q), :] = pieces[c * nfeat + k][j]


def one_hot(order, T):
    return jnp.where(subl((T, order.shape[1])) == order, 1.0, 0.0).astype(bf16)


def sort_kernel(idx_ref, mine_ref, theirs_ref, own_ref, sibling_ref, out_ref, s_ref):
    nfeat, M, f, T = own_ref.shape
    nz, nf, n = out_ref.shape[0], out_ref.shape[3], out_ref.shape[4]
    s_ref[nfeat * f :, :] = jnp.where(subl((nf - nfeat * f, T)) < 3, 1.0, 0.0)
    for s, (order_ref, x_ref) in enumerate(((mine_ref, own_ref), (theirs_ref, sibling_ref))):
        core = idx_ref[CORE] ^ s
        for m in range(M):
            for g in range(nfeat):
                s_ref[g * f : (g + 1) * f, :] = x_ref[g, m].astype(f32)
            y = nn(s_ref[...].astype(bf16), one_hot(order_ref[m], T)).astype(bf16)
            for z in range(nz):
                out_ref[z, core, m] = y[:, z * n : (z + 1) * n]


def pick_kernel(idx_ref, *refs):
    mine_ref, other_ref = refs[-2:]
    for j, ref in enumerate(refs[:-2]):
        mine_ref[idx_ref[ZED] ^ j] = ref[idx_ref[CORE]]
        other_ref[idx_ref[ZED] ^ j] = ref[1 - idx_ref[CORE]]


def unsort_kernel(mine_ref, other_ref, x_ref, got_ref, out_ref, s_ref):
    nz = x_ref.shape[0]
    nfeat, M, f, T = out_ref.shape
    for m in range(M):
        mine = jnp.concatenate([x_ref[z, m] for z in range(nz)], axis=1)
        other = jnp.concatenate([got_ref[z, m] for z in range(nz)], axis=1)
        s_ref[...] = nt(mine, one_hot(mine_ref[m], T)) + nt(other, one_hot(other_ref[m], T))
        for g in range(nfeat):
            out_ref[g, m] = s_ref[g * f : (g + 1) * f, :].astype(bf16)


def attend_kernel(idx_ref, seg_ref, ctx_ref, y_ref, *refs):
    pieces, refs = refs[:-17], refs[-17:]
    vec_ref, h_out, o_out, qkv_out, ext_out, wa_out, x_out, h_ref, o_ref, qkv_ref, ext_ref, wa_ref, wev_ref, kext_s, diag_s, e_s, sems = refs
    M, T, D = h_ref.shape
    Q, HD = T // 4, D // HEADS
    R, _, nf, n = y_ref.shape
    copies = Copies(sems)
    copies.start("x", y_ref, x_out)
    assemble(idx_ref, pieces, wa_ref)
    copies.start("wa", wa_ref, wa_out)
    t = wa_ref[:, 3 * D :].astype(f32).T
    wev_ref[...] = t.astype(bf16)
    vec_ref[...] = jnp.concatenate([jnp.zeros((1, D), f32), t[104:109] + t[109:114] + t[114:119], jnp.zeros((2, D), f32)], axis=0)
    wev = wev_ref[0:nf, :]
    c = LOG2E * HD**-0.5
    qext = jnp.where(lanes((Q, 128)) == 0, 1.0, 0.0).astype(bf16)
    lane = lanes((Q, 128))
    for m in range(M):
        for r in range(R):
            h_ref[m, r * n : (r + 1) * n, :] = tn(y_ref[r, m], wev).astype(bf16)
    copies.start("h", h_ref, h_out)
    for m in range(M):
        h = h_ref[m]
        qkv_ref[m, :, 0:D] = (nn(h, wa_ref[:, 0:D]) * c).astype(bf16)
        qkv_ref[m, :, D : 3 * D] = nn(h, wa_ref[:, D : 3 * D]).astype(bf16)
        copies.start(("qkv", m), qkv_ref.at[m], qkv_out.at[m])
        bias = jnp.where(ctx_ref[m, 0] == 1, 0.0, -1e30).astype(f32)
        bcol = jnp.broadcast_to(bias, (128, T)).T
        kext_s[...] = jnp.where(lanes((T, 128)) == 0, bcol, 0.0).astype(bf16)
        for b in range(4):
            row = jnp.broadcast_to(bias[:, b * Q : (b + 1) * Q], (Q, Q))
            diag_s[b] = jnp.where(subl((Q, Q)) == lanes((Q, Q)), 0.0, row)
        for base, nb, rows in neighbourhoods(seg_ref, m, T):
            every = pl.ds(base, nb * Q)
            exts = [jnp.where(lane == 12, 1.0, 0.0) for _ in range(nb)]
            for hd in range(HEADS):
                cq = slice(hd * HD, (hd + 1) * HD)
                ck = slice(D + hd * HD, D + (hd + 1) * HD)
                cv = slice(2 * D + hd * HD, 2 * D + (hd + 1) * HD)
                tops = []
                for qb in range(nb):
                    q = qkv_ref[m, pl.ds(rows[qb], Q), cq]
                    qa = jnp.concatenate([q, qext], axis=1)
                    s = []
                    for kb in range(nb):
                        k = qkv_ref[m, pl.ds(rows[kb], Q), ck]
                        if kb == qb:
                            s.append(nt(q, k) + diag_s[rows[kb] // Q])
                        else:
                            s.append(nt(qa, jnp.concatenate([k, kext_s[pl.ds(rows[kb], Q), :]], axis=1)))
                    top = jnp.max(functools.reduce(jnp.maximum, s), axis=1, keepdims=True)
                    tops.append(top)
                    for kb in range(nb):
                        e_s[hd % 2, qb * Q : (qb + 1) * Q, kb * Q : (kb + 1) * Q] = jnp.exp2(s[kb] - top).astype(bf16)
                v = qkv_ref[m, every, cv]
                acc = nn(e_s[hd % 2, 0 : nb * Q, 0 : nb * Q], jnp.concatenate([v, jnp.ones((nb * Q, 128), bf16)], axis=1))
                total = acc[:, HD:]
                o_ref[m, every, cq] = (acc[:, :HD] / total).astype(bf16)
                for qb in range(nb):
                    lse = tops[qb] + jnp.log2(total[qb * Q : (qb + 1) * Q])
                    for j, part in enumerate(split3(lse)):
                        exts[qb] = jnp.where(lane == 3 * hd + j, part, exts[qb])
            for qb in range(nb):
                ext_ref[m, pl.ds(rows[qb], Q), :] = exts[qb].astype(bf16)
        copies.start(("ext", m), ext_ref.at[m], ext_out.at[m])
        copies.start(("o", m), o_ref.at[m], o_out.at[m])
    copies.wait_all()


def gelu_parts(u):
    cdf = 0.5 + 0.5 * lax.erf(u * (2.0**-0.5))
    pdf = jnp.exp2(u * u * (-0.5 * LOG2E)) * (1.0 / math.sqrt(2.0 * math.pi))
    return cdf, pdf


def colsum(x):
    return jnp.sum(x.reshape(x.shape[0] // 8, 8, x.shape[1]), axis=0)


def mean(x):
    return jnp.mean(x, axis=1, keepdims=True)


def feed_kernel(np_, ng, idx_ref, vec_ref, h_hbm, o_hbm, cot_hbm, *refs):
    pieces, refs = refs[:np_], refs[np_:]
    gb_outs, refs = refs[:ng], refs[ng:]
    act_ref, da_out, do_out, dext_out, gv_ref, h_ref, o_ref, da_ref, do_ref, dext_ref, gb_ref, wb_s, cot_ref, y1_s, gr_s, db_s, du_s, act_s, sems = refs
    M, T, D = h_ref.shape
    F, HD, B = 2 * D, D // HEADS, T // 2
    wo, w1, w2 = slice(0, D), slice(D, D + F), slice(D + F, D + 2 * F)
    copies = Copies(sems)
    for m in range(M):
        copies.start(("o", m), o_hbm.at[m], o_ref.at[m])
        copies.start(("h", m), h_hbm.at[m], h_ref.at[m])
        copies.start(("cot", m), cot_hbm.at[m], cot_ref.at[m])
    assemble(idx_ref, pieces, wb_s)
    g1, s1, g2, s2, b2 = (vec_ref[j : j + 1, :] for j in range(1, 6))
    lane = lanes((B, 128))
    vsum = [0.0] * 5

    def chain(m, b):
        r = slice(b * B, (b + 1) * B)
        w = slice(m * T + b * B, m * T + (b + 1) * B)
        copies.wait(("o", m))
        o = o_ref[m, r, :]
        t = nn(o, wb_s[:, wo])
        yield
        copies.wait(("h", m))
        a = h_ref[m, r, :].astype(f32) + t
        ac = a - mean(a)
        i1 = lax.rsqrt(mean(ac * ac) + 1e-5)
        xh1 = ac * i1
        y1 = xh1 * g1 + s1
        y1b = y1.astype(bf16)
        y1_s[w, :] = y1b
        u = nn(y1b, wb_s[:, w1])
        yield
        cdf, pdf = gelu_parts(u)
        gr = (u * cdf).astype(bf16)
        gr_s[w, :] = gr
        dgelu = cdf + u * pdf
        t = nt(gr, wb_s[:, w2])
        yield
        z = y1 + t + b2
        zc = z - mean(z)
        i2 = lax.rsqrt(mean(zc * zc) + 1e-5)
        xh2 = zc * i2
        copies.wait(("act", b))
        act_s[b] = xh2 * g2 + s2
        copies.start(("act", b), act_s.at[b], act_ref.at[m, 0, pl.ds(b * B, B), :])
        copies.wait(("cot", m))
        c = cot_ref[m, 0, r, :].astype(f32)
        vsum[2] += colsum(c * xh2)
        vsum[3] += colsum(c)
        cg = c * g2
        db = i2 * (cg - mean(cg) - xh2 * mean(cg * xh2))
        vsum[4] += colsum(db)
        dbr = db.astype(bf16)
        db_s[w, :] = dbr
        t = nn(dbr, wb_s[:, w2])
        yield
        du = (t * dgelu).astype(bf16)
        du_s[w, :] = du
        t = nt(du, wb_s[:, w1])
        yield
        dy = db + t
        vsum[0] += colsum(dy * xh1)
        vsum[1] += colsum(dy)
        cg = dy * g1
        da = i1 * (cg - mean(cg) - xh1 * mean(cg * xh1))
        dar = da.astype(bf16)
        da_ref[w, :] = dar
        do = nt(dar, wb_s[:, wo]).astype(bf16)
        yield
        do_ref[m, r, :] = do
        od = o.astype(f32) * do.astype(f32)
        ext = jnp.zeros((B, 128), f32)
        for hd in range(HEADS):
            delta = jnp.sum(od[:, hd * HD : (hd + 1) * HD], axis=1, keepdims=True)
            for j, part in enumerate(split3(delta)):
                ext = jnp.where(lane == 3 * hd + j, part, ext)
        dext_ref[m, r, :] = ext.astype(bf16)
        copies.start(("da", m, b), da_ref.at[w, :], da_out.at[w, :])
        copies.start(("do", m, b), do_ref.at[m, r, :], do_out.at[m, r, :])
        copies.start(("dext", m, b), dext_ref.at[m, r, :], dext_out.at[m, r, :])

    for m in range(M):
        gens = [chain(m, b) for b in range(2)]
        for _ in range(7):
            for g in gens:
                next(g, None)
    gv_ref[...] = jnp.concatenate([jnp.zeros((1, D), f32)] + [jnp.sum(x, axis=0, keepdims=True) for x in vsum] + [jnp.zeros((2, D), f32)], axis=0)
    left = {wo.start: (o_ref[...].reshape(M * T, D), da_ref), w1.start: (y1_s, du_s), w2.start: (db_s, gr_s)}
    for cols in (w2, w1, wo):
        a, b = left[cols.start]
        g = tn(a[...], b[...]).astype(bf16)
        if ng == 1:
            gb_ref[:, cols] = g
            copies.start(("gb", cols.start), gb_ref.at[:, cols], gb_outs[0].at[:, cols])
        else:
            nr, q, _ = gb_outs[0].shape
            gb_ref[:, :, :, cols] = g.reshape(nr, ng, q, g.shape[1])
            for k, out in enumerate(gb_outs):
                copies.start(("gb", cols.start, k), gb_ref.at[:, idx_ref[FEAT] ^ k, :, cols], out.at[:, :, cols])
    copies.wait_all()


def back_kernel(nz, idx_ref, seg_ref, ctx_ref, gv_ref, do_hbm, dext_hbm, da_hbm, qkv_hbm, ext_hbm, h_hbm, wa_hbm, x_hbm, *refs):
    outs, refs = refs[:nz], refs[nz:]
    keep_ref, send_ref, do_ref, dext_ref, da_ref, qkv_ref, ext_ref, h_ref, wa_ref, x_ref, dqkv_s, kb_s, ku_s, diag_s, p_s, ds_s, acc_s, accx_s, dh_s, sems = refs
    M, T, D = do_ref.shape
    Q, HD = T // 4, D // HEADS
    nf, n = x_ref.shape[2], x_ref.shape[3]
    scale = HD**-0.5
    copies = Copies(sems)
    for m in range(M):
        for key, src, dst in (("ext", ext_hbm, ext_ref), ("qkv", qkv_hbm, qkv_ref), ("dext", dext_hbm, dext_ref), ("do", do_hbm, do_ref)):
            copies.start((key, m), src.at[m], dst.at[m])
    for key, src, dst in (("da", da_hbm, da_ref), ("h", h_hbm, h_ref), ("wa", wa_hbm, wa_ref), ("x", x_hbm, x_ref)):
        copies.start(key, src, dst)
    lane = lanes((T, 128))
    for m in range(M):
        bias = jnp.where(ctx_ref[m, 0] == 1, 0.0, -1e30).astype(f32)
        bcol = jnp.broadcast_to(bias, (128, T)).T
        for hd in range(HEADS):
            un = jnp.where((lane >= 3 * hd) & (lane < 3 * hd + 3), -1.0, 0.0)
            if m == 0:
                ku_s[hd] = un[:Q].astype(bf16)
            kb_s[hd] = jnp.where(lane == 12, bcol, un).astype(bf16)
        for b in range(4):
            col = bcol[b * Q : (b + 1) * Q, 0:1]
            diag_s[b] = jnp.where(subl((Q, Q)) == lanes((Q, Q)), 0.0, jnp.broadcast_to(col, (Q, Q)))
        for key in ("ext", "qkv", "dext", "do"):
            copies.wait((key, m))
        for base, nb, rows in neighbourhoods(seg_ref, m, T):
            every = pl.ds(base, nb * Q)
            out = pl.ds(pl.multiple_of(m * T + base, Q), nb * Q)
            w = nb * Q
            for hd in range(HEADS):
                cq = slice(hd * HD, (hd + 1) * HD)
                ck = slice(D + hd * HD, D + (hd + 1) * HD)
                cv = slice(2 * D + hd * HD, 2 * D + (hd + 1) * HD)
                for qb in range(nb):
                    here = pl.ds(rows[qb], Q)
                    qa = jnp.concatenate([qkv_ref[m, here, cq], ext_ref[m, here, :]], axis=1)
                    da = jnp.concatenate([do_ref[m, here, cq], dext_ref[m, here, :]], axis=1)
                    for kb in range(nb):
                        k = qkv_ref[m, pl.ds(rows[kb], Q), ck]
                        v = qkv_ref[m, pl.ds(rows[kb], Q), cv]
                        if kb == qb:
                            s = nt(jnp.concatenate([k, ku_s[hd]], axis=1), qa) + diag_s[rows[kb] // Q]
                        else:
                            s = nt(jnp.concatenate([k, kb_s[hd, pl.ds(rows[kb], Q), :]], axis=1), qa)
                        p = jnp.exp2(s)
                        dp = nt(jnp.concatenate([v, ku_s[hd]], axis=1), da)
                        p_s[hd % 2, kb * Q : (kb + 1) * Q, qb * Q : (qb + 1) * Q] = p.astype(bf16)
                        ds_s[hd % 2, kb * Q : (kb + 1) * Q, qb * Q : (qb + 1) * Q] = (p * dp).astype(bf16)
                p, ds = p_s[hd % 2, 0:w, 0:w], ds_s[hd % 2, 0:w, 0:w]
                dqkv_s[out, cv] = nn(p, do_ref[m, every, cq]).astype(bf16)
                dqkv_s[out, ck] = (nn(ds, qkv_ref[m, every, cq]) * LN2).astype(bf16)
                dqkv_s[out, cq] = (tn(qkv_ref[m, every, ck], ds) * scale).T.astype(bf16)
    for key in ("wa", "x", "da"):
        copies.wait(key)
    wev = wa_ref[:, 3 * D :].astype(f32).T.astype(bf16)[0:nf, :]
    dh_s[...] = (da_ref[...].astype(f32) + nt(dqkv_s[...], wa_ref[:, 0 : 3 * D])).astype(bf16)
    e = None
    for m in range(M):
        for j in range(nz):
            for s in range(2):
                r = (idx_ref[ZED] ^ j) * 2 + s
                dh = dh_s[pl.ds(pl.multiple_of(m * T + r * n, n), n), :]
                outs[j][s, m] = nt(wev, dh).astype(bf16)
                t = nn(x_ref[r, m], dh)
                e = t if e is None else e + t
    rest = jnp.concatenate([e[100:101], gv_ref[1:6, :], jnp.zeros((128 - nf - 6, D), f32)], axis=0)
    accx_s[...] = jnp.concatenate([e, rest], axis=0).T
    core = idx_ref[CORE]
    split_rows(accx_s, core, keep_ref, send_ref, slice(3 * D, 3 * D + 128))
    copies.wait("h")
    acc_s[...] = tn(h_ref[...].reshape(M * T, D), dqkv_s[...])
    split_rows(acc_s, core, keep_ref, send_ref, slice(0, 3 * D))


def core_kernel(keep_ref, got_ref, out_ref):
    nfeat, _, q, _ = out_ref.shape
    for g in range(nfeat):
        rows = slice(g * q, (g + 1) * q)
        out_ref[g] = (keep_ref[:, rows, :].astype(f32) + got_ref[:, rows, :].astype(f32)).astype(bf16)


def feat_kernel(na, idx_ref, a_ref, *refs):
    bs, outs = refs[:na], refs[na:]
    A = a_ref.shape[3]
    for j, out in enumerate(outs):
        out[:, 0:A] = sum(a_ref[g, idx_ref[ZED] ^ j].astype(f32) for g in range(a_ref.shape[0])).astype(bf16)
        if bs:
            out[:, A:] = bs[j][...]


def cut_kernel(idx_ref, x_ref, *outs):
    q = outs[0].shape[0]
    for g in range(len(outs)):
        for k, out in enumerate(outs):

            @pl.when((idx_ref[FEAT] ^ k) == g)
            def _():
                out[...] = x_ref[g * q : (g + 1) * q, :]


def feat_b_kernel(idx_ref, *refs):
    keep_ref, send_ref = refs[-2:]
    for z in range(keep_ref.shape[0]):
        for c, out in ((idx_ref[CORE], keep_ref), (1 - idx_ref[CORE], send_ref)):
            out[z] = sum(x[2 * z + c].astype(f32) for x in refs[:-2]).astype(bf16)


def core_b_kernel(idx_ref, keep_ref, got_ref, *outs):
    for j, out in enumerate(outs):
        z = idx_ref[ZED] ^ j
        out[...] = (keep_ref[z].astype(f32) + got_ref[z].astype(f32)).astype(bf16)


def rows_kernel(na, *refs):
    out = refs[-1]
    W = refs[0].shape[1]
    out[:, 0:W] = sum(x[...].astype(f32) for x in refs[:na]).astype(bf16)
    if len(refs) > na + 1:
        out[:, W:] = sum(x[...].astype(f32) for x in refs[na:-1]).astype(bf16)


def update(w, g, m, v, rate):
    m = 0.9 * m + 0.1 * g
    v = 0.95 * v + 0.05 * g * g
    return w - rate * ((m / (1.0 - 0.9**STEP)) / (jnp.sqrt(v / (1.0 - 0.95**STEP)) + 1e-8) + 0.1 * w), m, v


def adam_kernel(nfeat, idx_ref, *refs):
    gs, refs = refs[:nfeat], refs[nfeat:]
    ins, outs, held, g_s, sems = refs[:12], refs[12:24], refs[24:36], refs[36], refs[37]
    copies = Copies(sems)
    small = (0, 1, 2, 9, 10, 11)
    for i in small:
        copies.start(("in", i), ins[i], held[i])
    q = gs[0].shape[0]
    for k in range(nfeat):
        for f in range(nfeat):

            @pl.when((idx_ref[FEAT] ^ k) == f)
            def _():
                g_s[f * q : (f + 1) * q, :] = gs[k][...].astype(f32)

    D = ins[3].shape[1] // 4
    F, A = ins[0].shape[1], 3 * D + 128

    def step(i, g, rate):
        state = [(held if i + j in small else ins)[i + j][...] for j in range(3)]
        for j, x in enumerate(update(state[0], g, state[1], state[2], rate)):
            held[i + j][...] = x
            copies.start(("out", i + j), held[i + j], outs[i + j])

    step(6, g_s[:, A + D :], 0.02)
    step(3, jnp.concatenate([g_s[:, 0 : 3 * D], g_s[:, A : A + D]], axis=1), 0.25)
    for i in small:
        copies.wait(("in", i))
    x = g_s[:, 3 * D : A]
    step(0, x[:, 0:F], 0.08)
    step(9, x.T[104:110, :], 0.2)
    copies.wait_all()


def peer(x, axis, size, k):
    return lax.ppermute(x, axis, [(i, i ^ k) for i in range(size)])


def tie(x, *others):
    return lax.optimization_barrier((x, *others))[0]


def body(features, feat_mask, send_order, segment, context, cotangent, w_enc, w_attn, w_ffn, vectors, m_enc, v_enc, m_attn, v_attn, m_ffn, v_ffn, m_vec, v_vec):
    nfeat, nr = lax.axis_size("feat"), lax.axis_size("rows")
    nz = nr // 2
    fi, ri = lax.axis_index("feat"), lax.axis_index("rows")
    ci, zi = ri % 2, ri // 2
    idx = jnp.stack([ci, fi, zi]).astype(jnp.int32)
    M, tok, fl = features.shape
    T, F = tok // nfeat, fl * nfeat
    nf = -(-(F + 3) // 8) * 8
    Dl = w_attn.shape[0]
    D = Dl * nr
    n, q = T // nr, Dl // nfeat
    WA, WB = 3 * D + 128, 5 * D
    over_feat = lambda x: [x] + [peer(x, "feat", nfeat, k) for k in range(1, nfeat)]
    groups = [[2 * z + c for z in range(nz)] for c in range(2)]
    over_z = lambda x: [x] + [peer(x, "rows", nr, 2 * k) for k in range(1, nz)]
    to_z = lambda xs: [xs[0]] + [peer(xs[k], "rows", nr, 2 * k) for k in range(1, nz)]
    to_feat = lambda xs: [xs[0]] + [peer(xs[k], "feat", nfeat, k) for k in range(1, nfeat)]
    swap_z = lambda x: lax.all_to_all(x, "rows", 0, 0, axis_index_groups=groups, tiled=True)
    swap_feat = lambda x: lax.all_to_all(x, "feat", 0, 0, tiled=True)
    over_core = lambda x: peer(x, "rows", nr, 1)

    by_quarters = q % 16 == 0
    part_rows = q if by_quarters else Dl
    pack = call(
        functools.partial(pack_kernel, WA), shape((part_rows, WA + WB), bf16), idx, *[keep_far(a) for a in (w_attn, w_ffn, w_enc.T, vectors)],
        name="pack", flops=3 * 10**9, specs=[SMEM] + [HBM] * 4,
        scratch=[pltpu.VMEM(a, f32) for a in ((part_rows, 4 * D), (part_rows, 4 * D), w_enc.T.shape, vectors.shape)] + [pltpu.VMEM((Dl, 128), f32), pltpu.SemaphoreType.DMA((4,))],
    )
    order = send_order.reshape(M, nz, 2, n)
    order_mine = jnp.where(ci == 0, order[:, :, 0], order[:, :, 1]).reshape(M, 1, T // 2)
    order_other = jnp.where(ci == 0, order[:, :, 1], order[:, :, 0]).reshape(M, 1, T // 2)
    order_theirs = over_core(order_other)
    mask = feat_mask.transpose(2, 0, 1)
    xm = tie(features, pack).transpose(2, 0, 1) * mask.astype(bf16)
    xm = xm.reshape(fl, M, nfeat, T).transpose(2, 1, 0, 3)

    xm = swap_feat(xm)
    if by_quarters:
        pa, pb = call(join_kernel, [shape((nz, q, WA), bf16), shape((nz, q, WB), bf16)], idx, *over_z(pack), smem=1, name="join", flops=10**9)
        xm = tie(xm, pa)
        pa = over_feat(pa)
    x = call(
        sort_kernel, shape((nz, 2, M, nf, n), bf16), idx, order_mine, order_theirs, xm, over_core(xm),
        smem=1, scratch=[pltpu.VMEM((nf, T), f32)], name="sort", flops=3 * 10**9,
    )
    if by_quarters:
        pa = [pa[0]] + [tie(a, x) for a in pa[1:]]
        pa = pa + [over_core(a) for a in pa]
        pb = over_feat(tie(pb, x))
    else:
        pa = [lax.all_gather(pack[:, :WA], "rows", axis=0, tiled=True)]
        pb = [lax.all_gather(pack[:, WA:], "rows", axis=0, tiled=True)]
    x = swap_z(x).reshape(nr, M, nf, n)

    Q = T // 4
    dma = lambda k: pltpu.SemaphoreType.DMA((k,))
    ram = lambda d, *r: pltpu.VMEM(r, d)
    vec, h, o, qkv, ext, wa, x = call(
        attend_kernel,
        [far((8, D), f32), far((M, T, D), bf16), far((M, T, D), bf16), far((M, T, 3 * D), bf16), far((M, T, 128), bf16), far((D, WA), bf16), far((nr, M, nf, n), bf16)],
        idx, segment, context, x, *pa,
        smem=2, name="attend", flops=16 * 10**9, mib=36, outs=[VMEM] + [HBM] * 6,
        scratch=[ram(bf16, M, T, D), ram(bf16, M, T, D), ram(bf16, M, T, 3 * D), ram(bf16, M, T, 128), ram(bf16, D, WA), ram(bf16, 128, D), ram(bf16, T, 128), ram(f32, 4, Q, Q), ram(bf16, 2, BIG * Q, BIG * Q), dma(3 + 3 * M)],
    )

    if by_quarters:
        pb = [pb[0]] + [tie(a, o) for a in pb[1:]]
        pb = pb + [over_core(a) for a in pb]
    ng = nfeat if by_quarters else 1
    *grads_b, act, da, do, dext, gv = call(
        functools.partial(feed_kernel, len(pb), ng),
        [far((nr, q, WB) if by_quarters else (D, WB), bf16)] * ng
        + [far((M, 1, T, D), f32), far((M * T, D), bf16), far((M, T, D), bf16), far((M, T, 128), bf16), far((8, D), f32)],
        idx, keep_far(vec), *[keep_far(a) for a in (h, o, cotangent)], *pb,
        name="feed", flops=29 * 10**9, mib=56, specs=[SMEM, VMEM] + [HBM] * 3 + [VMEM] * len(pb), outs=[HBM] * (ng + 4) + [VMEM],
        scratch=[ram(bf16, M, T, D), ram(bf16, M, T, D), ram(bf16, M * T, D), ram(bf16, M, T, D), ram(bf16, M, T, 128), ram(bf16, *((nr, nfeat, q, WB) if by_quarters else (D, WB))), ram(bf16, D, WB), ram(bf16, M, 1, T, D), ram(bf16, M * T, D), ram(bf16, M * T, 2 * D), ram(bf16, M * T, D), ram(bf16, M * T, 2 * D), ram(f32, 2, T // 2, D), dma(3 * ng + 11 * M)],
    )
    if by_quarters:
        grads_b = to_feat(grads_b)
    else:
        sum_b = lax.psum_scatter(grads_b[0], "rows", scatter_dimension=0, tiled=True)

    *dxs, keep_a, send_a = call(
        functools.partial(back_kernel, nz),
        [shape((2, M, nf, n), bf16)] * nz + [shape((nz, Dl, WA), bf16)] * 2,
        idx, segment, context, keep_far(gv), *[keep_far(a) for a in (do, dext, da, qkv, ext, h, wa, x)],
        name="back", flops=29 * 10**9, mib=50, specs=[SMEM] * 2 + [VMEM] * 2 + [HBM] * 8,
        scratch=[ram(bf16, M, T, D), ram(bf16, M, T, 128), ram(bf16, M * T, D), ram(bf16, M, T, 3 * D), ram(bf16, M, T, 128), ram(bf16, M, T, D), ram(bf16, D, WA), ram(bf16, nr, M, nf, n), ram(bf16, M * T, 3 * D),
            ram(bf16, HEADS, T, 128), ram(bf16, HEADS, Q, 128), ram(f32, 4, Q, Q), ram(bf16, 2, BIG * Q, BIG * Q), ram(bf16, 2, BIG * Q, BIG * Q),
            ram(f32, D, 3 * D), ram(f32, D, 128), ram(bf16, M * T, D), dma(4 + 4 * M)],
    )

    got_a = over_core(send_a)
    if by_quarters:
        grads_b[0] = tie(grads_b[0], keep_a)
        keep_b, send_b = call(feat_b_kernel, [shape((nz, q, WB), bf16)] * 2, idx, *grads_b, smem=1, name="feat_sum_b", flops=10**9)
        got_b = over_core(send_b)
        keep_a = tie(keep_a, keep_b)
    part = call(core_kernel, shape((nfeat, nz, q, WA), bf16), keep_a, got_a, name="core_sum", flops=10**9)
    if by_quarters:
        sums = call(core_b_kernel, [shape((q, WB), bf16)] * nz, idx, tie(keep_b, part), got_b, smem=1, name="core_sum_b", flops=10**9)
        dxs[0] = tie(dxs[0], *sums)
    else:
        dxs[0] = tie(dxs[0], part)
        sums = to_feat(call(cut_kernel, [shape((q, WB), bf16)] * nfeat, idx, tie(sum_b, part), smem=1, name="cut", flops=10**9))
    dxs[1:] = [tie(a, part) for a in dxs[1:]]
    dxs = to_z(dxs)
    part = swap_feat(part)
    mine, other = call(pick_kernel, [shape((nz, M, nf, n), bf16)] * 2, idx, *dxs, smem=1, name="pick", flops=10**9)
    dx = call(
        unsort_kernel, shape((nfeat, M, fl, T), bf16), order_mine, order_other, mine, over_core(other),
        scratch=[pltpu.VMEM((nf, T), f32)], name="unsort", flops=3 * 10**9,
    )
    part = tie(part, dx)
    dx = swap_feat(dx)
    beside, sums = (sums, []) if by_quarters else ([], sums)
    part = to_z(call(functools.partial(feat_kernel, len(beside)), [shape((q, WA + len(beside) // nz * WB), bf16)] * nz, idx, part, *beside, smem=1, name="feat_sum", flops=10**9))
    grads = over_feat(call(functools.partial(rows_kernel, nz), shape((q, WA + WB), bf16), *part, *sums, name="rows_sum", flops=10**9))
    x_grad = dx.transpose(2, 1, 0, 3).reshape(fl, M, tok).astype(f32) * mask.astype(f32)
    state = [w_enc.T, m_enc.T, v_enc.T, w_attn, m_attn, v_attn, w_ffn, m_ffn, v_ffn, vectors, m_vec, v_vec]
    far_state = [keep_far(a) if a.size < Dl * D else a for a in state]
    new = call(
        functools.partial(adam_kernel, nfeat), [far(a.shape, f32) for a in state], idx, *grads, *far_state,
        specs=[SMEM] + [VMEM] * nfeat + [HBM if a.size < Dl * D else VMEM for a in state], outs=[HBM] * 12, scratch=[pltpu.VMEM(a.shape, f32) for a in state] + [pltpu.VMEM((Dl, WA + WB), f32), dma(18)], name="adamw", flops=4 * 10**9,
    )
    return (act, x_grad.transpose(1, 2, 0), *[x.T for x in new[:3]], *new[3:])


def solution(mesh):
    tok, grp = P(None, "rows", "feat"), P(None, "feat", "rows", None)
    col, row = P(None, "rows"), P("rows", None)
    return jax.shard_map(
        body,
        mesh=mesh,
        in_specs=(tok, tok, P(None, "rows", "feat", None), grp, grp, grp, col, row, row, col, col, col, row, row, row, row, col, col),
        out_specs=(grp, tok) + (col,) * 3 + (row,) * 6 + (col,) * 3,
        check_vma=False,
    )
```

time: 880 us -> 184 us (0.21)
  waiting for transfers between devices: 434 us -> 45.4 us
  matrix products: 171 us -> 0 us
  Pallas kernels: 0 us -> 82.1 us
  local copies, waits for them, and re-layouts: 79.1 us -> 3.51 us
  other arithmetic: 73.6 us -> 2.22 us
  blocking collectives: 68.5 us -> 0 us
  starting transfers between devices: 14.8 us -> 45.9 us
  between operations: 17.2 us -> 1.57 us
  loops' own time: 14 us -> 0 us
    reduce_scatter x4 -> x0, waiting for transfers between devices: 252 us -> none  [the longest x2 155 us: body(): lax.psum_scatter(partial_sum, 'feat', scatter_dimension=0, tiled=True)]
    dot_general x58 -> x0, matrix products: 171 us -> none  [the longest x20 50.1 us: contract(): lax.dot_general(left, right, (((left_dim,), (right_dim,)), ((), ())), pre...]
    psum x1 -> x0, waiting for transfers between devices: 93.6 us -> none  [body(): lax.psum(grad_enc.astype(jnp.bfloat16), 'feat').astype(jnp.float32)]
    pallas_call x0 -> x14, Pallas kernels: none -> 82.1 us  [call(): pl.pallas_call(kernel, out_shape=out_shape, in_specs=specs or [SMEM] * sm...]
    all_to_all x3 -> x4, waiting for transfers between devices: 58.1 us -> 2.75 us  [the longest x3 2.75 us: body(): swap_feat = lambda x: lax.all_to_all(x, 'feat', 0, 0, tiled=True)]
    ppermute x0 -> x34, waiting for transfers between devices: none -> 42.7 us  [peer(): return lax.ppermute(x, axis, [(i, i ^ k) for i in range(size)])]
    ppermute x0 -> x34, starting transfers between devices: none -> 29.9 us  [peer(): return lax.ppermute(x, axis, [(i, i ^ k) for i in range(size)])]
    all_gather x2 -> x0, blocking collectives: 29.8 us -> none  [the longest x1 15.7 us: body(): lax.all_gather(w_enc, 'rows', axis=1, tiled=True)]
  transfers between devices with their start and end apart: 14 -> 38, of which waited for: 10 -> 19; matrix products, arithmetic and copies ran while one was open for 21% -> 2% of each run, Pallas kernels for 0% -> 26%
where the time goes in v1:
time: 184 us; the launch traced here: 181 us
  Pallas kernels  82.1 us (45%)
  starting transfers between devices  45.9 us (25%)
  waiting for transfers between devices  45.4 us (25%)
  local copies, waits for them, and re-layouts  3.51 us (2%)
  other arithmetic  2.22 us (1%)
    pallas_call x14, Pallas kernels, call(): pl.pallas_call(kernel, out_shape=out_shape, in_specs=specs or [SMEM] * sm...  82.1 us
    ppermute x34, waiting for transfers between devices, peer(): return lax.ppermute(x, axis, [(i, i ^ k) for i in range(size)])  42.7 us
    ppermute x34, starting transfers between devices, peer(): return lax.ppermute(x, axis, [(i, i ^ k) for i in range(size)])  29.9 us
    all_to_all x3, starting transfers between devices, body(): swap_feat = lambda x: lax.all_to_all(x, 'feat', 0, 0, tiled=True)  12.1 us
    all_to_all x1, starting transfers between devices, body(): lax.all_to_all(x, 'rows', 0, 0, axis_index_groups=groups, tiled=True)  3.93 us
  transfers between devices with their start and end apart: 38, of which 19 were waited for; matrix products, arithmetic and copies ran while one was open for 2% of the time, Pallas kernels for 26%

profile of v1, /device:TPU:0, one launch (start us, length us, event | category | flops | bytes accessed | tf_op | source)
XLA Modules:
  0.0 180.7 jit_solution(10162329066511912615)
XLA Ops:
  0.7 1.6 pack.1.refs_0_
  3.1 1.1 copy.40
  4.2 5.2 %all-to-all-start = ((bf16[4,2,25,1024]{3,1,2,0:T(2,128)(2,1)}), bf16[4,2,25,1024]{3,1,2,0:T(2,128)(2,1)S(1)}, u32[]{:S(2)}, u32[]{:S(2)}) async-start(bf16[4,2,25,1024]{3,1,2,0:T(2,128)(2,1)} %copy.40), calls=%async_computation | async-start | bytes 819200 | tf_op jit(solution)/shard_map/all_to_all | solution.py:580
  9.4 3.6 %collective-permute-start.3 = (bf16[16,4224]{1,0:T(8,128)(2,1)S(1)}, bf16[16,4224]{1,0:T(8,128)(2,1)S(1)}, u32[]{:S(2)}, u32[]{:S(2)}) collective-permute-start(bf16[16,4224]{1,0:T(8,128)(2,1)S(1)} %pack.1.refs_0_), channel_id=1, source_target_pairs={{0,6},{1,7},{2,4},{3,5},{4,2},{5,3},{6,0},{7,1},{8,14},{9,15},{10,... | collective-permute-start | bytes 405512 | tf_op jit(solution)/shard_map/ppermute | solution.py:554
  13.0 0.8 collective-permute-start.1
  13.8 4.0 %collective-permute-done.3.refs_3_ = bf16[16,4224]{1,0:T(8,128)(2,1)S(1)} collective-permute-done((bf16[16,4224]{1,0:T(8,128)(2,1)S(1)}, bf16[16,4224]{1,0:T(8,128)(2,1)S(1)}, u32[]{:S(2)}, u32[]{:S(2)}) %collective-permute-start.3) | collective-permute-done | bytes 135200 | tf_op jit(solution)/shard_map/ppermute | solution.py:554
  17.7 6.5 %collective-permute-done.2.refs_2_ = bf16[16,4224]{1,0:T(8,128)(2,1)S(1)} collective-permute-done((bf16[16,4224]{1,0:T(8,128)(2,1)S(1)}, bf16[16,4224]{1,0:T(8,128)(2,1)S(1)}, u32[]{:S(2)}, u32[]{:S(2)}) %collective-permute-start.2) | collective-permute-done | bytes 135200 | tf_op jit(solution)/shard_map/ppermute | solution.py:554
  24.2 0.6 join.1
  25.6 1.3 collective-permute-done.theirs_ref
  26.9 2.3 %sort.1 = bf16[4,2,2,104,128]{4,3,2,1,0:T(8,128)(2,1)} custom-call(s32[3]{0:T(128)S(1)} %pad_add_fusion.idx_ref, s32[2,1,512]{2,1,0:T(1,128)S(1)} %bitcast.35, s32[2,1,512]{2,1,0:T(1,128)S(1)} %collective-permute-done.theirs_ref, bf16[4,2,25,1024]{3,2,1,0:T(8,128)(2,1)S(1)} %copy.42.own_ref, bf16[4,2,25,1024]{3,2,1,0:T(8,128)(2,1)S(1)} %collective-permute-done.4.sibling_ref), custom_call_target="tpu_custom_call" | custom-call | flops 3000000000 | bytes 1000000 | tf_op jit(solution)/shard_map/sort/pallas_call | solution.py:56
  29.3 3.9 %all-to-all-start.1 = ((bf16[4,2,2,104,128]{4,3,2,1,0:T(8,128)(2,1)}), bf16[4,2,2,104,128]{4,3,2,1,0:T(8,128)(2,1)S(1)}, u32[]{:S(2)}, u32[]{:S(2)}) async-start(bf16[4,2,2,104,128]{4,3,2,1,0:T(8,128)(2,1)} %sort.1), calls=%async_computation.1 | async-start | bytes 851968 | tf_op jit(solution)/shard_map/all_to_all | solution.py:579
  33.2 2.6 %collective-permute-start.7 = (bf16[4,16,1664]{2,1,0:T(8,128)(2,1)S(1)}, bf16[4,16,1664]{2,1,0:T(8,128)(2,1)S(1)}, u32[]{:S(2)}, u32[]{:S(2)}) collective-permute-start(bf16[4,16,1664]{2,1,0:T(8,128)(2,1)S(1)} %get-tuple-element.80.refs_0_), channel_id=1, source_target_pairs={{0,24},{8,16},{16,8},{24,0},{1,25},{9,17},{17,9},{25,1},{2,26},{10... | collective-permute-start | bytes 638984 | tf_op jit(solution)/shard_map/ppermute | solution.py:554
  36.8 5.6 %collective-permute-done.7.refs_3_ = bf16[4,16,1664]{2,1,0:T(8,128)(2,1)S(1)} collective-permute-done((bf16[4,16,1664]{2,1,0:T(8,128)(2,1)S(1)}, bf16[4,16,1664]{2,1,0:T(8,128)(2,1)S(1)}, u32[]{:S(2)}, u32[]{:S(2)}) %collective-permute-start.7) | collective-permute-done | bytes 213024 | tf_op jit(solution)/shard_map/ppermute | solution.py:554
  42.4 3.4 %collective-permute-done.6.refs_2_ = bf16[4,16,1664]{2,1,0:T(8,128)(2,1)S(1)} collective-permute-done((bf16[4,16,1664]{2,1,0:T(8,128)(2,1)S(1)}, bf16[4,16,1664]{2,1,0:T(8,128)(2,1)S(1)}, u32[]{:S(2)}, u32[]{:S(2)}) %collective-permute-start.6) | collective-permute-done | bytes 213024 | tf_op jit(solution)/shard_map/ppermute | solution.py:554
  47.0 1.5 collective-permute-start.14
  48.6 1.4 collective-permute-start.13
  50.6 14.9 %attend.1 = (f32[8,512]{1,0:T(8,128)}, bf16[2,1024,512]{2,1,0:T(8,128)(2,1)}, bf16[2,1024,512]{2,1,0:T(8,128)(2,1)}, bf16[2,1024,1536]{2,1,0:T(8,128)(2,1)}, bf1...) custom-call(s32[3]{0:T(128)S(1)} %pad_add_fusion.idx_ref, ...), custom_call_target="tpu_custom_call" | custom-call | flops 16000000000 | bytes 1000000 | tf_op jit(solution)/shard_map/attend/pallas_call | solution.py:56
  66.1 1.2 collective-permute-done.16.refs_5_
  68.8 27.9 %feed.1 = (bf16[8,16,2560]{2,1,0:T(8,128)(2,1)}, bf16[8,16,2560]{2,1,0:T(8,128)(2,1)}, bf16[8,16,2560]{2,1,0:T(8,128)(2,1)}, bf16[8,16,2560]{2,1,0:T(8,128)(2,1)...) custom-call(s32[3]{0:T(128)} %copy-done, ...), custom_call_target="tpu_custom_call" | custom-call | flops 28999999488 | bytes 1000000 | tf_op jit(solution)/shard_map/feed/pallas_call | solution.py:56
  96.8 1.5 collective-permute-start.19
  98.3 0.6 collective-permute-start.20
  98.9 1.4 collective-permute-start.21
  100.3 26.3 %back.1 = (bf16[2,2,104,128]{3,2,1,0:T(8,128)(2,1)S(1)}, bf16[2,2,104,128]{3,2,1,0:T(8,128)(2,1)S(1)}, bf16[2,2,104,128]{3,2,1,0:T(8,128)(2,1)S(1)}, bf16[2,2,10...) custom-call(s32[3]{0:T(128)S(1)} %copy-done.1, ...), custom_call_target="tpu_custom_call" | custom-call | flops 28999999488 | bytes 1000000 | tf_op jit(solution)/shard_map/back/pallas_call | solution.py:56
  126.7 2.4 %collective-permute-done.20.refs_2_ = bf16[8,16,2560]{2,1,0:T(8,128)(2,1)S(1)} collective-permute-done((bf16[8,16,2560]{2,1,0:T(8,128)(2,1)}, bf16[8,16,2560]{2,1,0:T(8,128)(2,1)S(1)}, u32[]{:S(2)}, u32[]{:S(2)}) %collective-permute-start.20) | collective-permute-done | bytes 655392 | tf_op jit(solution)/shard_map/ppermute | solution.py:554
  129.0 0.9 feat_sum_b.1
  130.0 1.2 core_sum.1
  131.2 1.7 collective-permute-start.24
  132.9 2.4 %collective-permute-start.25 = (bf16[2,2,104,128]{3,2,1,0:T(8,128)(2,1)S(1)}, bf16[2,2,104,128]{3,2,1,0:T(8,128)(2,1)S(1)}, u32[]{:S(2)}, u32[]{:S(2)}) collective-permute-start(bf16[2,2,104,128]{3,2,1,0:T(8,128)(2,1)S(1)} %get-tuple-element.122), channel_id=1, source_target_pairs={{0,4},{1,5},{2,6},{3,7},{4,0},{5,1},{6,2},{7,3},{8,12},{9,13},{10,... | collective-permute-start | bytes 319496 | tf_op jit(solution)/shard_map/ppermute | solution.py:554
  135.6 3.5 %all-to-all-start.3 = ((bf16[4,4,16,1664]{3,2,1,0:T(8,128)(2,1)}), bf16[4,4,16,1664]{3,2,1,0:T(8,128)(2,1)S(1)}, u32[]{:S(2)}, u32[]{:S(2)}) async-start(bf16[4,4,16,1664]{3,2,1,0:T(8,128)(2,1)} %core_sum.1), calls=%async_computation.3 | async-start | bytes 1703936 | tf_op jit(solution)/shard_map/all_to_all | solution.py:580
  139.1 0.6 core_sum_b.1
  139.7 4.4 %collective-permute-done.25.refs_2_ = bf16[2,2,104,128]{3,2,1,0:T(8,128)(2,1)S(1)} collective-permute-done((bf16[2,2,104,128]{3,2,1,0:T(8,128)(2,1)S(1)}, bf16[2,2,104,128]{3,2,1,0:T(8,128)(2,1)S(1)}, u32[]{:S(2)}, u32[]{:S(2)}) %collective-permute-start.25) | collective-permute-done | bytes 106528 | tf_op jit(solution)/shard_map/ppermute | solution.py:554
  144.2 0.6 pick.1
  144.8 1.5 collective-permute-done.27.got_ref
  146.3 1.5 unsort.1
  147.8 1.2 copy.43
  149.0 1.7 all-to-all-done.3.a_ref
  150.7 3.5 %all-to-all-start.2 = ((bf16[4,2,25,1024]{3,1,2,0:T(2,128)(2,1)}), bf16[4,2,25,1024]{3,1,2,0:T(2,128)(2,1)S(1)}, u32[]{:S(2)}, u32[]{:S(2)}) async-start(bf16[4,2,25,1024]{3,1,2,0:T(2,128)(2,1)} %copy.43), calls=%async_computation.2 | async-start | bytes 819200 | tf_op jit(solution)/shard_map/all_to_all | solution.py:580
  154.1 0.7 feat_sum.1
  154.8 0.9 collective-permute-start.28
  155.7 3.3 %collective-permute-start.29 = (bf16[16,4224]{1,0:T(8,128)(2,1)S(1)}, bf16[16,4224]{1,0:T(8,128)(2,1)S(1)}, u32[]{:S(2)}, u32[]{:S(2)}) collective-permute-start(bf16[16,4224]{1,0:T(8,128)(2,1)S(1)} %get-tuple-element.130), channel_id=1, source_target_pairs={{0,4},{1,5},{2,6},{3,7},{4,0},{5,1},{6,2},{7,3},{8,12},{9,13},{10,... | collective-permute-start | bytes 405512 | tf_op jit(solution)/shard_map/ppermute | solution.py:554
  159.3 1.1 all-to-all-done.2
  160.7 0.9 collective-permute-done.28.refs_1_
  161.6 7.3 %collective-permute-done.29.refs_2_ = bf16[16,4224]{1,0:T(8,128)(2,1)S(1)} collective-permute-done((bf16[16,4224]{1,0:T(8,128)(2,1)S(1)}, bf16[16,4224]{1,0:T(8,128)(2,1)S(1)}, u32[]{:S(2)}, u32[]{:S(2)}) %collective-permute-start.29) | collective-permute-done | bytes 135200 | tf_op jit(solution)/shard_map/ppermute | solution.py:554
  169.0 2.6 %collective-permute-start.33 = (bf16[16,4224]{1,0:T(8,128)(2,1)S(1)}, bf16[16,4224]{1,0:T(8,128)(2,1)S(1)}, u32[]{:S(2)}, u32[]{:S(2)}) collective-permute-start(bf16[16,4224]{1,0:T(8,128)(2,1)S(1)} %rows_sum.1.refs_0_), channel_id=1, source_target_pairs={{0,24},{8,16},{16,8},{24,0},{1,25},{9,17},{17,9},{25,1},{2,26},{10... | collective-permute-start | bytes 405512 | tf_op jit(solution)/shard_map/ppermute | solution.py:554
  172.5 1.4 fusion
  173.9 1.1 collective-permute-done.33.refs_3_
  175.0 1.7 collective-permute-done.32.refs_2_
  177.2 3.0 %adamw.1 = (f32[64,100]{1,0:T(8,128)}, f32[64,100]{1,0:T(8,128)}, f32[64,100]{1,0:T(8,128)}, f32[64,2048]{1,0:T(8,128)}, f32[64,2048]{1,0:T(8,128)}, /*index=5*/...) custom-call(s32[3]{0:T(128)S(1)} %copy-done.1, ...), custom_call_target="tpu_custom_call" | custom-call | flops 4000000000 | bytes 1000000 | tf_op jit(solution)/shard_map/adamw/pallas_call | solution.py:56
  (97 shorter events, 9.3 us)
Async XLA Ops:
  0.7 49.8 %copy-start = (s32[3]{0:T(128)}, s32[3]{0:T(128)S(1)}, u32[]{:S(2)}) copy-start(s32[3]{0:T(128)S(1)} %pad_add_fusion.idx_ref) | copy-start | bytes 40
  4.2 20.6 %all-to-all-start = ((bf16[4,2,25,1024]{3,1,2,0:T(2,128)(2,1)}), bf16[4,2,25,1024]{3,1,2,0:T(2,128)(2,1)S(1)}, u32[]{:S(2)}, u32[]{:S(2)}) async-start(bf16[4,2,25,1024]{3,1,2,0:T(2,128)(2,1)} %copy.40), calls=%async_computation | async-start | bytes 819200 | tf_op jit(solution)/shard_map/all_to_all | solution.py:580
  9.4 8.3 %collective-permute-start.3 = (bf16[16,4224]{1,0:T(8,128)(2,1)S(1)}, bf16[16,4224]{1,0:T(8,128)(2,1)S(1)}, u32[]{:S(2)}, u32[]{:S(2)}) collective-permute-start(bf16[16,4224]{1,0:T(8,128)(2,1)S(1)} %pack.1.refs_0_), channel_id=1, source_target_pairs={{0,6},{1,7},{2,4},{3,5},{4,2},{5,3},{6,0},{7,1},{8,14},{9,15},{10,... | collective-permute-start | bytes 405512 | tf_op jit(solution)/shard_map/ppermute | solution.py:554
  13.0 11.2 %collective-permute-start.2 = (bf16[16,4224]{1,0:T(8,128)(2,1)S(1)}, bf16[16,4224]{1,0:T(8,128)(2,1)S(1)}, u32[]{:S(2)}, u32[]{:S(2)}) collective-permute-start(bf16[16,4224]{1,0:T(8,128)(2,1)S(1)} %pack.1.refs_0_), channel_id=1, source_target_pairs={{0,4},{1,5},{2,6},{3,7},{4,0},{5,1},{6,2},{7,3},{8,12},{9,13},{10,... | collective-permute-start | bytes 405512 | tf_op jit(solution)/shard_map/ppermute | solution.py:554
  13.0 11.2 %collective-permute-start.1 = (bf16[16,4224]{1,0:T(8,128)(2,1)S(1)}, bf16[16,4224]{1,0:T(8,128)(2,1)S(1)}, u32[]{:S(2)}, u32[]{:S(2)}) collective-permute-start(bf16[16,4224]{1,0:T(8,128)(2,1)S(1)} %pack.1.refs_0_), channel_id=1, source_target_pairs={{0,2},{1,3},{2,0},{3,1},{4,6},{5,7},{6,4},{7,5},{8,10},{9,11},{10,... | collective-permute-start | bytes 405512 | tf_op jit(solution)/shard_map/ppermute | solution.py:554
  13.7 11.3 %copy-start.15 = (s32[2,1,1,1024]{3,2,1,0:T(1,128)S(1)}, s32[2,1,1,1024]{3,2,1,0:T(1,128)}, u32[]{:S(2)}) copy-start(s32[2,1,1,1024]{3,2,1,0:T(1,128)} %param.20) | copy-start | bytes 24580
  24.8 25.2 %copy-start.8 = (bf16[4,16,2560]{2,1,0:T(8,128)(2,1)}, bf16[4,16,2560]{2,1,0:T(8,128)(2,1)S(1)}, u32[]{:S(2)}) copy-start(bf16[4,16,2560]{2,1,0:T(8,128)(2,1)S(1)} %get-tuple-element.89.refs_0_) | copy-start | bytes 983044
  24.9 2.0 %collective-permute-start.4 = (bf16[4,2,25,1024]{3,2,1,0:T(8,128)(2,1)S(1)}, bf16[4,2,25,1024]{3,2,1,0:T(8,128)(2,1)S(1)}, u32[]{:S(2)}, u32[]{:S(2)}) collective-permute-start(bf16[4,2,25,1024]{3,2,1,0:T(8,128)(2,1)S(1)} %copy.42.own_ref), channel_id=1, source_target_pairs={{0,1},{1,0},{2,3},{3,2},{4,5},{5,4},{6,7},{7,6},{8,9},{9,8},{10,11... | collective-permute-start | bytes 1228808 | tf_op jit(solution)/shard_map/ppermute | solution.py:554
  25.1 1.9 %collective-permute-start = (s32[2,1,512]{2,1,0:T(1,128)S(1)}, s32[2,1,512]{2,1,0:T(1,128)S(1)}, u32[]{:S(2)}, u32[]{:S(2)}) collective-permute-start(s32[2,1,512]{2,1,0:T(1,128)S(1)} %bitcast.33), channel_id=1, source_target_pairs={{0,1},{1,0},{2,3},{3,2},{4,5},{5,4},{6,7},{7,6},{8,9},{9,8},{10,11... | collective-permute-start | bytes 12296 | tf_op jit(solution)/shard_map/ppermute | solution.py:554
  26.9 23.6 %copy-start.9 = (s32[2,1,1,1024]{3,2,1,0:T(1,128)S(1)}, s32[2,1,1,1024]{3,2,1,0:T(1,128)}, u32[]{:S(2)}) copy-start(s32[2,1,1,1024]{3,2,1,0:T(1,128)} %seg_ref.3) | copy-start | bytes 24580
  26.9 23.6 %copy-start.10 = (s32[2,1,1,1024]{3,2,1,0:T(1,128)S(1)}, s32[2,1,1,1024]{3,2,1,0:T(1,128)}, u32[]{:S(2)}) copy-start(s32[2,1,1,1024]{3,2,1,0:T(1,128)} %ctx_ref.3) | copy-start | bytes 24580
  29.3 21.3 %all-to-all-start.1 = ((bf16[4,2,2,104,128]{4,3,2,1,0:T(8,128)(2,1)}), bf16[4,2,2,104,128]{4,3,2,1,0:T(8,128)(2,1)S(1)}, u32[]{:S(2)}, u32[]{:S(2)}) async-start(bf16[4,2,2,104,128]{4,3,2,1,0:T(8,128)(2,1)} %sort.1), calls=%async_computation.1 | async-start | bytes 851968 | tf_op jit(solution)/shard_map/all_to_all | solution.py:579
  33.2 9.1 %collective-permute-start.7 = (bf16[4,16,1664]{2,1,0:T(8,128)(2,1)S(1)}, bf16[4,16,1664]{2,1,0:T(8,128)(2,1)S(1)}, u32[]{:S(2)}, u32[]{:S(2)}) collective-permute-start(bf16[4,16,1664]{2,1,0:T(8,128)(2,1)S(1)} %get-tuple-element.80.refs_0_), channel_id=1, source_target_pairs={{0,24},{8,16},{16,8},{24,0},{1,25},{9,17},{17,9},{25,1},{2,26},{10... | collective-permute-start | bytes 638984 | tf_op jit(solution)/shard_map/ppermute | solution.py:554
  35.8 10.0 %collective-permute-start.6 = (bf16[4,16,1664]{2,1,0:T(8,128)(2,1)S(1)}, bf16[4,16,1664]{2,1,0:T(8,128)(2,1)S(1)}, u32[]{:S(2)}, u32[]{:S(2)}) collective-permute-start(bf16[4,16,1664]{2,1,0:T(8,128)(2,1)S(1)} %get-tuple-element.80.refs_0_), channel_id=1, source_target_pairs={{0,16},{8,24},{16,0},{24,8},{1,17},{9,25},{17,1},{25,9},{2,18},{10... | collective-permute-start | bytes 638984 | tf_op jit(solution)/shard_map/ppermute | solution.py:554
  36.4 9.6 %collective-permute-start.5 = (bf16[4,16,1664]{2,1,0:T(8,128)(2,1)S(1)}, bf16[4,16,1664]{2,1,0:T(8,128)(2,1)S(1)}, u32[]{:S(2)}, u32[]{:S(2)}) collective-permute-start(bf16[4,16,1664]{2,1,0:T(8,128)(2,1)S(1)} %get-tuple-element.80.refs_0_), channel_id=1, source_target_pairs={{0,8},{8,0},{16,24},{24,16},{1,9},{9,1},{17,25},{25,17},{2,10},{10... | collective-permute-start | bytes 638984 | tf_op jit(solution)/shard_map/ppermute | solution.py:554
  36.8 10.3 %collective-permute-start.8 = (bf16[4,16,1664]{2,1,0:T(8,128)(2,1)S(1)}, bf16[4,16,1664]{2,1,0:T(8,128)(2,1)S(1)}, u32[]{:S(2)}, u32[]{:S(2)}) collective-permute-start(bf16[4,16,1664]{2,1,0:T(8,128)(2,1)S(1)} %get-tuple-element.80.refs_0_), channel_id=1, source_target_pairs={{0,1},{1,0},{2,3},{3,2},{4,5},{5,4},{6,7},{7,6},{8,9},{9,8},{10,11... | collective-permute-start | bytes 638984 | tf_op jit(solution)/shard_map/ppermute | solution.py:554
  46.0 2.6 %collective-permute-start.9 = (bf16[4,16,1664]{2,1,0:T(8,128)(2,1)S(1)}, bf16[4,16,1664]{2,1,0:T(8,128)(2,1)S(1)}, u32[]{:S(2)}, u32[]{:S(2)}) collective-permute-start(bf16[4,16,1664]{2,1,0:T(8,128)(2,1)S(1)} %collective-permute-done.5.refs_1_), channel_id=1, source_target_pairs={{0,1},{1,0},{2,3},{3,2},{4,5},{5,4},{6,7},{7,6},{8,9},{9,8},{10,11... | collective-permute-start | bytes 638984 | tf_op jit(solution)/shard_map/ppermute | solution.py:554
  46.0 4.0 %collective-permute-start.10 = (bf16[4,16,1664]{2,1,0:T(8,128)(2,1)S(1)}, bf16[4,16,1664]{2,1,0:T(8,128)(2,1)S(1)}, u32[]{:S(2)}, u32[]{:S(2)}) collective-permute-start(bf16[4,16,1664]{2,1,0:T(8,128)(2,1)S(1)} %collective-permute-done.6.refs_2_), channel_id=1, source_target_pairs={{0,1},{1,0},{2,3},{3,2},{4,5},{5,4},{6,7},{7,6},{8,9},{9,8},{10,11... | collective-permute-start | bytes 638984 | tf_op jit(solution)/shard_map/ppermute | solution.py:554
  46.5 4.0 %collective-permute-start.11 = (bf16[4,16,1664]{2,1,0:T(8,128)(2,1)S(1)}, bf16[4,16,1664]{2,1,0:T(8,128)(2,1)S(1)}, u32[]{:S(2)}, u32[]{:S(2)}) collective-permute-start(bf16[4,16,1664]{2,1,0:T(8,128)(2,1)S(1)} %collective-permute-done.7.refs_3_), channel_id=1, source_target_pairs={{0,1},{1,0},{2,3},{3,2},{4,5},{5,4},{6,7},{7,6},{8,9},{9,8},{10,11... | collective-permute-start | bytes 638984 | tf_op jit(solution)/shard_map/ppermute | solution.py:554
  46.5 19.6 %collective-permute-start.15 = (bf16[4,16,2560]{2,1,0:T(8,128)(2,1)S(1)}, bf16[4,16,2560]{2,1,0:T(8,128)(2,1)S(1)}, u32[]{:S(2)}, u32[]{:S(2)}) collective-permute-start(bf16[4,16,2560]{2,1,0:T(8,128)(2,1)S(1)} %get-tuple-element.89.refs_0_), channel_id=1, source_target_pairs={{0,1},{1,0},{2,3},{3,2},{4,5},{5,4},{6,7},{7,6},{8,9},{9,8},{10,11... | collective-permute-start | bytes 983048 | tf_op jit(solution)/shard_map/ppermute | solution.py:554
  47.0 18.4 %collective-permute-start.14 = (bf16[4,16,2560]{2,1,0:T(8,128)(2,1)S(1)}, bf16[4,16,2560]{2,1,0:T(8,128)(2,1)S(1)}, u32[]{:S(2)}, u32[]{:S(2)}) collective-permute-start(bf16[4,16,2560]{2,1,0:T(8,128)(2,1)S(1)} %get-tuple-element.89.refs_0_), channel_id=1, source_target_pairs={{0,24},{8,16},{16,8},{24,0},{1,25},{9,17},{17,9},{25,1},{2,26},{10... | collective-permute-start | bytes 983048 | tf_op jit(solution)/shard_map/ppermute | solution.py:554
  48.6 16.9 %collective-permute-start.13 = (bf16[4,16,2560]{2,1,0:T(8,128)(2,1)S(1)}, bf16[4,16,2560]{2,1,0:T(8,128)(2,1)S(1)}, u32[]{:S(2)}, u32[]{:S(2)}) collective-permute-start(bf16[4,16,2560]{2,1,0:T(8,128)(2,1)S(1)} %get-tuple-element.89.refs_0_), channel_id=1, source_target_pairs={{0,16},{8,24},{16,0},{24,8},{1,17},{9,25},{17,1},{25,9},{2,18},{10... | collective-permute-start | bytes 983048 | tf_op jit(solution)/shard_map/ppermute | solution.py:554
  50.0 15.5 %collective-permute-start.12 = (bf16[4,16,2560]{2,1,0:T(8,128)(2,1)S(1)}, bf16[4,16,2560]{2,1,0:T(8,128)(2,1)}, u32[]{:S(2)}, u32[]{:S(2)}) collective-permute-start(bf16[4,16,2560]{2,1,0:T(8,128)(2,1)S(1)} %get-tuple-element.89.refs_0_), channel_id=1, source_target_pairs={{0,8},{8,0},{16,24},{24,16},{1,9},{9,1},{17,25},{25,17},{2,10},{10... | collective-permute-start | bytes 983048 | tf_op jit(solution)/shard_map/ppermute | solution.py:554
  65.5 1.9 %collective-permute-start.16 = (bf16[4,16,2560]{2,1,0:T(8,128)(2,1)}, bf16[4,16,2560]{2,1,0:T(8,128)(2,1)S(1)}, u32[]{:S(2)}, u32[]{:S(2)}) collective-permute-start(bf16[4,16,2560]{2,1,0:T(8,128)(2,1)} %collective-permute-done.12.refs_1_), channel_id=1, source_target_pairs={{0,1},{1,0},{2,3},{3,2},{4,5},{5,4},{6,7},{7,6},{8,9},{9,8},{10,11... | collective-permute-start | bytes 983048 | tf_op jit(solution)/shard_map/ppermute | solution.py:554
  65.6 2.1 %collective-permute-start.17 = (bf16[4,16,2560]{2,1,0:T(8,128)(2,1)S(1)}, bf16[4,16,2560]{2,1,0:T(8,128)(2,1)S(1)}, u32[]{:S(2)}, u32[]{:S(2)}) collective-permute-start(bf16[4,16,2560]{2,1,0:T(8,128)(2,1)S(1)} %collective-permute-done.13.refs_2_), channel_id=1, source_target_pairs={{0,1},{1,0},{2,3},{3,2},{4,5},{5,4},{6,7},{7,6},{8,9},{9,8},{10,11... | collective-permute-start | bytes 983048 | tf_op jit(solution)/shard_map/ppermute | solution.py:554
  66.1 2.1 %collective-permute-start.18 = (bf16[4,16,2560]{2,1,0:T(8,128)(2,1)S(1)}, bf16[4,16,2560]{2,1,0:T(8,128)(2,1)S(1)}, u32[]{:S(2)}, u32[]{:S(2)}) collective-permute-start(bf16[4,16,2560]{2,1,0:T(8,128)(2,1)S(1)} %collective-permute-done.14.refs_3_), channel_id=1, source_target_pairs={{0,1},{1,0},{2,3},{3,2},{4,5},{5,4},{6,7},{7,6},{8,9},{9,8},{10,11... | collective-permute-start | bytes 983048 | tf_op jit(solution)/shard_map/ppermute | solution.py:554
  68.8 31.5 %copy-start.1 = (s32[3]{0:T(128)S(1)}, s32[3]{0:T(128)}, u32[]{:S(2)}) copy-start(s32[3]{0:T(128)} %copy-done) | copy-start | bytes 40
  96.8 29.9 %collective-permute-start.19 = (bf16[8,16,2560]{2,1,0:T(8,128)(2,1)}, bf16[8,16,2560]{2,1,0:T(8,128)(2,1)S(1)}, u32[]{:S(2)}, u32[]{:S(2)}) collective-permute-start(bf16[8,16,2560]{2,1,0:T(8,128)(2,1)} %get-tuple-element.106), channel_id=1, source_target_pairs={{0,8},{8,0},{16,24},{24,16},{1,9},{9,1},{17,25},{25,17},{2,10},{10... | collective-permute-start | bytes 1966088 | tf_op jit(solution)/shard_map/ppermute | solution.py:554
  98.3 30.8 %collective-permute-start.20 = (bf16[8,16,2560]{2,1,0:T(8,128)(2,1)}, bf16[8,16,2560]{2,1,0:T(8,128)(2,1)S(1)}, u32[]{:S(2)}, u32[]{:S(2)}) collective-permute-start(bf16[8,16,2560]{2,1,0:T(8,128)(2,1)} %get-tuple-element.107), channel_id=1, source_target_pairs={{0,16},{8,24},{16,0},{24,8},{1,17},{9,25},{17,1},{25,9},{2,18},{10... | collective-permute-start | bytes 1966088 | tf_op jit(solution)/shard_map/ppermute | solution.py:554
  98.9 30.1 %collective-permute-start.21 = (bf16[8,16,2560]{2,1,0:T(8,128)(2,1)}, bf16[8,16,2560]{2,1,0:T(8,128)(2,1)S(1)}, u32[]{:S(2)}, u32[]{:S(2)}) collective-permute-start(bf16[8,16,2560]{2,1,0:T(8,128)(2,1)} %get-tuple-element.108), channel_id=1, source_target_pairs={{0,24},{8,16},{16,8},{24,0},{1,25},{9,17},{17,9},{25,1},{2,26},{10... | collective-permute-start | bytes 1966088 | tf_op jit(solution)/shard_map/ppermute | solution.py:554
  100.3 28.7 %copy-start.11 = (bf16[8,16,2560]{2,1,0:T(8,128)(2,1)S(1)}, bf16[8,16,2560]{2,1,0:T(8,128)(2,1)}, u32[]{:S(2)}) copy-start(bf16[8,16,2560]{2,1,0:T(8,128)(2,1)} %get-tuple-element.105.refs_0_) | copy-start | bytes 1966084
  126.6 3.4 %collective-permute-start.22 = (bf16[4,64,1664]{2,1,0:T(8,128)(2,1)S(1)}, bf16[4,64,1664]{2,1,0:T(8,128)(2,1)S(1)}, u32[]{:S(2)}, u32[]{:S(2)}) collective-permute-start(bf16[4,64,1664]{2,1,0:T(8,128)(2,1)S(1)} %get-tuple-element.111), channel_id=1, source_target_pairs={{0,1},{1,0},{2,3},{3,2},{4,5},{5,4},{6,7},{7,6},{8,9},{9,8},{10,11... | collective-permute-start | bytes 2555912 | tf_op jit(solution)/shard_map/ppermute | solution.py:554
  129.9 9.2 %collective-permute-start.23 = (bf16[4,16,2560]{2,1,0:T(8,128)(2,1)S(1)}, bf16[4,16,2560]{2,1,0:T(8,128)(2,1)S(1)}, u32[]{:S(2)}, u32[]{:S(2)}) collective-permute-start(bf16[4,16,2560]{2,1,0:T(8,128)(2,1)S(1)} %get-tuple-element.113), channel_id=1, source_target_pairs={{0,1},{1,0},{2,3},{3,2},{4,5},{5,4},{6,7},{7,6},{8,9},{9,8},{10,11... | collective-permute-start | bytes 983048 | tf_op jit(solution)/shard_map/ppermute | solution.py:554
  131.2 8.5 %collective-permute-start.24 = (bf16[2,2,104,128]{3,2,1,0:T(8,128)(2,1)S(1)}, bf16[2,2,104,128]{3,2,1,0:T(8,128)(2,1)S(1)}, u32[]{:S(2)}, u32[]{:S(2)}) collective-permute-start(bf16[2,2,104,128]{3,2,1,0:T(8,128)(2,1)S(1)} %get-tuple-element.120), channel_id=1, source_target_pairs={{0,2},{1,3},{2,0},{3,1},{4,6},{5,7},{6,4},{7,5},{8,10},{9,11},{10,... | collective-permute-start | bytes 319496 | tf_op jit(solution)/shard_map/ppermute | solution.py:554
  132.9 11.3 %collective-permute-start.25 = (bf16[2,2,104,128]{3,2,1,0:T(8,128)(2,1)S(1)}, bf16[2,2,104,128]{3,2,1,0:T(8,128)(2,1)S(1)}, u32[]{:S(2)}, u32[]{:S(2)}) collective-permute-start(bf16[2,2,104,128]{3,2,1,0:T(8,128)(2,1)S(1)} %get-tuple-element.122), channel_id=1, source_target_pairs={{0,4},{1,5},{2,6},{3,7},{4,0},{5,1},{6,2},{7,3},{8,12},{9,13},{10,... | collective-permute-start | bytes 319496 | tf_op jit(solution)/shard_map/ppermute | solution.py:554
  135.3 8.9 %collective-permute-start.26 = (bf16[2,2,104,128]{3,2,1,0:T(8,128)(2,1)S(1)}, bf16[2,2,104,128]{3,2,1,0:T(8,128)(2,1)S(1)}, u32[]{:S(2)}, u32[]{:S(2)}) collective-permute-start(bf16[2,2,104,128]{3,2,1,0:T(8,128)(2,1)S(1)} %get-tuple-element.124), channel_id=1, source_target_pairs={{0,6},{1,7},{2,4},{3,5},{4,2},{5,3},{6,0},{7,1},{8,14},{9,15},{10,... | collective-permute-start | bytes 319496 | tf_op jit(solution)/shard_map/ppermute | solution.py:554
  135.6 15.1 %all-to-all-start.3 = ((bf16[4,4,16,1664]{3,2,1,0:T(8,128)(2,1)}), bf16[4,4,16,1664]{3,2,1,0:T(8,128)(2,1)S(1)}, u32[]{:S(2)}, u32[]{:S(2)}) async-start(bf16[4,4,16,1664]{3,2,1,0:T(8,128)(2,1)} %core_sum.1), calls=%async_computation.3 | async-start | bytes 1703936 | tf_op jit(solution)/shard_map/all_to_all | solution.py:580
  144.8 1.5 collective-permute-start.27
  150.7 9.6 %all-to-all-start.2 = ((bf16[4,2,25,1024]{3,1,2,0:T(2,128)(2,1)}), bf16[4,2,25,1024]{3,1,2,0:T(2,128)(2,1)S(1)}, u32[]{:S(2)}, u32[]{:S(2)}) async-start(bf16[4,2,25,1024]{3,1,2,0:T(2,128)(2,1)} %copy.43), calls=%async_computation.2 | async-start | bytes 819200 | tf_op jit(solution)/shard_map/all_to_all | solution.py:580
  154.8 6.8 %collective-permute-start.28 = (bf16[16,4224]{1,0:T(8,128)(2,1)S(1)}, bf16[16,4224]{1,0:T(8,128)(2,1)S(1)}, u32[]{:S(2)}, u32[]{:S(2)}) collective-permute-start(bf16[16,4224]{1,0:T(8,128)(2,1)S(1)} %get-tuple-element.129), channel_id=1, source_target_pairs={{0,2},{1,3},{2,0},{3,1},{4,6},{5,7},{6,4},{7,5},{8,10},{9,11},{10,... | collective-permute-start | bytes 405512 | tf_op jit(solution)/shard_map/ppermute | solution.py:554
  155.7 13.2 %collective-permute-start.29 = (bf16[16,4224]{1,0:T(8,128)(2,1)S(1)}, bf16[16,4224]{1,0:T(8,128)(2,1)S(1)}, u32[]{:S(2)}, u32[]{:S(2)}) collective-permute-start(bf16[16,4224]{1,0:T(8,128)(2,1)S(1)} %get-tuple-element.130), channel_id=1, source_target_pairs={{0,4},{1,5},{2,6},{3,7},{4,0},{5,1},{6,2},{7,3},{8,12},{9,13},{10,... | collective-permute-start | bytes 405512 | tf_op jit(solution)/shard_map/ppermute | solution.py:554
  159.0 9.9 %collective-permute-start.30 = (bf16[16,4224]{1,0:T(8,128)(2,1)S(1)}, bf16[16,4224]{1,0:T(8,128)(2,1)S(1)}, u32[]{:S(2)}, u32[]{:S(2)}) collective-permute-start(bf16[16,4224]{1,0:T(8,128)(2,1)S(1)} %get-tuple-element.131), channel_id=1, source_target_pairs={{0,6},{1,7},{2,4},{3,5},{4,2},{5,3},{6,0},{7,1},{8,14},{9,15},{10,... | collective-permute-start | bytes 405512 | tf_op jit(solution)/shard_map/ppermute | solution.py:554
  160.7 11.8 %copy-start.13 = (s32[2,4096,25]{1,0,2:T(2,128)S(1)}, s32[2,4096,25]{1,0,2:T(2,128)}, u32[]{:S(2)}) copy-start(s32[2,4096,25]{1,0,2:T(2,128)} %param.19) | copy-start | bytes 2457604
  168.9 8.3 %copy-start.6 = (f32[64,2048]{1,0:T(8,128)S(1)}, f32[64,2048]{1,0:T(8,128)}, u32[]{:S(2)}) copy-start(f32[64,2048]{1,0:T(8,128)} %refs_11_.1) | copy-start | bytes 1572868
  168.9 8.3 %copy-start.7 = (f32[64,2048]{1,0:T(8,128)S(1)}, f32[64,2048]{1,0:T(8,128)}, u32[]{:S(2)}) copy-start(f32[64,2048]{1,0:T(8,128)} %refs_12_.1) | copy-start | bytes 1572868
  169.0 6.0 %collective-permute-start.33 = (bf16[16,4224]{1,0:T(8,128)(2,1)S(1)}, bf16[16,4224]{1,0:T(8,128)(2,1)S(1)}, u32[]{:S(2)}, u32[]{:S(2)}) collective-permute-start(bf16[16,4224]{1,0:T(8,128)(2,1)S(1)} %rows_sum.1.refs_0_), channel_id=1, source_target_pairs={{0,24},{8,16},{16,8},{24,0},{1,25},{9,17},{17,9},{25,1},{2,26},{10... | collective-permute-start | bytes 405512 | tf_op jit(solution)/shard_map/ppermute | solution.py:554
  171.6 5.0 %collective-permute-start.32 = (bf16[16,4224]{1,0:T(8,128)(2,1)S(1)}, bf16[16,4224]{1,0:T(8,128)(2,1)S(1)}, u32[]{:S(2)}, u32[]{:S(2)}) collective-permute-start(bf16[16,4224]{1,0:T(8,128)(2,1)S(1)} %rows_sum.1.refs_0_), channel_id=1, source_target_pairs={{0,16},{8,24},{16,0},{24,8},{1,17},{9,25},{17,1},{25,9},{2,18},{10... | collective-permute-start | bytes 405512 | tf_op jit(solution)/shard_map/ppermute | solution.py:554
  172.2 5.0 %collective-permute-start.31 = (bf16[16,4224]{1,0:T(8,128)(2,1)S(1)}, bf16[16,4224]{1,0:T(8,128)(2,1)S(1)}, u32[]{:S(2)}, u32[]{:S(2)}) collective-permute-start(bf16[16,4224]{1,0:T(8,128)(2,1)S(1)} %rows_sum.1.refs_0_), channel_id=1, source_target_pairs={{0,8},{8,0},{16,24},{24,16},{1,9},{9,1},{17,25},{25,17},{2,10},{10... | collective-permute-start | bytes 405512 | tf_op jit(solution)/shard_map/ppermute | solution.py:554
  (12 other events, 45.7 us)

commit v2 on v1

--- a/solution.py
+++ b/solution.py
@@ -145,15 +145,25 @@
 
 def join_kernel(idx_ref, *refs):
     a_ref, b_ref = refs[-2:]
-    A = a_ref.shape[2]
+    A = a_ref.shape[3]
     for j, ref in enumerate(refs[:-2]):
-        a_ref[idx_ref[ZED] ^ j] = ref[:, 0:A]
-        b_ref[idx_ref[ZED] ^ j] = ref[:, A:]
+        z = idx_ref[ZED] ^ j
+        b_ref[z] = ref[:, A:]
+        for g in range(a_ref.shape[0]):
+            a_ref[g, z] = ref[:, 0:A]
 
 
 def assemble(idx_ref, pieces, dst):
     if len(pieces) == 1:
         dst[...] = pieces[0][...]
+        return
+    if len(pieces) == 2:
+        nfeat, nz, q, _ = pieces[0].shape
+        for c in range(2):
+            for g in range(nfeat):
+                for j in range(nz):
+                    r = (j * 2 + (idx_ref[CORE] ^ c)) * (nfeat * q) + g * q
+                    dst[pl.ds(pl.multiple_of(r, q), q), :] = pieces[c][g, j]
         return
     nz, q, _ = pieces[0].shape
     nfeat = len(pieces) // 2
@@ -168,18 +178,26 @@
     return jnp.where(subl((T, order.shape[1])) == order, 1.0, 0.0).astype(bf16)
 
 
-def sort_kernel(idx_ref, mine_ref, theirs_ref, own_ref, sibling_ref, out_ref, s_ref):
-    nfeat, M, f, T = own_ref.shape
-    nz, nf, n = out_ref.shape[0], out_ref.shape[3], out_ref.shape[4]
+def sort_kernel(nfeat, idx_ref, mine_ref, theirs_ref, *refs):
+    xs, outs, s_ref, y_ref = refs[: 2 * nfeat], refs[2 * nfeat : -2], refs[-2], refs[-1]
+    M, f, T = xs[0].shape
+    nz, nf, n = y_ref.shape
     s_ref[nfeat * f :, :] = jnp.where(subl((nf - nfeat * f, T)) < 3, 1.0, 0.0)
-    for s, (order_ref, x_ref) in enumerate(((mine_ref, own_ref), (theirs_ref, sibling_ref))):
+    for s, order_ref in enumerate((mine_ref, theirs_ref)):
         core = idx_ref[CORE] ^ s
         for m in range(M):
-            for g in range(nfeat):
-                s_ref[g * f : (g + 1) * f, :] = x_ref[g, m].astype(f32)
+            for k in range(nfeat):
+                for g in range(nfeat):
+
+                    @pl.when((idx_ref[FEAT] ^ k) == g)
+                    def _():
+                        s_ref[g * f : (g + 1) * f, :] = xs[s * nfeat + k][m].astype(f32)
+
             y = nn(s_ref[...].astype(bf16), one_hot(order_ref[m], T)).astype(bf16)
             for z in range(nz):
-                out_ref[z, core, m] = y[:, z * n : (z + 1) * n]
+                y_ref[z] = y[:, z * n : (z + 1) * n]
+            for j, out in enumerate(outs):
+                out[core, m] = y_ref[idx_ref[ZED] ^ j]
 
 
 def pick_kernel(idx_ref, *refs):
@@ -200,14 +218,16 @@
             out_ref[g, m] = s_ref[g * f : (g + 1) * f, :].astype(bf16)
 
 
-def attend_kernel(idx_ref, seg_ref, ctx_ref, y_ref, *refs):
+def attend_kernel(nz, idx_ref, seg_ref, ctx_ref, *refs):
+    ys, refs = refs[:nz], refs[nz:]
     pieces, refs = refs[:-17], refs[-17:]
     vec_ref, h_out, o_out, qkv_out, ext_out, wa_out, x_out, h_ref, o_ref, qkv_ref, ext_ref, wa_ref, wev_ref, kext_s, diag_s, e_s, sems = refs
     M, T, D = h_ref.shape
     Q, HD = T // 4, D // HEADS
-    R, _, nf, n = y_ref.shape
+    nf, n = ys[0].shape[2], ys[0].shape[3]
     copies = Copies(sems)
-    copies.start("x", y_ref, x_out)
+    for j in range(nz):
+        copies.start(("x", j), ys[j], x_out.at[pl.ds(2 * (idx_ref[ZED] ^ j), 2)])
     assemble(idx_ref, pieces, wa_ref)
     copies.start("wa", wa_ref, wa_out)
     t = wa_ref[:, 3 * D :].astype(f32).T
@@ -218,8 +238,10 @@
     qext = jnp.where(lanes((Q, 128)) == 0, 1.0, 0.0).astype(bf16)
     lane = lanes((Q, 128))
     for m in range(M):
-        for r in range(R):
-            h_ref[m, r * n : (r + 1) * n, :] = tn(y_ref[r, m], wev).astype(bf16)
+        for j in range(nz):
+            for s in range(2):
+                r = pl.multiple_of(((idx_ref[ZED] ^ j) * 2 + s) * n, n)
+                h_ref[m, pl.ds(r, n), :] = tn(ys[j][s, m], wev).astype(bf16)
     copies.start("h", h_ref, h_out)
     for m in range(M):
         h = h_ref[m]
@@ -592,36 +614,39 @@
     order_other = jnp.where(ci == 0, order[:, :, 1], order[:, :, 0]).reshape(M, 1, T // 2)
     order_theirs = over_core(order_other)
     mask = feat_mask.transpose(2, 0, 1)
-    xm = tie(features, pack).transpose(2, 0, 1) * mask.astype(bf16)
-    xm = xm.reshape(fl, M, nfeat, T).transpose(2, 1, 0, 3)
-
-    xm = swap_feat(xm)
+    feats = tie(features, pack).transpose(2, 0, 1)
+    xs = []
+    for k in range(nfeat):
+        part = lambda a: lax.dynamic_slice_in_dim(a, (fi ^ k) * T, T, 2)
+        xs.append((part(feats) * part(mask).astype(bf16)).transpose(1, 0, 2))
+    xs = to_feat(xs)
     if by_quarters:
-        pa, pb = call(join_kernel, [shape((nz, q, WA), bf16), shape((nz, q, WB), bf16)], idx, *over_z(pack), smem=1, name="join", flops=10**9)
-        xm = tie(xm, pa)
-        pa = over_feat(pa)
-    x = call(
-        sort_kernel, shape((nz, 2, M, nf, n), bf16), idx, order_mine, order_theirs, xm, over_core(xm),
-        smem=1, scratch=[pltpu.VMEM((nf, T), f32)], name="sort", flops=3 * 10**9,
+        pa, pb = call(join_kernel, [shape((nfeat, nz, q, WA), bf16), shape((nz, q, WB), bf16)], idx, *over_z(pack), smem=1, name="join", flops=10**9)
+        pa = swap_feat(pa)
+    xs = xs + [over_core(x) for x in xs]
+    ys = call(
+        functools.partial(sort_kernel, nfeat), [shape((2, M, nf, n), bf16)] * nz, idx, order_mine, order_theirs, *xs,
+        smem=1, scratch=[pltpu.VMEM((nf, T), f32), pltpu.VMEM((nz, nf, n), bf16)], name="sort", flops=3 * 10**9,
     )
+    own = ys[0]
+    ys = to_z(ys)
     if by_quarters:
-        pa = [pa[0]] + [tie(a, x) for a in pa[1:]]
-        pa = pa + [over_core(a) for a in pa]
-        pb = over_feat(tie(pb, x))
+        pa = tie(pa, *ys[1:])
+        pa = [pa, over_core(pa)]
+        pb = over_feat(tie(pb, own))
     else:
         pa = [lax.all_gather(pack[:, :WA], "rows", axis=0, tiled=True)]
         pb = [lax.all_gather(pack[:, WA:], "rows", axis=0, tiled=True)]
-    x = swap_z(x).reshape(nr, M, nf, n)
 
     Q = T // 4
     dma = lambda k: pltpu.SemaphoreType.DMA((k,))
     ram = lambda d, *r: pltpu.VMEM(r, d)
     vec, h, o, qkv, ext, wa, x = call(
-        attend_kernel,
+        functools.partial(attend_kernel, nz),
         [far((8, D), f32), far((M, T, D), bf16), far((M, T, D), bf16), far((M, T, 3 * D), bf16), far((M, T, 128), bf16), far((D, WA), bf16), far((nr, M, nf, n), bf16)],
-        idx, segment, context, x, *pa,
+        idx, segment, context, *ys, *pa,
         smem=2, name="attend", flops=16 * 10**9, mib=36, outs=[VMEM] + [HBM] * 6,
-        scratch=[ram(bf16, M, T, D), ram(bf16, M, T, D), ram(bf16, M, T, 3 * D), ram(bf16, M, T, 128), ram(bf16, D, WA), ram(bf16, 128, D), ram(bf16, T, 128), ram(f32, 4, Q, Q), ram(bf16, 2, BIG * Q, BIG * Q), dma(3 + 3 * M)],
+        scratch=[ram(bf16, M, T, D), ram(bf16, M, T, D), ram(bf16, M, T, 3 * D), ram(bf16, M, T, 128), ram(bf16, D, WA), ram(bf16, 128, D), ram(bf16, T, 128), ram(f32, 4, Q, Q), ram(bf16, 2, BIG * Q, BIG * Q), dma(nz + 2 + 3 * M)],
     )
 
     if by_quarters:

time: 184 us -> 179 us (0.973)
  waiting for transfers between devices: 45.4 us -> 38.3 us
  starting transfers between devices: 45.9 us -> 47.9 us
    ppermute x34 -> x37, starting transfers between devices: 29.9 us -> 37.3 us  [peer(): return lax.ppermute(x, axis, [(i, i ^ k) for i in range(size)])]
    ppermute x34 -> x37, waiting for transfers between devices: 42.7 us -> 35.4 us  [peer(): return lax.ppermute(x, axis, [(i, i ^ k) for i in range(size)])]
    all_to_all x1 -> x0, starting transfers between devices: 3.93 us -> none  [body(): lax.all_to_all(x, 'rows', 0, 0, axis_index_groups=groups, tiled=True)]
  transfers between devices with their start and end apart: 38 -> 40, of which waited for: 19 -> 17; matrix products, arithmetic and copies ran while one was open for 2% -> 2% of each run, Pallas kernels for 26% -> 29%
where the time goes in v2:
time: 179 us; the launch traced here: 176 us
  Pallas kernels  83.4 us (47%)
  starting transfers between devices  47.9 us (27%)
  waiting for transfers between devices  38.3 us (21%)
  local copies, waits for them, and re-layouts  2.39 us (1%)
  other arithmetic  2.03 us (1%)
    pallas_call x14, Pallas kernels, call(): pl.pallas_call(kernel, out_shape=out_shape, in_specs=specs or [SMEM] * sm...  83.4 us
    ppermute x37, starting transfers between devices, peer(): return lax.ppermute(x, axis, [(i, i ^ k) for i in range(size)])  37.3 us
    ppermute x37, waiting for transfers between devices, peer(): return lax.ppermute(x, axis, [(i, i ^ k) for i in range(size)])  35.4 us
    all_to_all x3, starting transfers between devices, body(): swap_feat = lambda x: lax.all_to_all(x, 'feat', 0, 0, tiled=True)  10.7 us
  transfers between devices with their start and end apart: 40, of which 17 were waited for; matrix products, arithmetic and copies ran while one was open for 2% of the time, Pallas kernels for 29%

profile of v2, /device:TPU:0, one launch (start us, length us, event | category | flops | bytes accessed | tf_op | source)
XLA Modules:
  0.0 175.6 jit_solution(2165888307476136145)
XLA Ops:
  0.7 1.6 pack.1.refs_0_
  2.3 5.1 %collective-permute-start.13 = (bf16[16,4224]{1,0:T(8,128)(2,1)S(1)}, bf16[16,4224]{1,0:T(8,128)(2,1)S(1)}, u32[]{:S(2)}, u32[]{:S(2)}) collective-permute-start(bf16[16,4224]{1,0:T(8,128)(2,1)S(1)} %pack.1.refs_0_), channel_id=1, source_target_pairs={{0,6},{1,7},{2,4},{3,5},{4,2},{5,3},{6,0},{7,1},{8,14},{9,15},{10,... | collective-permute-start | bytes 405512 | tf_op jit(solution)/shard_map/ppermute | solution.py:576
  7.5 0.6 collective-permute-start.11
  8.8 2.7 %collective-permute-start.3 = (bf16[2,25,1024]{2,1,0:T(8,128)(2,1)S(1)}, bf16[2,25,1024]{2,1,0:T(8,128)(2,1)S(1)}, u32[]{:S(2)}, u32[]{:S(2)}) collective-permute-start(bf16[2,25,1024]{2,1,0:T(8,128)(2,1)S(1)} %get-tuple-element.150), channel_id=1, source_target_pairs={{0,24},{8,16},{16,8},{24,0},{1,25},{9,17},{17,9},{25,1},{2,26},{10... | collective-permute-start | bytes 307208 | tf_op jit(solution)/shard_map/ppermute | solution.py:576
  12.0 1.7 collective-permute-start.1
  13.7 5.2 %collective-permute-done.12.refs_2_ = bf16[16,4224]{1,0:T(8,128)(2,1)S(1)} collective-permute-done((bf16[16,4224]{1,0:T(8,128)(2,1)S(1)}, bf16[16,4224]{1,0:T(8,128)(2,1)S(1)}, u32[]{:S(2)}, u32[]{:S(2)}) %collective-permute-start.12) | collective-permute-done | bytes 135200 | tf_op jit(solution)/shard_map/ppermute | solution.py:576
  18.9 1.5 join.1
  20.4 3.7 %all-to-all-start = ((bf16[4,4,16,1664]{3,2,1,0:T(8,128)(2,1)}), bf16[4,4,16,1664]{3,2,1,0:T(8,128)(2,1)S(1)}, u32[]{:S(2)}, u32[]{:S(2)}) async-start(bf16[4,4,16,1664]{3,2,1,0:T(8,128)(2,1)} %get-tuple-element.85), calls=%async_computation | async-start | bytes 1703936 | tf_op jit(solution)/shard_map/all_to_all | solution.py:602
  25.3 1.0 collective-permute-done.theirs_ref
  26.3 2.7 %sort.1 = (bf16[2,2,104,128]{3,2,1,0:T(8,128)(2,1)S(1)}, bf16[2,2,104,128]{3,2,1,0:T(8,128)(2,1)S(1)}, bf16[2,2,104,128]{3,2,1,0:T(8,128)(2,1)S(1)}, bf16[2,2,104,128]{3,2,1,0:T(8,128)(2,1)S(1)}) custom-call(s32[3]{0:T(128)S(1)} %pad_add_fusion.idx_ref, s32[2,1,512]{2,1,0:T(1,128)S(1)} %bitcast.38, s32[2,1,512]{2,1,0:T(1,128)S(1)} %collective-permute-done.theirs_ref, ...), custom_call_target="tpu_custom_call" | custom-call | flops 3000000000 | bytes 1000000 | tf_op jit(solution)/shard_map/sort/pallas_call | solution.py:56
  29.2 2.9 %collective-permute-start.9 = (bf16[2,2,104,128]{3,2,1,0:T(8,128)(2,1)S(1)}, bf16[2,2,104,128]{3,2,1,0:T(8,128)(2,1)S(1)}, u32[]{:S(2)}, u32[]{:S(2)}) collective-permute-start(bf16[2,2,104,128]{3,2,1,0:T(8,128)(2,1)S(1)} %get-tuple-element.83), channel_id=1, source_target_pairs={{0,4},{1,5},{2,6},{3,7},{4,0},{5,1},{6,2},{7,3},{8,12},{9,13},{10,... | collective-permute-start | bytes 319496 | tf_op jit(solution)/shard_map/ppermute | solution.py:576
  32.1 1.3 collective-permute-start.10
  33.4 2.5 %collective-permute-done.8.refs_1_ = bf16[2,2,104,128]{3,2,1,0:T(8,128)(2,1)S(1)} collective-permute-done((bf16[2,2,104,128]{3,2,1,0:T(8,128)(2,1)S(1)}, bf16[2,2,104,128]{3,2,1,0:T(8,128)(2,1)S(1)}, u32[]{:S(2)}, u32[]{:S(2)}) %collective-permute-start.8) | collective-permute-done | bytes 106528 | tf_op jit(solution)/shard_map/ppermute | solution.py:576
  35.9 4.6 %collective-permute-done.9.refs_2_ = bf16[2,2,104,128]{3,2,1,0:T(8,128)(2,1)S(1)} collective-permute-done((bf16[2,2,104,128]{3,2,1,0:T(8,128)(2,1)S(1)}, bf16[2,2,104,128]{3,2,1,0:T(8,128)(2,1)S(1)}, u32[]{:S(2)}, u32[]{:S(2)}) %collective-permute-start.9) | collective-permute-done | bytes 106528 | tf_op jit(solution)/shard_map/ppermute | solution.py:576
  41.0 2.8 %collective-permute-start.17 = (bf16[4,16,2560]{2,1,0:T(8,128)(2,1)S(1)}, bf16[4,16,2560]{2,1,0:T(8,128)(2,1)S(1)}, u32[]{:S(2)}, u32[]{:S(2)}) collective-permute-start(bf16[4,16,2560]{2,1,0:T(8,128)(2,1)S(1)} %get-tuple-element.91.refs_0_), channel_id=1, source_target_pairs={{0,24},{8,16},{16,8},{24,0},{1,25},{9,17},{17,9},{25,1},{2,26},{10... | collective-permute-start | bytes 983048 | tf_op jit(solution)/shard_map/ppermute | solution.py:576
  44.5 14.9 %attend.1 = (f32[8,512]{1,0:T(8,128)}, bf16[2,1024,512]{2,1,0:T(8,128)(2,1)}, bf16[2,1024,512]{2,1,0:T(8,128)(2,1)}, bf16[2,1024,1536]{2,1,0:T(8,128)(2,1)}, bf1...) custom-call(s32[3]{0:T(128)S(1)} %pad_add_fusion.idx_ref, ...), custom_call_target="tpu_custom_call" | custom-call | flops 16000000000 | bytes 1000000 | tf_op jit(solution)/shard_map/attend/pallas_call | solution.py:56
  60.2 1.0 collective-permute-done.19.refs_5_
  62.9 27.9 %feed.1 = (bf16[8,16,2560]{2,1,0:T(8,128)(2,1)}, bf16[8,16,2560]{2,1,0:T(8,128)(2,1)}, bf16[8,16,2560]{2,1,0:T(8,128)(2,1)}, bf16[8,16,2560]{2,1,0:T(8,128)(2,1)...) custom-call(s32[3]{0:T(128)} %copy-done, ...), custom_call_target="tpu_custom_call" | custom-call | flops 28999999488 | bytes 1000000 | tf_op jit(solution)/shard_map/feed/pallas_call | solution.py:56
  90.8 1.9 %collective-permute-start.22 = (bf16[8,16,2560]{2,1,0:T(8,128)(2,1)}, bf16[8,16,2560]{2,1,0:T(8,128)(2,1)S(1)}, u32[]{:S(2)}, u32[]{:S(2)}) collective-permute-start(bf16[8,16,2560]{2,1,0:T(8,128)(2,1)} %get-tuple-element.108), channel_id=1, source_target_pairs={{0,8},{8,0},{16,24},{24,16},{1,9},{9,1},{17,25},{25,17},{2,10},{10... | collective-permute-start | bytes 1966088 | tf_op jit(solution)/shard_map/ppermute | solution.py:576
  92.7 1.5 collective-permute-start.23
  94.3 26.3 %back.1 = (bf16[2,2,104,128]{3,2,1,0:T(8,128)(2,1)S(1)}, bf16[2,2,104,128]{3,2,1,0:T(8,128)(2,1)S(1)}, bf16[2,2,104,128]{3,2,1,0:T(8,128)(2,1)S(1)}, bf16[2,2,10...) custom-call(s32[3]{0:T(128)S(1)} %copy-done.1, ...), custom_call_target="tpu_custom_call" | custom-call | flops 28999999488 | bytes 1000000 | tf_op jit(solution)/shard_map/back/pallas_call | solution.py:56
  120.7 2.7 %collective-permute-done.23.refs_2_ = bf16[8,16,2560]{2,1,0:T(8,128)(2,1)S(1)} collective-permute-done((bf16[8,16,2560]{2,1,0:T(8,128)(2,1)}, bf16[8,16,2560]{2,1,0:T(8,128)(2,1)S(1)}, u32[]{:S(2)}, u32[]{:S(2)}) %collective-permute-start.23) | collective-permute-done | bytes 655392 | tf_op jit(solution)/shard_map/ppermute | solution.py:576
  123.5 0.9 feat_sum_b.1
  124.4 1.2 core_sum.1
  125.6 2.3 %collective-permute-start.27 = (bf16[2,2,104,128]{3,2,1,0:T(8,128)(2,1)S(1)}, bf16[2,2,104,128]{3,2,1,0:T(8,128)(2,1)S(1)}, u32[]{:S(2)}, u32[]{:S(2)}) collective-permute-start(bf16[2,2,104,128]{3,2,1,0:T(8,128)(2,1)S(1)} %get-tuple-element.122), channel_id=1, source_target_pairs={{0,2},{1,3},{2,0},{3,1},{4,6},{5,7},{6,4},{7,5},{8,10},{9,11},{10,... | collective-permute-start | bytes 319496 | tf_op jit(solution)/shard_map/ppermute | solution.py:576
  127.8 1.0 collective-permute-start.28
  128.8 1.5 collective-permute-start.29
  130.3 3.5 %all-to-all-start.2 = ((bf16[4,4,16,1664]{3,2,1,0:T(8,128)(2,1)}), bf16[4,4,16,1664]{3,2,1,0:T(8,128)(2,1)S(1)}, u32[]{:S(2)}, u32[]{:S(2)}) async-start(bf16[4,4,16,1664]{3,2,1,0:T(8,128)(2,1)} %core_sum.1), calls=%async_computation.2 | async-start | bytes 1703936 | tf_op jit(solution)/shard_map/all_to_all | solution.py:602
  133.8 0.6 core_sum_b.1
  134.4 4.7 %collective-permute-done.28.refs_2_ = bf16[2,2,104,128]{3,2,1,0:T(8,128)(2,1)S(1)} collective-permute-done((bf16[2,2,104,128]{3,2,1,0:T(8,128)(2,1)S(1)}, bf16[2,2,104,128]{3,2,1,0:T(8,128)(2,1)S(1)}, u32[]{:S(2)}, u32[]{:S(2)}) %collective-permute-start.28) | collective-permute-done | bytes 106528 | tf_op jit(solution)/shard_map/ppermute | solution.py:576
  139.1 0.6 pick.1
  139.8 1.5 collective-permute-done.30.got_ref
  141.2 1.5 unsort.1
  142.7 1.2 copy.63
  143.9 1.7 all-to-all-done.2.a_ref
  145.7 3.5 %all-to-all-start.1 = ((bf16[4,2,25,1024]{3,1,2,0:T(2,128)(2,1)}), bf16[4,2,25,1024]{3,1,2,0:T(2,128)(2,1)S(1)}, u32[]{:S(2)}, u32[]{:S(2)}) async-start(bf16[4,2,25,1024]{3,1,2,0:T(2,128)(2,1)} %copy.63), calls=%async_computation.1 | async-start | bytes 819200 | tf_op jit(solution)/shard_map/all_to_all | solution.py:602
  149.1 0.7 feat_sum.1
  149.8 0.8 collective-permute-start.31
  150.6 2.2 %collective-permute-start.32 = (bf16[16,4224]{1,0:T(8,128)(2,1)S(1)}, bf16[16,4224]{1,0:T(8,128)(2,1)S(1)}, u32[]{:S(2)}, u32[]{:S(2)}) collective-permute-start(bf16[16,4224]{1,0:T(8,128)(2,1)S(1)} %get-tuple-element.132), channel_id=1, source_target_pairs={{0,4},{1,5},{2,6},{3,7},{4,0},{5,1},{6,2},{7,3},{8,12},{9,13},{10,... | collective-permute-start | bytes 405512 | tf_op jit(solution)/shard_map/ppermute | solution.py:576
  152.8 1.5 collective-permute-start.33
  154.3 1.1 all-to-all-done.1
  155.8 0.9 collective-permute-done.31.refs_1_
  156.7 7.1 %collective-permute-done.32.refs_2_ = bf16[16,4224]{1,0:T(8,128)(2,1)S(1)} collective-permute-done((bf16[16,4224]{1,0:T(8,128)(2,1)S(1)}, bf16[16,4224]{1,0:T(8,128)(2,1)S(1)}, u32[]{:S(2)}, u32[]{:S(2)}) %collective-permute-start.32) | collective-permute-done | bytes 135200 | tf_op jit(solution)/shard_map/ppermute | solution.py:576
  163.9 2.6 %collective-permute-start.36 = (bf16[16,4224]{1,0:T(8,128)(2,1)S(1)}, bf16[16,4224]{1,0:T(8,128)(2,1)S(1)}, u32[]{:S(2)}, u32[]{:S(2)}) collective-permute-start(bf16[16,4224]{1,0:T(8,128)(2,1)S(1)} %rows_sum.1.refs_0_), channel_id=1, source_target_pairs={{0,24},{8,16},{16,8},{24,0},{1,25},{9,17},{17,9},{25,1},{2,26},{10... | collective-permute-start | bytes 405512 | tf_op jit(solution)/shard_map/ppermute | solution.py:576
  167.5 1.4 fusion
  168.8 1.1 collective-permute-done.36.refs_3_
  169.9 1.7 collective-permute-done.35.refs_2_
  172.2 3.0 %adamw.1 = (f32[64,100]{1,0:T(8,128)}, f32[64,100]{1,0:T(8,128)}, f32[64,100]{1,0:T(8,128)}, f32[64,2048]{1,0:T(8,128)}, f32[64,2048]{1,0:T(8,128)}, /*index=5*/...) custom-call(s32[3]{0:T(128)S(1)} %copy-done.1, ...), custom_call_target="tpu_custom_call" | custom-call | flops 4000000000 | bytes 1000000 | tf_op jit(solution)/shard_map/adamw/pallas_call | solution.py:56
  (100 shorter events, 8.5 us)
Async XLA Ops:
  0.7 43.8 %copy-start = (s32[3]{0:T(128)}, s32[3]{0:T(128)S(1)}, u32[]{:S(2)}) copy-start(s32[3]{0:T(128)S(1)} %pad_add_fusion.idx_ref) | copy-start | bytes 40
  2.3 9.6 %collective-permute-start.13 = (bf16[16,4224]{1,0:T(8,128)(2,1)S(1)}, bf16[16,4224]{1,0:T(8,128)(2,1)S(1)}, u32[]{:S(2)}, u32[]{:S(2)}) collective-permute-start(bf16[16,4224]{1,0:T(8,128)(2,1)S(1)} %pack.1.refs_0_), channel_id=1, source_target_pairs={{0,6},{1,7},{2,4},{3,5},{4,2},{5,3},{6,0},{7,1},{8,14},{9,15},{10,... | collective-permute-start | bytes 405512 | tf_op jit(solution)/shard_map/ppermute | solution.py:576
  7.5 11.4 %collective-permute-start.12 = (bf16[16,4224]{1,0:T(8,128)(2,1)S(1)}, bf16[16,4224]{1,0:T(8,128)(2,1)S(1)}, u32[]{:S(2)}, u32[]{:S(2)}) collective-permute-start(bf16[16,4224]{1,0:T(8,128)(2,1)S(1)} %pack.1.refs_0_), channel_id=1, source_target_pairs={{0,4},{1,5},{2,6},{3,7},{4,0},{5,1},{6,2},{7,3},{8,12},{9,13},{10,... | collective-permute-start | bytes 405512 | tf_op jit(solution)/shard_map/ppermute | solution.py:576
  7.5 11.4 %collective-permute-start.11 = (bf16[16,4224]{1,0:T(8,128)(2,1)S(1)}, bf16[16,4224]{1,0:T(8,128)(2,1)S(1)}, u32[]{:S(2)}, u32[]{:S(2)}) collective-permute-start(bf16[16,4224]{1,0:T(8,128)(2,1)S(1)} %pack.1.refs_0_), channel_id=1, source_target_pairs={{0,2},{1,3},{2,0},{3,1},{4,6},{5,7},{6,4},{7,5},{8,10},{9,11},{10,... | collective-permute-start | bytes 405512 | tf_op jit(solution)/shard_map/ppermute | solution.py:576
  8.8 15.4 %collective-permute-start.3 = (bf16[2,25,1024]{2,1,0:T(8,128)(2,1)S(1)}, bf16[2,25,1024]{2,1,0:T(8,128)(2,1)S(1)}, u32[]{:S(2)}, u32[]{:S(2)}) collective-permute-start(bf16[2,25,1024]{2,1,0:T(8,128)(2,1)S(1)} %get-tuple-element.150), channel_id=1, source_target_pairs={{0,24},{8,16},{16,8},{24,0},{1,25},{9,17},{17,9},{25,1},{2,26},{10... | collective-permute-start | bytes 307208 | tf_op jit(solution)/shard_map/ppermute | solution.py:576
  11.4 13.1 %collective-permute-start.2 = (bf16[2,25,1024]{2,1,0:T(8,128)(2,1)S(1)}, bf16[2,25,1024]{2,1,0:T(8,128)(2,1)S(1)}, u32[]{:S(2)}, u32[]{:S(2)}) collective-permute-start(bf16[2,25,1024]{2,1,0:T(8,128)(2,1)S(1)} %get-tuple-element.151), channel_id=1, source_target_pairs={{0,16},{8,24},{16,0},{24,8},{1,17},{9,25},{17,1},{25,9},{2,18},{10... | collective-permute-start | bytes 307208 | tf_op jit(solution)/shard_map/ppermute | solution.py:576
  12.0 12.8 %collective-permute-start.1 = (bf16[2,25,1024]{2,1,0:T(8,128)(2,1)S(1)}, bf16[2,25,1024]{2,1,0:T(8,128)(2,1)S(1)}, u32[]{:S(2)}, u32[]{:S(2)}) collective-permute-start(bf16[2,25,1024]{2,1,0:T(8,128)(2,1)S(1)} %get-tuple-element.152), channel_id=1, source_target_pairs={{0,8},{8,0},{16,24},{24,16},{1,9},{9,1},{17,25},{25,17},{2,10},{10... | collective-permute-start | bytes 307208 | tf_op jit(solution)/shard_map/ppermute | solution.py:576
  18.9 7.3 %collective-permute-start.4 = (bf16[2,25,1024]{2,1,0:T(8,128)(2,1)S(1)}, bf16[2,25,1024]{2,1,0:T(8,128)(2,1)S(1)}, u32[]{:S(2)}, u32[]{:S(2)}) collective-permute-start(bf16[2,25,1024]{2,1,0:T(8,128)(2,1)S(1)} %get-tuple-element.153.refs_0_), channel_id=1, source_target_pairs={{0,1},{1,0},{2,3},{3,2},{4,5},{5,4},{6,7},{7,6},{8,9},{9,8},{10,11... | collective-permute-start | bytes 307208 | tf_op jit(solution)/shard_map/ppermute | solution.py:576
  20.4 23.9 %copy-start.8 = (bf16[4,16,2560]{2,1,0:T(8,128)(2,1)}, bf16[4,16,2560]{2,1,0:T(8,128)(2,1)S(1)}, u32[]{:S(2)}) copy-start(bf16[4,16,2560]{2,1,0:T(8,128)(2,1)S(1)} %get-tuple-element.91.refs_0_) | copy-start | bytes 983044
  20.4 20.1 %all-to-all-start = ((bf16[4,4,16,1664]{3,2,1,0:T(8,128)(2,1)}), bf16[4,4,16,1664]{3,2,1,0:T(8,128)(2,1)S(1)}, u32[]{:S(2)}, u32[]{:S(2)}) async-start(bf16[4,4,16,1664]{3,2,1,0:T(8,128)(2,1)} %get-tuple-element.85), calls=%async_computation | async-start | bytes 1703936 | tf_op jit(solution)/shard_map/all_to_all | solution.py:602
  24.2 2.1 %collective-permute-start.7 = (bf16[2,25,1024]{2,1,0:T(8,128)(2,1)S(1)}, bf16[2,25,1024]{2,1,0:T(8,128)(2,1)S(1)}, u32[]{:S(2)}, u32[]{:S(2)}) collective-permute-start(bf16[2,25,1024]{2,1,0:T(8,128)(2,1)S(1)} %collective-permute-done.3.refs_3_), channel_id=1, source_target_pairs={{0,1},{1,0},{2,3},{3,2},{4,5},{5,4},{6,7},{7,6},{8,9},{9,8},{10,11... | collective-permute-start | bytes 307208 | tf_op jit(solution)/shard_map/ppermute | solution.py:576
  24.5 1.7 collective-permute-start.6
  24.8 1.5 collective-permute-start.5
  25.1 1.2 collective-permute-start
  26.3 18.3 %copy-start.9 = (s32[2,1,1,1024]{3,2,1,0:T(1,128)S(1)}, s32[2,1,1,1024]{3,2,1,0:T(1,128)}, u32[]{:S(2)}) copy-start(s32[2,1,1,1024]{3,2,1,0:T(1,128)} %seg_ref.3) | copy-start | bytes 24580
  26.3 18.3 %copy-start.10 = (s32[2,1,1,1024]{3,2,1,0:T(1,128)S(1)}, s32[2,1,1,1024]{3,2,1,0:T(1,128)}, u32[]{:S(2)}) copy-start(s32[2,1,1,1024]{3,2,1,0:T(1,128)} %ctx_ref.3) | copy-start | bytes 24580
  29.0 6.9 %collective-permute-start.8 = (bf16[2,2,104,128]{3,2,1,0:T(8,128)(2,1)S(1)}, bf16[2,2,104,128]{3,2,1,0:T(8,128)(2,1)S(1)}, u32[]{:S(2)}, u32[]{:S(2)}) collective-permute-start(bf16[2,2,104,128]{3,2,1,0:T(8,128)(2,1)S(1)} %get-tuple-element.82), channel_id=1, source_target_pairs={{0,2},{1,3},{2,0},{3,1},{4,6},{5,7},{6,4},{7,5},{8,10},{9,11},{10,... | collective-permute-start | bytes 319496 | tf_op jit(solution)/shard_map/ppermute | solution.py:576
  29.2 11.3 %collective-permute-start.9 = (bf16[2,2,104,128]{3,2,1,0:T(8,128)(2,1)S(1)}, bf16[2,2,104,128]{3,2,1,0:T(8,128)(2,1)S(1)}, u32[]{:S(2)}, u32[]{:S(2)}) collective-permute-start(bf16[2,2,104,128]{3,2,1,0:T(8,128)(2,1)S(1)} %get-tuple-element.83), channel_id=1, source_target_pairs={{0,4},{1,5},{2,6},{3,7},{4,0},{5,1},{6,2},{7,3},{8,12},{9,13},{10,... | collective-permute-start | bytes 319496 | tf_op jit(solution)/shard_map/ppermute | solution.py:576
  32.1 8.4 %collective-permute-start.10 = (bf16[2,2,104,128]{3,2,1,0:T(8,128)(2,1)S(1)}, bf16[2,2,104,128]{3,2,1,0:T(8,128)(2,1)S(1)}, u32[]{:S(2)}, u32[]{:S(2)}) collective-permute-start(bf16[2,2,104,128]{3,2,1,0:T(8,128)(2,1)S(1)} %get-tuple-element.84), channel_id=1, source_target_pairs={{0,6},{1,7},{2,4},{3,5},{4,2},{5,3},{6,0},{7,1},{8,14},{9,15},{10,... | collective-permute-start | bytes 319496 | tf_op jit(solution)/shard_map/ppermute | solution.py:576
  40.5 4.0 %collective-permute-start.14 = (bf16[4,4,16,1664]{3,2,1,0:T(8,128)(2,1)S(1)}, bf16[4,4,16,1664]{3,2,1,0:T(8,128)(2,1)S(1)}, u32[]{:S(2)}, u32[]{:S(2)}) collective-permute-start(bf16[4,4,16,1664]{3,2,1,0:T(8,128)(2,1)S(1)} %all-to-all-done.refs_4_), channel_id=1, source_target_pairs={{0,1},{1,0},{2,3},{3,2},{4,5},{5,4},{6,7},{7,6},{8,9},{9,8},{10,11... | collective-permute-start | bytes 2555912 | tf_op jit(solution)/shard_map/ppermute | solution.py:576
  40.5 19.7 %collective-permute-start.18 = (bf16[4,16,2560]{2,1,0:T(8,128)(2,1)S(1)}, bf16[4,16,2560]{2,1,0:T(8,128)(2,1)S(1)}, u32[]{:S(2)}, u32[]{:S(2)}) collective-permute-start(bf16[4,16,2560]{2,1,0:T(8,128)(2,1)S(1)} %get-tuple-element.91.refs_0_), channel_id=1, source_target_pairs={{0,1},{1,0},{2,3},{3,2},{4,5},{5,4},{6,7},{7,6},{8,9},{9,8},{10,11... | collective-permute-start | bytes 983048 | tf_op jit(solution)/shard_map/ppermute | solution.py:576
  41.0 18.5 %collective-permute-start.17 = (bf16[4,16,2560]{2,1,0:T(8,128)(2,1)S(1)}, bf16[4,16,2560]{2,1,0:T(8,128)(2,1)S(1)}, u32[]{:S(2)}, u32[]{:S(2)}) collective-permute-start(bf16[4,16,2560]{2,1,0:T(8,128)(2,1)S(1)} %get-tuple-element.91.refs_0_), channel_id=1, source_target_pairs={{0,24},{8,16},{16,8},{24,0},{1,25},{9,17},{17,9},{25,1},{2,26},{10... | collective-permute-start | bytes 983048 | tf_op jit(solution)/shard_map/ppermute | solution.py:576
  43.8 15.7 %collective-permute-start.16 = (bf16[4,16,2560]{2,1,0:T(8,128)(2,1)S(1)}, bf16[4,16,2560]{2,1,0:T(8,128)(2,1)S(1)}, u32[]{:S(2)}, u32[]{:S(2)}) collective-permute-start(bf16[4,16,2560]{2,1,0:T(8,128)(2,1)S(1)} %get-tuple-element.91.refs_0_), channel_id=1, source_target_pairs={{0,16},{8,24},{16,0},{24,8},{1,17},{9,25},{17,1},{25,9},{2,18},{10... | collective-permute-start | bytes 983048 | tf_op jit(solution)/shard_map/ppermute | solution.py:576
  44.3 15.2 %collective-permute-start.15 = (bf16[4,16,2560]{2,1,0:T(8,128)(2,1)S(1)}, bf16[4,16,2560]{2,1,0:T(8,128)(2,1)S(1)}, u32[]{:S(2)}, u32[]{:S(2)}) collective-permute-start(bf16[4,16,2560]{2,1,0:T(8,128)(2,1)S(1)} %get-tuple-element.91.refs_0_), channel_id=1, source_target_pairs={{0,8},{8,0},{16,24},{24,16},{1,9},{9,1},{17,25},{25,17},{2,10},{10... | collective-permute-start | bytes 983048 | tf_op jit(solution)/shard_map/ppermute | solution.py:576
  59.6 1.7 collective-permute-start.19
  59.6 2.1 %collective-permute-start.20 = (bf16[4,16,2560]{2,1,0:T(8,128)(2,1)S(1)}, bf16[4,16,2560]{2,1,0:T(8,128)(2,1)S(1)}, u32[]{:S(2)}, u32[]{:S(2)}) collective-permute-start(bf16[4,16,2560]{2,1,0:T(8,128)(2,1)S(1)} %collective-permute-done.16.refs_2_), channel_id=1, source_target_pairs={{0,1},{1,0},{2,3},{3,2},{4,5},{5,4},{6,7},{7,6},{8,9},{9,8},{10,11... | collective-permute-start | bytes 983048 | tf_op jit(solution)/shard_map/ppermute | solution.py:576
  60.1 2.1 %collective-permute-start.21 = (bf16[4,16,2560]{2,1,0:T(8,128)(2,1)S(1)}, bf16[4,16,2560]{2,1,0:T(8,128)(2,1)S(1)}, u32[]{:S(2)}, u32[]{:S(2)}) collective-permute-start(bf16[4,16,2560]{2,1,0:T(8,128)(2,1)S(1)} %collective-permute-done.17.refs_3_), channel_id=1, source_target_pairs={{0,1},{1,0},{2,3},{3,2},{4,5},{5,4},{6,7},{7,6},{8,9},{9,8},{10,11... | collective-permute-start | bytes 983048 | tf_op jit(solution)/shard_map/ppermute | solution.py:576
  62.9 31.4 %copy-start.1 = (s32[3]{0:T(128)S(1)}, s32[3]{0:T(128)}, u32[]{:S(2)}) copy-start(s32[3]{0:T(128)} %copy-done) | copy-start | bytes 40
  90.8 29.9 %collective-permute-start.22 = (bf16[8,16,2560]{2,1,0:T(8,128)(2,1)}, bf16[8,16,2560]{2,1,0:T(8,128)(2,1)S(1)}, u32[]{:S(2)}, u32[]{:S(2)}) collective-permute-start(bf16[8,16,2560]{2,1,0:T(8,128)(2,1)} %get-tuple-element.108), channel_id=1, source_target_pairs={{0,8},{8,0},{16,24},{24,16},{1,9},{9,1},{17,25},{25,17},{2,10},{10... | collective-permute-start | bytes 1966088 | tf_op jit(solution)/shard_map/ppermute | solution.py:576
  92.7 30.8 %collective-permute-start.23 = (bf16[8,16,2560]{2,1,0:T(8,128)(2,1)}, bf16[8,16,2560]{2,1,0:T(8,128)(2,1)S(1)}, u32[]{:S(2)}, u32[]{:S(2)}) collective-permute-start(bf16[8,16,2560]{2,1,0:T(8,128)(2,1)} %get-tuple-element.109), channel_id=1, source_target_pairs={{0,16},{8,24},{16,0},{24,8},{1,17},{9,25},{17,1},{25,9},{2,18},{10... | collective-permute-start | bytes 1966088 | tf_op jit(solution)/shard_map/ppermute | solution.py:576
  94.2 29.3 %collective-permute-start.24 = (bf16[8,16,2560]{2,1,0:T(8,128)(2,1)}, bf16[8,16,2560]{2,1,0:T(8,128)(2,1)S(1)}, u32[]{:S(2)}, u32[]{:S(2)}) collective-permute-start(bf16[8,16,2560]{2,1,0:T(8,128)(2,1)} %get-tuple-element.110), channel_id=1, source_target_pairs={{0,24},{8,16},{16,8},{24,0},{1,25},{9,17},{17,9},{25,1},{2,26},{10... | collective-permute-start | bytes 1966088 | tf_op jit(solution)/shard_map/ppermute | solution.py:576
  94.3 29.1 %copy-start.11 = (bf16[8,16,2560]{2,1,0:T(8,128)(2,1)S(1)}, bf16[8,16,2560]{2,1,0:T(8,128)(2,1)}, u32[]{:S(2)}) copy-start(bf16[8,16,2560]{2,1,0:T(8,128)(2,1)} %get-tuple-element.107.refs_0_) | copy-start | bytes 1966084
  120.6 3.8 %collective-permute-start.25 = (bf16[4,64,1664]{2,1,0:T(8,128)(2,1)S(1)}, bf16[4,64,1664]{2,1,0:T(8,128)(2,1)S(1)}, u32[]{:S(2)}, u32[]{:S(2)}) collective-permute-start(bf16[4,64,1664]{2,1,0:T(8,128)(2,1)S(1)} %get-tuple-element.113), channel_id=1, source_target_pairs={{0,1},{1,0},{2,3},{3,2},{4,5},{5,4},{6,7},{7,6},{8,9},{9,8},{10,11... | collective-permute-start | bytes 2555912 | tf_op jit(solution)/shard_map/ppermute | solution.py:576
  124.3 9.5 %collective-permute-start.26 = (bf16[4,16,2560]{2,1,0:T(8,128)(2,1)S(1)}, bf16[4,16,2560]{2,1,0:T(8,128)(2,1)S(1)}, u32[]{:S(2)}, u32[]{:S(2)}) collective-permute-start(bf16[4,16,2560]{2,1,0:T(8,128)(2,1)S(1)} %get-tuple-element.115), channel_id=1, source_target_pairs={{0,1},{1,0},{2,3},{3,2},{4,5},{5,4},{6,7},{7,6},{8,9},{9,8},{10,11... | collective-permute-start | bytes 983048 | tf_op jit(solution)/shard_map/ppermute | solution.py:576
  125.6 8.9 %collective-permute-start.27 = (bf16[2,2,104,128]{3,2,1,0:T(8,128)(2,1)S(1)}, bf16[2,2,104,128]{3,2,1,0:T(8,128)(2,1)S(1)}, u32[]{:S(2)}, u32[]{:S(2)}) collective-permute-start(bf16[2,2,104,128]{3,2,1,0:T(8,128)(2,1)S(1)} %get-tuple-element.122), channel_id=1, source_target_pairs={{0,2},{1,3},{2,0},{3,1},{4,6},{5,7},{6,4},{7,5},{8,10},{9,11},{10,... | collective-permute-start | bytes 319496 | tf_op jit(solution)/shard_map/ppermute | solution.py:576
  127.8 11.3 %collective-permute-start.28 = (bf16[2,2,104,128]{3,2,1,0:T(8,128)(2,1)S(1)}, bf16[2,2,104,128]{3,2,1,0:T(8,128)(2,1)S(1)}, u32[]{:S(2)}, u32[]{:S(2)}) collective-permute-start(bf16[2,2,104,128]{3,2,1,0:T(8,128)(2,1)S(1)} %get-tuple-element.124), channel_id=1, source_target_pairs={{0,4},{1,5},{2,6},{3,7},{4,0},{5,1},{6,2},{7,3},{8,12},{9,13},{10,... | collective-permute-start | bytes 319496 | tf_op jit(solution)/shard_map/ppermute | solution.py:576
  128.8 10.3 %collective-permute-start.29 = (bf16[2,2,104,128]{3,2,1,0:T(8,128)(2,1)S(1)}, bf16[2,2,104,128]{3,2,1,0:T(8,128)(2,1)S(1)}, u32[]{:S(2)}, u32[]{:S(2)}) collective-permute-start(bf16[2,2,104,128]{3,2,1,0:T(8,128)(2,1)S(1)} %get-tuple-element.126), channel_id=1, source_target_pairs={{0,6},{1,7},{2,4},{3,5},{4,2},{5,3},{6,0},{7,1},{8,14},{9,15},{10,... | collective-permute-start | bytes 319496 | tf_op jit(solution)/shard_map/ppermute | solution.py:576
  130.3 15.4 %all-to-all-start.2 = ((bf16[4,4,16,1664]{3,2,1,0:T(8,128)(2,1)}), bf16[4,4,16,1664]{3,2,1,0:T(8,128)(2,1)S(1)}, u32[]{:S(2)}, u32[]{:S(2)}) async-start(bf16[4,4,16,1664]{3,2,1,0:T(8,128)(2,1)} %core_sum.1), calls=%async_computation.2 | async-start | bytes 1703936 | tf_op jit(solution)/shard_map/all_to_all | solution.py:602
  139.7 1.5 collective-permute-start.30
  145.7 9.7 %all-to-all-start.1 = ((bf16[4,2,25,1024]{3,1,2,0:T(2,128)(2,1)}), bf16[4,2,25,1024]{3,1,2,0:T(2,128)(2,1)S(1)}, u32[]{:S(2)}, u32[]{:S(2)}) async-start(bf16[4,2,25,1024]{3,1,2,0:T(2,128)(2,1)} %copy.63), calls=%async_computation.1 | async-start | bytes 819200 | tf_op jit(solution)/shard_map/all_to_all | solution.py:602
  149.8 6.9 %collective-permute-start.31 = (bf16[16,4224]{1,0:T(8,128)(2,1)S(1)}, bf16[16,4224]{1,0:T(8,128)(2,1)S(1)}, u32[]{:S(2)}, u32[]{:S(2)}) collective-permute-start(bf16[16,4224]{1,0:T(8,128)(2,1)S(1)} %get-tuple-element.131), channel_id=1, source_target_pairs={{0,2},{1,3},{2,0},{3,1},{4,6},{5,7},{6,4},{7,5},{8,10},{9,11},{10,... | collective-permute-start | bytes 405512 | tf_op jit(solution)/shard_map/ppermute | solution.py:576
  150.6 13.2 %collective-permute-start.32 = (bf16[16,4224]{1,0:T(8,128)(2,1)S(1)}, bf16[16,4224]{1,0:T(8,128)(2,1)S(1)}, u32[]{:S(2)}, u32[]{:S(2)}) collective-permute-start(bf16[16,4224]{1,0:T(8,128)(2,1)S(1)} %get-tuple-element.132), channel_id=1, source_target_pairs={{0,4},{1,5},{2,6},{3,7},{4,0},{5,1},{6,2},{7,3},{8,12},{9,13},{10,... | collective-permute-start | bytes 405512 | tf_op jit(solution)/shard_map/ppermute | solution.py:576
  152.8 11.0 %collective-permute-start.33 = (bf16[16,4224]{1,0:T(8,128)(2,1)S(1)}, bf16[16,4224]{1,0:T(8,128)(2,1)S(1)}, u32[]{:S(2)}, u32[]{:S(2)}) collective-permute-start(bf16[16,4224]{1,0:T(8,128)(2,1)S(1)} %get-tuple-element.133), channel_id=1, source_target_pairs={{0,6},{1,7},{2,4},{3,5},{4,2},{5,3},{6,0},{7,1},{8,14},{9,15},{10,... | collective-permute-start | bytes 405512 | tf_op jit(solution)/shard_map/ppermute | solution.py:576
  163.8 8.3 %copy-start.6 = (f32[64,2048]{1,0:T(8,128)S(1)}, f32[64,2048]{1,0:T(8,128)}, u32[]{:S(2)}) copy-start(f32[64,2048]{1,0:T(8,128)} %refs_11_.1) | copy-start | bytes 1572868
  163.8 8.3 %copy-start.7 = (f32[64,2048]{1,0:T(8,128)S(1)}, f32[64,2048]{1,0:T(8,128)}, u32[]{:S(2)}) copy-start(f32[64,2048]{1,0:T(8,128)} %refs_12_.1) | copy-start | bytes 1572868
  163.9 6.0 %collective-permute-start.36 = (bf16[16,4224]{1,0:T(8,128)(2,1)S(1)}, bf16[16,4224]{1,0:T(8,128)(2,1)S(1)}, u32[]{:S(2)}, u32[]{:S(2)}) collective-permute-start(bf16[16,4224]{1,0:T(8,128)(2,1)S(1)} %rows_sum.1.refs_0_), channel_id=1, source_target_pairs={{0,24},{8,16},{16,8},{24,0},{1,25},{9,17},{17,9},{25,1},{2,26},{10... | collective-permute-start | bytes 405512 | tf_op jit(solution)/shard_map/ppermute | solution.py:576
  166.5 5.0 %collective-permute-start.35 = (bf16[16,4224]{1,0:T(8,128)(2,1)S(1)}, bf16[16,4224]{1,0:T(8,128)(2,1)S(1)}, u32[]{:S(2)}, u32[]{:S(2)}) collective-permute-start(bf16[16,4224]{1,0:T(8,128)(2,1)S(1)} %rows_sum.1.refs_0_), channel_id=1, source_target_pairs={{0,16},{8,24},{16,0},{24,8},{1,17},{9,25},{17,1},{25,9},{2,18},{10... | collective-permute-start | bytes 405512 | tf_op jit(solution)/shard_map/ppermute | solution.py:576
  167.1 5.0 %collective-permute-start.34 = (bf16[16,4224]{1,0:T(8,128)(2,1)S(1)}, bf16[16,4224]{1,0:T(8,128)(2,1)S(1)}, u32[]{:S(2)}, u32[]{:S(2)}) collective-permute-start(bf16[16,4224]{1,0:T(8,128)(2,1)S(1)} %rows_sum.1.refs_0_), channel_id=1, source_target_pairs={{0,8},{8,0},{16,24},{24,16},{1,9},{9,1},{17,25},{25,17},{2,10},{10... | collective-permute-start | bytes 405512 | tf_op jit(solution)/shard_map/ppermute | solution.py:576
  (14 other events, 65.6 us)

commit v3 on v2

--- a/solution.py
+++ b/solution.py
@@ -481,8 +481,15 @@
     core = idx_ref[CORE]
     split_rows(accx_s, core, keep_ref, send_ref, slice(3 * D, 3 * D + 128))
     copies.wait("h")
-    acc_s[...] = tn(h_ref[...].reshape(M * T, D), dqkv_s[...])
-    split_rows(acc_s, core, keep_ref, send_ref, slice(0, 3 * D))
+    g = tn(h_ref[...].reshape(M * T, D), dqkv_s[...])
+    if len(acc_s.shape) == 3:
+        acc_s[...] = g.astype(bf16).reshape(acc_s.shape)
+        for z in range(keep_ref.shape[0]):
+            keep_ref[z, :, 0 : 3 * D] = acc_s[2 * z + core]
+            send_ref[z, :, 0 : 3 * D] = acc_s[2 * z + 1 - core]
+    else:
+        acc_s[...] = g
+        split_rows(acc_s, core, keep_ref, send_ref, slice(0, 3 * D))
 
 
 def core_kernel(keep_ref, got_ref, out_ref):
@@ -673,7 +680,7 @@
         name="back", flops=29 * 10**9, mib=50, specs=[SMEM] * 2 + [VMEM] * 2 + [HBM] * 8,
         scratch=[ram(bf16, M, T, D), ram(bf16, M, T, 128), ram(bf16, M * T, D), ram(bf16, M, T, 3 * D), ram(bf16, M, T, 128), ram(bf16, M, T, D), ram(bf16, D, WA), ram(bf16, nr, M, nf, n), ram(bf16, M * T, 3 * D),
             ram(bf16, HEADS, T, 128), ram(bf16, HEADS, Q, 128), ram(f32, 4, Q, Q), ram(bf16, 2, BIG * Q, BIG * Q), ram(bf16, 2, BIG * Q, BIG * Q),
-            ram(f32, D, 3 * D), ram(f32, D, 128), ram(bf16, M * T, D), dma(4 + 4 * M)],
+            ram(bf16, nr, Dl, 3 * D) if by_quarters else ram(f32, D, 3 * D), ram(f32, D, 128), ram(bf16, M * T, D), dma(4 + 4 * M)],
     )
 
     got_a = over_core(send_a)

time: 179 us -> 179 us (level)
  no operation moved by 1% of the time
where the time goes in v3:
time: 179 us; the launch traced here: 176 us
  Pallas kernels  83.3 us (47%)
  starting transfers between devices  47.9 us (27%)
  waiting for transfers between devices  38.4 us (21%)
  local copies, waits for them, and re-layouts  2.39 us (1%)
  other arithmetic  2.03 us (1%)
    pallas_call x14, Pallas kernels, call(): pl.pallas_call(kernel, out_shape=out_shape, in_specs=specs or [SMEM] * sm...  83.3 us
    ppermute x37, starting transfers between devices, peer(): return lax.ppermute(x, axis, [(i, i ^ k) for i in range(size)])  37.3 us
    ppermute x37, waiting for transfers between devices, peer(): return lax.ppermute(x, axis, [(i, i ^ k) for i in range(size)])  35.5 us
    all_to_all x3, starting transfers between devices, body(): swap_feat = lambda x: lax.all_to_all(x, 'feat', 0, 0, tiled=True)  10.7 us
  transfers between devices with their start and end apart: 40, of which 17 were waited for; matrix products, arithmetic and copies ran while one was open for 2% of the time, Pallas kernels for 29%

profile of v3, /device:TPU:0, one launch (start us, length us, event | category | flops | bytes accessed | tf_op | source)
XLA Modules:
  0.0 175.6 jit_solution(1148687396890538873)
XLA Ops:
  0.7 1.6 pack.1.refs_0_
  2.3 5.1 %collective-permute-start.13 = (bf16[16,4224]{1,0:T(8,128)(2,1)S(1)}, bf16[16,4224]{1,0:T(8,128)(2,1)S(1)}, u32[]{:S(2)}, u32[]{:S(2)}) collective-permute-start(bf16[16,4224]{1,0:T(8,128)(2,1)S(1)} %pack.1.refs_0_), channel_id=1, source_target_pairs={{0,6},{1,7},{2,4},{3,5},{4,2},{5,3},{6,0},{7,1},{8,14},{9,15},{10,... | collective-permute-start | bytes 405512 | tf_op jit(solution)/shard_map/ppermute | solution.py:583
  7.5 0.6 collective-permute-start.11
  8.8 2.7 %collective-permute-start.3 = (bf16[2,25,1024]{2,1,0:T(8,128)(2,1)S(1)}, bf16[2,25,1024]{2,1,0:T(8,128)(2,1)S(1)}, u32[]{:S(2)}, u32[]{:S(2)}) collective-permute-start(bf16[2,25,1024]{2,1,0:T(8,128)(2,1)S(1)} %get-tuple-element.150), channel_id=1, source_target_pairs={{0,24},{8,16},{16,8},{24,0},{1,25},{9,17},{17,9},{25,1},{2,26},{10... | collective-permute-start | bytes 307208 | tf_op jit(solution)/shard_map/ppermute | solution.py:583
  12.0 1.7 collective-permute-start.1
  13.7 5.2 %collective-permute-done.12.refs_2_ = bf16[16,4224]{1,0:T(8,128)(2,1)S(1)} collective-permute-done((bf16[16,4224]{1,0:T(8,128)(2,1)S(1)}, bf16[16,4224]{1,0:T(8,128)(2,1)S(1)}, u32[]{:S(2)}, u32[]{:S(2)}) %collective-permute-start.12) | collective-permute-done | bytes 135200 | tf_op jit(solution)/shard_map/ppermute | solution.py:583
  18.9 1.5 join.1
  20.4 3.7 %all-to-all-start = ((bf16[4,4,16,1664]{3,2,1,0:T(8,128)(2,1)}), bf16[4,4,16,1664]{3,2,1,0:T(8,128)(2,1)S(1)}, u32[]{:S(2)}, u32[]{:S(2)}) async-start(bf16[4,4,16,1664]{3,2,1,0:T(8,128)(2,1)} %get-tuple-element.85), calls=%async_computation | async-start | bytes 1703936 | tf_op jit(solution)/shard_map/all_to_all | solution.py:609
  25.3 1.0 collective-permute-done.theirs_ref
  26.3 2.7 %sort.1 = (bf16[2,2,104,128]{3,2,1,0:T(8,128)(2,1)S(1)}, bf16[2,2,104,128]{3,2,1,0:T(8,128)(2,1)S(1)}, bf16[2,2,104,128]{3,2,1,0:T(8,128)(2,1)S(1)}, bf16[2,2,104,128]{3,2,1,0:T(8,128)(2,1)S(1)}) custom-call(s32[3]{0:T(128)S(1)} %pad_add_fusion.idx_ref, s32[2,1,512]{2,1,0:T(1,128)S(1)} %bitcast.38, s32[2,1,512]{2,1,0:T(1,128)S(1)} %collective-permute-done.theirs_ref, ...), custom_call_target="tpu_custom_call" | custom-call | flops 3000000000 | bytes 1000000 | tf_op jit(solution)/shard_map/sort/pallas_call | solution.py:56
  29.2 2.9 %collective-permute-start.9 = (bf16[2,2,104,128]{3,2,1,0:T(8,128)(2,1)S(1)}, bf16[2,2,104,128]{3,2,1,0:T(8,128)(2,1)S(1)}, u32[]{:S(2)}, u32[]{:S(2)}) collective-permute-start(bf16[2,2,104,128]{3,2,1,0:T(8,128)(2,1)S(1)} %get-tuple-element.83), channel_id=1, source_target_pairs={{0,4},{1,5},{2,6},{3,7},{4,0},{5,1},{6,2},{7,3},{8,12},{9,13},{10,... | collective-permute-start | bytes 319496 | tf_op jit(solution)/shard_map/ppermute | solution.py:583
  32.1 1.3 collective-permute-start.10
  33.4 2.5 %collective-permute-done.8.refs_1_ = bf16[2,2,104,128]{3,2,1,0:T(8,128)(2,1)S(1)} collective-permute-done((bf16[2,2,104,128]{3,2,1,0:T(8,128)(2,1)S(1)}, bf16[2,2,104,128]{3,2,1,0:T(8,128)(2,1)S(1)}, u32[]{:S(2)}, u32[]{:S(2)}) %collective-permute-start.8) | collective-permute-done | bytes 106528 | tf_op jit(solution)/shard_map/ppermute | solution.py:583
  35.9 4.6 %collective-permute-done.9.refs_2_ = bf16[2,2,104,128]{3,2,1,0:T(8,128)(2,1)S(1)} collective-permute-done((bf16[2,2,104,128]{3,2,1,0:T(8,128)(2,1)S(1)}, bf16[2,2,104,128]{3,2,1,0:T(8,128)(2,1)S(1)}, u32[]{:S(2)}, u32[]{:S(2)}) %collective-permute-start.9) | collective-permute-done | bytes 106528 | tf_op jit(solution)/shard_map/ppermute | solution.py:583
  41.0 2.8 %collective-permute-start.17 = (bf16[4,16,2560]{2,1,0:T(8,128)(2,1)S(1)}, bf16[4,16,2560]{2,1,0:T(8,128)(2,1)S(1)}, u32[]{:S(2)}, u32[]{:S(2)}) collective-permute-start(bf16[4,16,2560]{2,1,0:T(8,128)(2,1)S(1)} %get-tuple-element.91.refs_0_), channel_id=1, source_target_pairs={{0,24},{8,16},{16,8},{24,0},{1,25},{9,17},{17,9},{25,1},{2,26},{10... | collective-permute-start | bytes 983048 | tf_op jit(solution)/shard_map/ppermute | solution.py:583
  44.5 14.9 %attend.1 = (f32[8,512]{1,0:T(8,128)}, bf16[2,1024,512]{2,1,0:T(8,128)(2,1)}, bf16[2,1024,512]{2,1,0:T(8,128)(2,1)}, bf16[2,1024,1536]{2,1,0:T(8,128)(2,1)}, bf1...) custom-call(s32[3]{0:T(128)S(1)} %pad_add_fusion.idx_ref, ...), custom_call_target="tpu_custom_call" | custom-call | flops 16000000000 | bytes 1000000 | tf_op jit(solution)/shard_map/attend/pallas_call | solution.py:56
  60.2 1.0 collective-permute-done.19.refs_5_
  62.9 27.9 %feed.1 = (bf16[8,16,2560]{2,1,0:T(8,128)(2,1)}, bf16[8,16,2560]{2,1,0:T(8,128)(2,1)}, bf16[8,16,2560]{2,1,0:T(8,128)(2,1)}, bf16[8,16,2560]{2,1,0:T(8,128)(2,1)...) custom-call(s32[3]{0:T(128)} %copy-done, ...), custom_call_target="tpu_custom_call" | custom-call | flops 28999999488 | bytes 1000000 | tf_op jit(solution)/shard_map/feed/pallas_call | solution.py:56
  90.8 1.9 %collective-permute-start.22 = (bf16[8,16,2560]{2,1,0:T(8,128)(2,1)}, bf16[8,16,2560]{2,1,0:T(8,128)(2,1)S(1)}, u32[]{:S(2)}, u32[]{:S(2)}) collective-permute-start(bf16[8,16,2560]{2,1,0:T(8,128)(2,1)} %get-tuple-element.108), channel_id=1, source_target_pairs={{0,8},{8,0},{16,24},{24,16},{1,9},{9,1},{17,25},{25,17},{2,10},{10... | collective-permute-start | bytes 1966088 | tf_op jit(solution)/shard_map/ppermute | solution.py:583
  92.7 1.5 collective-permute-start.23
  94.3 26.2 %back.1 = (bf16[2,2,104,128]{3,2,1,0:T(8,128)(2,1)S(1)}, bf16[2,2,104,128]{3,2,1,0:T(8,128)(2,1)S(1)}, bf16[2,2,104,128]{3,2,1,0:T(8,128)(2,1)S(1)}, bf16[2,2,10...) custom-call(s32[3]{0:T(128)S(1)} %copy-done.1, ...), custom_call_target="tpu_custom_call" | custom-call | flops 28999999488 | bytes 1000000 | tf_op jit(solution)/shard_map/back/pallas_call | solution.py:56
  120.7 2.8 %collective-permute-done.23.refs_2_ = bf16[8,16,2560]{2,1,0:T(8,128)(2,1)S(1)} collective-permute-done((bf16[8,16,2560]{2,1,0:T(8,128)(2,1)}, bf16[8,16,2560]{2,1,0:T(8,128)(2,1)S(1)}, u32[]{:S(2)}, u32[]{:S(2)}) %collective-permute-start.23) | collective-permute-done | bytes 655392 | tf_op jit(solution)/shard_map/ppermute | solution.py:583
  123.5 0.9 feat_sum_b.1
  124.4 1.2 core_sum.1
  125.6 2.3 %collective-permute-start.27 = (bf16[2,2,104,128]{3,2,1,0:T(8,128)(2,1)S(1)}, bf16[2,2,104,128]{3,2,1,0:T(8,128)(2,1)S(1)}, u32[]{:S(2)}, u32[]{:S(2)}) collective-permute-start(bf16[2,2,104,128]{3,2,1,0:T(8,128)(2,1)S(1)} %get-tuple-element.122), channel_id=1, source_target_pairs={{0,2},{1,3},{2,0},{3,1},{4,6},{5,7},{6,4},{7,5},{8,10},{9,11},{10,... | collective-permute-start | bytes 319496 | tf_op jit(solution)/shard_map/ppermute | solution.py:583
  127.8 1.0 collective-permute-start.28
  128.8 1.5 collective-permute-start.29
  130.3 3.5 %all-to-all-start.2 = ((bf16[4,4,16,1664]{3,2,1,0:T(8,128)(2,1)}), bf16[4,4,16,1664]{3,2,1,0:T(8,128)(2,1)S(1)}, u32[]{:S(2)}, u32[]{:S(2)}) async-start(bf16[4,4,16,1664]{3,2,1,0:T(8,128)(2,1)} %core_sum.1), calls=%async_computation.2 | async-start | bytes 1703936 | tf_op jit(solution)/shard_map/all_to_all | solution.py:609
  133.8 0.6 core_sum_b.1
  134.4 4.7 %collective-permute-done.28.refs_2_ = bf16[2,2,104,128]{3,2,1,0:T(8,128)(2,1)S(1)} collective-permute-done((bf16[2,2,104,128]{3,2,1,0:T(8,128)(2,1)S(1)}, bf16[2,2,104,128]{3,2,1,0:T(8,128)(2,1)S(1)}, u32[]{:S(2)}, u32[]{:S(2)}) %collective-permute-start.28) | collective-permute-done | bytes 106528 | tf_op jit(solution)/shard_map/ppermute | solution.py:583
  139.1 0.6 pick.1
  139.8 1.5 collective-permute-done.30.got_ref
  141.2 1.5 unsort.1
  142.7 1.2 copy.63
  143.9 1.7 all-to-all-done.2.a_ref
  145.7 3.5 %all-to-all-start.1 = ((bf16[4,2,25,1024]{3,1,2,0:T(2,128)(2,1)}), bf16[4,2,25,1024]{3,1,2,0:T(2,128)(2,1)S(1)}, u32[]{:S(2)}, u32[]{:S(2)}) async-start(bf16[4,2,25,1024]{3,1,2,0:T(2,128)(2,1)} %copy.63), calls=%async_computation.1 | async-start | bytes 819200 | tf_op jit(solution)/shard_map/all_to_all | solution.py:609
  149.1 0.7 feat_sum.1
  149.8 0.8 collective-permute-start.31
  150.6 2.2 %collective-permute-start.32 = (bf16[16,4224]{1,0:T(8,128)(2,1)S(1)}, bf16[16,4224]{1,0:T(8,128)(2,1)S(1)}, u32[]{:S(2)}, u32[]{:S(2)}) collective-permute-start(bf16[16,4224]{1,0:T(8,128)(2,1)S(1)} %get-tuple-element.132), channel_id=1, source_target_pairs={{0,4},{1,5},{2,6},{3,7},{4,0},{5,1},{6,2},{7,3},{8,12},{9,13},{10,... | collective-permute-start | bytes 405512 | tf_op jit(solution)/shard_map/ppermute | solution.py:583
  152.8 1.5 collective-permute-start.33
  154.3 1.1 all-to-all-done.1
  155.8 0.9 collective-permute-done.31.refs_1_
  156.7 7.1 %collective-permute-done.32.refs_2_ = bf16[16,4224]{1,0:T(8,128)(2,1)S(1)} collective-permute-done((bf16[16,4224]{1,0:T(8,128)(2,1)S(1)}, bf16[16,4224]{1,0:T(8,128)(2,1)S(1)}, u32[]{:S(2)}, u32[]{:S(2)}) %collective-permute-start.32) | collective-permute-done | bytes 135200 | tf_op jit(solution)/shard_map/ppermute | solution.py:583
  163.9 2.6 %collective-permute-start.36 = (bf16[16,4224]{1,0:T(8,128)(2,1)S(1)}, bf16[16,4224]{1,0:T(8,128)(2,1)S(1)}, u32[]{:S(2)}, u32[]{:S(2)}) collective-permute-start(bf16[16,4224]{1,0:T(8,128)(2,1)S(1)} %rows_sum.1.refs_0_), channel_id=1, source_target_pairs={{0,24},{8,16},{16,8},{24,0},{1,25},{9,17},{17,9},{25,1},{2,26},{10... | collective-permute-start | bytes 405512 | tf_op jit(solution)/shard_map/ppermute | solution.py:583
  167.5 1.4 fusion
  168.8 1.1 collective-permute-done.36.refs_3_
  169.9 1.7 collective-permute-done.35.refs_2_
  172.2 3.0 %adamw.1 = (f32[64,100]{1,0:T(8,128)}, f32[64,100]{1,0:T(8,128)}, f32[64,100]{1,0:T(8,128)}, f32[64,2048]{1,0:T(8,128)}, f32[64,2048]{1,0:T(8,128)}, /*index=5*/...) custom-call(s32[3]{0:T(128)S(1)} %copy-done.1, ...), custom_call_target="tpu_custom_call" | custom-call | flops 4000000000 | bytes 1000000 | tf_op jit(solution)/shard_map/adamw/pallas_call | solution.py:56
  (100 shorter events, 8.5 us)
Async XLA Ops:
  0.7 43.8 %copy-start = (s32[3]{0:T(128)}, s32[3]{0:T(128)S(1)}, u32[]{:S(2)}) copy-start(s32[3]{0:T(128)S(1)} %pad_add_fusion.idx_ref) | copy-start | bytes 40
  2.3 9.6 %collective-permute-start.13 = (bf16[16,4224]{1,0:T(8,128)(2,1)S(1)}, bf16[16,4224]{1,0:T(8,128)(2,1)S(1)}, u32[]{:S(2)}, u32[]{:S(2)}) collective-permute-start(bf16[16,4224]{1,0:T(8,128)(2,1)S(1)} %pack.1.refs_0_), channel_id=1, source_target_pairs={{0,6},{1,7},{2,4},{3,5},{4,2},{5,3},{6,0},{7,1},{8,14},{9,15},{10,... | collective-permute-start | bytes 405512 | tf_op jit(solution)/shard_map/ppermute | solution.py:583
  7.5 11.4 %collective-permute-start.12 = (bf16[16,4224]{1,0:T(8,128)(2,1)S(1)}, bf16[16,4224]{1,0:T(8,128)(2,1)S(1)}, u32[]{:S(2)}, u32[]{:S(2)}) collective-permute-start(bf16[16,4224]{1,0:T(8,128)(2,1)S(1)} %pack.1.refs_0_), channel_id=1, source_target_pairs={{0,4},{1,5},{2,6},{3,7},{4,0},{5,1},{6,2},{7,3},{8,12},{9,13},{10,... | collective-permute-start | bytes 405512 | tf_op jit(solution)/shard_map/ppermute | solution.py:583
  7.5 11.4 %collective-permute-start.11 = (bf16[16,4224]{1,0:T(8,128)(2,1)S(1)}, bf16[16,4224]{1,0:T(8,128)(2,1)S(1)}, u32[]{:S(2)}, u32[]{:S(2)}) collective-permute-start(bf16[16,4224]{1,0:T(8,128)(2,1)S(1)} %pack.1.refs_0_), channel_id=1, source_target_pairs={{0,2},{1,3},{2,0},{3,1},{4,6},{5,7},{6,4},{7,5},{8,10},{9,11},{10,... | collective-permute-start | bytes 405512 | tf_op jit(solution)/shard_map/ppermute | solution.py:583
  8.8 15.4 %collective-permute-start.3 = (bf16[2,25,1024]{2,1,0:T(8,128)(2,1)S(1)}, bf16[2,25,1024]{2,1,0:T(8,128)(2,1)S(1)}, u32[]{:S(2)}, u32[]{:S(2)}) collective-permute-start(bf16[2,25,1024]{2,1,0:T(8,128)(2,1)S(1)} %get-tuple-element.150), channel_id=1, source_target_pairs={{0,24},{8,16},{16,8},{24,0},{1,25},{9,17},{17,9},{25,1},{2,26},{10... | collective-permute-start | bytes 307208 | tf_op jit(solution)/shard_map/ppermute | solution.py:583
  11.4 13.1 %collective-permute-start.2 = (bf16[2,25,1024]{2,1,0:T(8,128)(2,1)S(1)}, bf16[2,25,1024]{2,1,0:T(8,128)(2,1)S(1)}, u32[]{:S(2)}, u32[]{:S(2)}) collective-permute-start(bf16[2,25,1024]{2,1,0:T(8,128)(2,1)S(1)} %get-tuple-element.151), channel_id=1, source_target_pairs={{0,16},{8,24},{16,0},{24,8},{1,17},{9,25},{17,1},{25,9},{2,18},{10... | collective-permute-start | bytes 307208 | tf_op jit(solution)/shard_map/ppermute | solution.py:583
  12.0 12.8 %collective-permute-start.1 = (bf16[2,25,1024]{2,1,0:T(8,128)(2,1)S(1)}, bf16[2,25,1024]{2,1,0:T(8,128)(2,1)S(1)}, u32[]{:S(2)}, u32[]{:S(2)}) collective-permute-start(bf16[2,25,1024]{2,1,0:T(8,128)(2,1)S(1)} %get-tuple-element.152), channel_id=1, source_target_pairs={{0,8},{8,0},{16,24},{24,16},{1,9},{9,1},{17,25},{25,17},{2,10},{10... | collective-permute-start | bytes 307208 | tf_op jit(solution)/shard_map/ppermute | solution.py:583
  18.9 7.3 %collective-permute-start.4 = (bf16[2,25,1024]{2,1,0:T(8,128)(2,1)S(1)}, bf16[2,25,1024]{2,1,0:T(8,128)(2,1)S(1)}, u32[]{:S(2)}, u32[]{:S(2)}) collective-permute-start(bf16[2,25,1024]{2,1,0:T(8,128)(2,1)S(1)} %get-tuple-element.153.refs_0_), channel_id=1, source_target_pairs={{0,1},{1,0},{2,3},{3,2},{4,5},{5,4},{6,7},{7,6},{8,9},{9,8},{10,11... | collective-permute-start | bytes 307208 | tf_op jit(solution)/shard_map/ppermute | solution.py:583
  20.4 23.9 %copy-start.8 = (bf16[4,16,2560]{2,1,0:T(8,128)(2,1)}, bf16[4,16,2560]{2,1,0:T(8,128)(2,1)S(1)}, u32[]{:S(2)}) copy-start(bf16[4,16,2560]{2,1,0:T(8,128)(2,1)S(1)} %get-tuple-element.91.refs_0_) | copy-start | bytes 983044
  20.4 20.1 %all-to-all-start = ((bf16[4,4,16,1664]{3,2,1,0:T(8,128)(2,1)}), bf16[4,4,16,1664]{3,2,1,0:T(8,128)(2,1)S(1)}, u32[]{:S(2)}, u32[]{:S(2)}) async-start(bf16[4,4,16,1664]{3,2,1,0:T(8,128)(2,1)} %get-tuple-element.85), calls=%async_computation | async-start | bytes 1703936 | tf_op jit(solution)/shard_map/all_to_all | solution.py:609
  24.2 2.1 %collective-permute-start.7 = (bf16[2,25,1024]{2,1,0:T(8,128)(2,1)S(1)}, bf16[2,25,1024]{2,1,0:T(8,128)(2,1)S(1)}, u32[]{:S(2)}, u32[]{:S(2)}) collective-permute-start(bf16[2,25,1024]{2,1,0:T(8,128)(2,1)S(1)} %collective-permute-done.3.refs_3_), channel_id=1, source_target_pairs={{0,1},{1,0},{2,3},{3,2},{4,5},{5,4},{6,7},{7,6},{8,9},{9,8},{10,11... | collective-permute-start | bytes 307208 | tf_op jit(solution)/shard_map/ppermute | solution.py:583
  24.5 1.7 collective-permute-start.6
  24.8 1.5 collective-permute-start.5
  25.1 1.2 collective-permute-start
  26.3 18.3 %copy-start.9 = (s32[2,1,1,1024]{3,2,1,0:T(1,128)S(1)}, s32[2,1,1,1024]{3,2,1,0:T(1,128)}, u32[]{:S(2)}) copy-start(s32[2,1,1,1024]{3,2,1,0:T(1,128)} %seg_ref.3) | copy-start | bytes 24580
  26.3 18.3 %copy-start.10 = (s32[2,1,1,1024]{3,2,1,0:T(1,128)S(1)}, s32[2,1,1,1024]{3,2,1,0:T(1,128)}, u32[]{:S(2)}) copy-start(s32[2,1,1,1024]{3,2,1,0:T(1,128)} %ctx_ref.3) | copy-start | bytes 24580
  29.0 6.9 %collective-permute-start.8 = (bf16[2,2,104,128]{3,2,1,0:T(8,128)(2,1)S(1)}, bf16[2,2,104,128]{3,2,1,0:T(8,128)(2,1)S(1)}, u32[]{:S(2)}, u32[]{:S(2)}) collective-permute-start(bf16[2,2,104,128]{3,2,1,0:T(8,128)(2,1)S(1)} %get-tuple-element.82), channel_id=1, source_target_pairs={{0,2},{1,3},{2,0},{3,1},{4,6},{5,7},{6,4},{7,5},{8,10},{9,11},{10,... | collective-permute-start | bytes 319496 | tf_op jit(solution)/shard_map/ppermute | solution.py:583
  29.2 11.3 %collective-permute-start.9 = (bf16[2,2,104,128]{3,2,1,0:T(8,128)(2,1)S(1)}, bf16[2,2,104,128]{3,2,1,0:T(8,128)(2,1)S(1)}, u32[]{:S(2)}, u32[]{:S(2)}) collective-permute-start(bf16[2,2,104,128]{3,2,1,0:T(8,128)(2,1)S(1)} %get-tuple-element.83), channel_id=1, source_target_pairs={{0,4},{1,5},{2,6},{3,7},{4,0},{5,1},{6,2},{7,3},{8,12},{9,13},{10,... | collective-permute-start | bytes 319496 | tf_op jit(solution)/shard_map/ppermute | solution.py:583
  32.1 8.4 %collective-permute-start.10 = (bf16[2,2,104,128]{3,2,1,0:T(8,128)(2,1)S(1)}, bf16[2,2,104,128]{3,2,1,0:T(8,128)(2,1)S(1)}, u32[]{:S(2)}, u32[]{:S(2)}) collective-permute-start(bf16[2,2,104,128]{3,2,1,0:T(8,128)(2,1)S(1)} %get-tuple-element.84), channel_id=1, source_target_pairs={{0,6},{1,7},{2,4},{3,5},{4,2},{5,3},{6,0},{7,1},{8,14},{9,15},{10,... | collective-permute-start | bytes 319496 | tf_op jit(solution)/shard_map/ppermute | solution.py:583
  40.5 4.0 %collective-permute-start.14 = (bf16[4,4,16,1664]{3,2,1,0:T(8,128)(2,1)S(1)}, bf16[4,4,16,1664]{3,2,1,0:T(8,128)(2,1)S(1)}, u32[]{:S(2)}, u32[]{:S(2)}) collective-permute-start(bf16[4,4,16,1664]{3,2,1,0:T(8,128)(2,1)S(1)} %all-to-all-done.refs_4_), channel_id=1, source_target_pairs={{0,1},{1,0},{2,3},{3,2},{4,5},{5,4},{6,7},{7,6},{8,9},{9,8},{10,11... | collective-permute-start | bytes 2555912 | tf_op jit(solution)/shard_map/ppermute | solution.py:583
  40.5 19.7 %collective-permute-start.18 = (bf16[4,16,2560]{2,1,0:T(8,128)(2,1)S(1)}, bf16[4,16,2560]{2,1,0:T(8,128)(2,1)S(1)}, u32[]{:S(2)}, u32[]{:S(2)}) collective-permute-start(bf16[4,16,2560]{2,1,0:T(8,128)(2,1)S(1)} %get-tuple-element.91.refs_0_), channel_id=1, source_target_pairs={{0,1},{1,0},{2,3},{3,2},{4,5},{5,4},{6,7},{7,6},{8,9},{9,8},{10,11... | collective-permute-start | bytes 983048 | tf_op jit(solution)/shard_map/ppermute | solution.py:583
  41.0 18.5 %collective-permute-start.17 = (bf16[4,16,2560]{2,1,0:T(8,128)(2,1)S(1)}, bf16[4,16,2560]{2,1,0:T(8,128)(2,1)S(1)}, u32[]{:S(2)}, u32[]{:S(2)}) collective-permute-start(bf16[4,16,2560]{2,1,0:T(8,128)(2,1)S(1)} %get-tuple-element.91.refs_0_), channel_id=1, source_target_pairs={{0,24},{8,16},{16,8},{24,0},{1,25},{9,17},{17,9},{25,1},{2,26},{10... | collective-permute-start | bytes 983048 | tf_op jit(solution)/shard_map/ppermute | solution.py:583
  43.8 15.7 %collective-permute-start.16 = (bf16[4,16,2560]{2,1,0:T(8,128)(2,1)S(1)}, bf16[4,16,2560]{2,1,0:T(8,128)(2,1)S(1)}, u32[]{:S(2)}, u32[]{:S(2)}) collective-permute-start(bf16[4,16,2560]{2,1,0:T(8,128)(2,1)S(1)} %get-tuple-element.91.refs_0_), channel_id=1, source_target_pairs={{0,16},{8,24},{16,0},{24,8},{1,17},{9,25},{17,1},{25,9},{2,18},{10... | collective-permute-start | bytes 983048 | tf_op jit(solution)/shard_map/ppermute | solution.py:583
  44.3 15.2 %collective-permute-start.15 = (bf16[4,16,2560]{2,1,0:T(8,128)(2,1)S(1)}, bf16[4,16,2560]{2,1,0:T(8,128)(2,1)S(1)}, u32[]{:S(2)}, u32[]{:S(2)}) collective-permute-start(bf16[4,16,2560]{2,1,0:T(8,128)(2,1)S(1)} %get-tuple-element.91.refs_0_), channel_id=1, source_target_pairs={{0,8},{8,0},{16,24},{24,16},{1,9},{9,1},{17,25},{25,17},{2,10},{10... | collective-permute-start | bytes 983048 | tf_op jit(solution)/shard_map/ppermute | solution.py:583
  59.6 1.7 collective-permute-start.19
  59.6 2.1 %collective-permute-start.20 = (bf16[4,16,2560]{2,1,0:T(8,128)(2,1)S(1)}, bf16[4,16,2560]{2,1,0:T(8,128)(2,1)S(1)}, u32[]{:S(2)}, u32[]{:S(2)}) collective-permute-start(bf16[4,16,2560]{2,1,0:T(8,128)(2,1)S(1)} %collective-permute-done.16.refs_2_), channel_id=1, source_target_pairs={{0,1},{1,0},{2,3},{3,2},{4,5},{5,4},{6,7},{7,6},{8,9},{9,8},{10,11... | collective-permute-start | bytes 983048 | tf_op jit(solution)/shard_map/ppermute | solution.py:583
  60.1 2.1 %collective-permute-start.21 = (bf16[4,16,2560]{2,1,0:T(8,128)(2,1)S(1)}, bf16[4,16,2560]{2,1,0:T(8,128)(2,1)S(1)}, u32[]{:S(2)}, u32[]{:S(2)}) collective-permute-start(bf16[4,16,2560]{2,1,0:T(8,128)(2,1)S(1)} %collective-permute-done.17.refs_3_), channel_id=1, source_target_pairs={{0,1},{1,0},{2,3},{3,2},{4,5},{5,4},{6,7},{7,6},{8,9},{9,8},{10,11... | collective-permute-start | bytes 983048 | tf_op jit(solution)/shard_map/ppermute | solution.py:583
  62.9 31.4 %copy-start.1 = (s32[3]{0:T(128)S(1)}, s32[3]{0:T(128)}, u32[]{:S(2)}) copy-start(s32[3]{0:T(128)} %copy-done) | copy-start | bytes 40
  90.8 29.9 %collective-permute-start.22 = (bf16[8,16,2560]{2,1,0:T(8,128)(2,1)}, bf16[8,16,2560]{2,1,0:T(8,128)(2,1)S(1)}, u32[]{:S(2)}, u32[]{:S(2)}) collective-permute-start(bf16[8,16,2560]{2,1,0:T(8,128)(2,1)} %get-tuple-element.108), channel_id=1, source_target_pairs={{0,8},{8,0},{16,24},{24,16},{1,9},{9,1},{17,25},{25,17},{2,10},{10... | collective-permute-start | bytes 1966088 | tf_op jit(solution)/shard_map/ppermute | solution.py:583
  92.7 30.8 %collective-permute-start.23 = (bf16[8,16,2560]{2,1,0:T(8,128)(2,1)}, bf16[8,16,2560]{2,1,0:T(8,128)(2,1)S(1)}, u32[]{:S(2)}, u32[]{:S(2)}) collective-permute-start(bf16[8,16,2560]{2,1,0:T(8,128)(2,1)} %get-tuple-element.109), channel_id=1, source_target_pairs={{0,16},{8,24},{16,0},{24,8},{1,17},{9,25},{17,1},{25,9},{2,18},{10... | collective-permute-start | bytes 1966088 | tf_op jit(solution)/shard_map/ppermute | solution.py:583
  94.2 29.3 %collective-permute-start.24 = (bf16[8,16,2560]{2,1,0:T(8,128)(2,1)}, bf16[8,16,2560]{2,1,0:T(8,128)(2,1)S(1)}, u32[]{:S(2)}, u32[]{:S(2)}) collective-permute-start(bf16[8,16,2560]{2,1,0:T(8,128)(2,1)} %get-tuple-element.110), channel_id=1, source_target_pairs={{0,24},{8,16},{16,8},{24,0},{1,25},{9,17},{17,9},{25,1},{2,26},{10... | collective-permute-start | bytes 1966088 | tf_op jit(solution)/shard_map/ppermute | solution.py:583
  94.3 29.1 %copy-start.11 = (bf16[8,16,2560]{2,1,0:T(8,128)(2,1)S(1)}, bf16[8,16,2560]{2,1,0:T(8,128)(2,1)}, u32[]{:S(2)}) copy-start(bf16[8,16,2560]{2,1,0:T(8,128)(2,1)} %get-tuple-element.107.refs_0_) | copy-start | bytes 1966084
  120.6 3.8 %collective-permute-start.25 = (bf16[4,64,1664]{2,1,0:T(8,128)(2,1)S(1)}, bf16[4,64,1664]{2,1,0:T(8,128)(2,1)S(1)}, u32[]{:S(2)}, u32[]{:S(2)}) collective-permute-start(bf16[4,64,1664]{2,1,0:T(8,128)(2,1)S(1)} %get-tuple-element.113), channel_id=1, source_target_pairs={{0,1},{1,0},{2,3},{3,2},{4,5},{5,4},{6,7},{7,6},{8,9},{9,8},{10,11... | collective-permute-start | bytes 2555912 | tf_op jit(solution)/shard_map/ppermute | solution.py:583
  124.3 9.5 %collective-permute-start.26 = (bf16[4,16,2560]{2,1,0:T(8,128)(2,1)S(1)}, bf16[4,16,2560]{2,1,0:T(8,128)(2,1)S(1)}, u32[]{:S(2)}, u32[]{:S(2)}) collective-permute-start(bf16[4,16,2560]{2,1,0:T(8,128)(2,1)S(1)} %get-tuple-element.115), channel_id=1, source_target_pairs={{0,1},{1,0},{2,3},{3,2},{4,5},{5,4},{6,7},{7,6},{8,9},{9,8},{10,11... | collective-permute-start | bytes 983048 | tf_op jit(solution)/shard_map/ppermute | solution.py:583
  125.6 8.9 %collective-permute-start.27 = (bf16[2,2,104,128]{3,2,1,0:T(8,128)(2,1)S(1)}, bf16[2,2,104,128]{3,2,1,0:T(8,128)(2,1)S(1)}, u32[]{:S(2)}, u32[]{:S(2)}) collective-permute-start(bf16[2,2,104,128]{3,2,1,0:T(8,128)(2,1)S(1)} %get-tuple-element.122), channel_id=1, source_target_pairs={{0,2},{1,3},{2,0},{3,1},{4,6},{5,7},{6,4},{7,5},{8,10},{9,11},{10,... | collective-permute-start | bytes 319496 | tf_op jit(solution)/shard_map/ppermute | solution.py:583
  127.8 11.3 %collective-permute-start.28 = (bf16[2,2,104,128]{3,2,1,0:T(8,128)(2,1)S(1)}, bf16[2,2,104,128]{3,2,1,0:T(8,128)(2,1)S(1)}, u32[]{:S(2)}, u32[]{:S(2)}) collective-permute-start(bf16[2,2,104,128]{3,2,1,0:T(8,128)(2,1)S(1)} %get-tuple-element.124), channel_id=1, source_target_pairs={{0,4},{1,5},{2,6},{3,7},{4,0},{5,1},{6,2},{7,3},{8,12},{9,13},{10,... | collective-permute-start | bytes 319496 | tf_op jit(solution)/shard_map/ppermute | solution.py:583
  128.8 10.3 %collective-permute-start.29 = (bf16[2,2,104,128]{3,2,1,0:T(8,128)(2,1)S(1)}, bf16[2,2,104,128]{3,2,1,0:T(8,128)(2,1)S(1)}, u32[]{:S(2)}, u32[]{:S(2)}) collective-permute-start(bf16[2,2,104,128]{3,2,1,0:T(8,128)(2,1)S(1)} %get-tuple-element.126), channel_id=1, source_target_pairs={{0,6},{1,7},{2,4},{3,5},{4,2},{5,3},{6,0},{7,1},{8,14},{9,15},{10,... | collective-permute-start | bytes 319496 | tf_op jit(solution)/shard_map/ppermute | solution.py:583
  130.3 15.4 %all-to-all-start.2 = ((bf16[4,4,16,1664]{3,2,1,0:T(8,128)(2,1)}), bf16[4,4,16,1664]{3,2,1,0:T(8,128)(2,1)S(1)}, u32[]{:S(2)}, u32[]{:S(2)}) async-start(bf16[4,4,16,1664]{3,2,1,0:T(8,128)(2,1)} %core_sum.1), calls=%async_computation.2 | async-start | bytes 1703936 | tf_op jit(solution)/shard_map/all_to_all | solution.py:609
  139.7 1.5 collective-permute-start.30
  145.7 9.7 %all-to-all-start.1 = ((bf16[4,2,25,1024]{3,1,2,0:T(2,128)(2,1)}), bf16[4,2,25,1024]{3,1,2,0:T(2,128)(2,1)S(1)}, u32[]{:S(2)}, u32[]{:S(2)}) async-start(bf16[4,2,25,1024]{3,1,2,0:T(2,128)(2,1)} %copy.63), calls=%async_computation.1 | async-start | bytes 819200 | tf_op jit(solution)/shard_map/all_to_all | solution.py:609
  149.8 6.9 %collective-permute-start.31 = (bf16[16,4224]{1,0:T(8,128)(2,1)S(1)}, bf16[16,4224]{1,0:T(8,128)(2,1)S(1)}, u32[]{:S(2)}, u32[]{:S(2)}) collective-permute-start(bf16[16,4224]{1,0:T(8,128)(2,1)S(1)} %get-tuple-element.131), channel_id=1, source_target_pairs={{0,2},{1,3},{2,0},{3,1},{4,6},{5,7},{6,4},{7,5},{8,10},{9,11},{10,... | collective-permute-start | bytes 405512 | tf_op jit(solution)/shard_map/ppermute | solution.py:583
  150.6 13.2 %collective-permute-start.32 = (bf16[16,4224]{1,0:T(8,128)(2,1)S(1)}, bf16[16,4224]{1,0:T(8,128)(2,1)S(1)}, u32[]{:S(2)}, u32[]{:S(2)}) collective-permute-start(bf16[16,4224]{1,0:T(8,128)(2,1)S(1)} %get-tuple-element.132), channel_id=1, source_target_pairs={{0,4},{1,5},{2,6},{3,7},{4,0},{5,1},{6,2},{7,3},{8,12},{9,13},{10,... | collective-permute-start | bytes 405512 | tf_op jit(solution)/shard_map/ppermute | solution.py:583
  152.8 11.0 %collective-permute-start.33 = (bf16[16,4224]{1,0:T(8,128)(2,1)S(1)}, bf16[16,4224]{1,0:T(8,128)(2,1)S(1)}, u32[]{:S(2)}, u32[]{:S(2)}) collective-permute-start(bf16[16,4224]{1,0:T(8,128)(2,1)S(1)} %get-tuple-element.133), channel_id=1, source_target_pairs={{0,6},{1,7},{2,4},{3,5},{4,2},{5,3},{6,0},{7,1},{8,14},{9,15},{10,... | collective-permute-start | bytes 405512 | tf_op jit(solution)/shard_map/ppermute | solution.py:583
  163.8 8.3 %copy-start.6 = (f32[64,2048]{1,0:T(8,128)S(1)}, f32[64,2048]{1,0:T(8,128)}, u32[]{:S(2)}) copy-start(f32[64,2048]{1,0:T(8,128)} %refs_11_.1) | copy-start | bytes 1572868
  163.8 8.3 %copy-start.7 = (f32[64,2048]{1,0:T(8,128)S(1)}, f32[64,2048]{1,0:T(8,128)}, u32[]{:S(2)}) copy-start(f32[64,2048]{1,0:T(8,128)} %refs_12_.1) | copy-start | bytes 1572868
  163.9 6.0 %collective-permute-start.36 = (bf16[16,4224]{1,0:T(8,128)(2,1)S(1)}, bf16[16,4224]{1,0:T(8,128)(2,1)S(1)}, u32[]{:S(2)}, u32[]{:S(2)}) collective-permute-start(bf16[16,4224]{1,0:T(8,128)(2,1)S(1)} %rows_sum.1.refs_0_), channel_id=1, source_target_pairs={{0,24},{8,16},{16,8},{24,0},{1,25},{9,17},{17,9},{25,1},{2,26},{10... | collective-permute-start | bytes 405512 | tf_op jit(solution)/shard_map/ppermute | solution.py:583
  166.5 5.0 %collective-permute-start.35 = (bf16[16,4224]{1,0:T(8,128)(2,1)S(1)}, bf16[16,4224]{1,0:T(8,128)(2,1)S(1)}, u32[]{:S(2)}, u32[]{:S(2)}) collective-permute-start(bf16[16,4224]{1,0:T(8,128)(2,1)S(1)} %rows_sum.1.refs_0_), channel_id=1, source_target_pairs={{0,16},{8,24},{16,0},{24,8},{1,17},{9,25},{17,1},{25,9},{2,18},{10... | collective-permute-start | bytes 405512 | tf_op jit(solution)/shard_map/ppermute | solution.py:583
  167.1 5.0 %collective-permute-start.34 = (bf16[16,4224]{1,0:T(8,128)(2,1)S(1)}, bf16[16,4224]{1,0:T(8,128)(2,1)S(1)}, u32[]{:S(2)}, u32[]{:S(2)}) collective-permute-start(bf16[16,4224]{1,0:T(8,128)(2,1)S(1)} %rows_sum.1.refs_0_), channel_id=1, source_target_pairs={{0,8},{8,0},{16,24},{24,16},{1,9},{9,1},{17,25},{25,17},{2,10},{10... | collective-permute-start | bytes 405512 | tf_op jit(solution)/shard_map/ppermute | solution.py:583
  (14 other events, 65.6 us)
